TPU v7x, 128 devices: a whole 4x4x4 slice. The times are simulated.
128 devices in a mesh: tx: 4 (over x), ty: 16 (over y, z), mem: 2 (over core).
Axes of the slice: x: 4, y: 4, z: 4, core: 2. Of those that a mesh axis runs over, the one named last changes fastest.
Arguments:
- volume: bfloat16 [64, 40, 192, 128], P(('tx', 'ty'), 'mem'), may hold values from -15 to 15
- super_matrix: bfloat16 [64, 192, 128, 128], P(('tx', 'ty')), may hold values from -0.5 to 0.5
- observed: bfloat16 [64, 24576], P(('tx', 'ty')), may hold values from -16 to 16
- error_var: float32 [64, 24576], P(('tx', 'ty')), may hold values from 24 to 384
- obs_cells: int32 [64, 24576], P(('tx', 'ty')), may hold values from 0 to 2047, as said below
- counts: int32 [64, 64], P(('tx', 'ty')), may hold values from 1 to 768, 24576 in all within a row
- state: bfloat16 [40, 8, 64, 2048], P('mem', None, 'tx', 'ty'), may hold values from -8 to 8
Outputs:
- analysis: bfloat16 [40, 8, 64, 2048], P('mem', None, 'tx', 'ty')
Inputs may be any that keep to these rules, and one draw needn't show every extreme that they name: Each radar's counts over the tiles sum to 24576, and each radar's largest count is exactly 768. `obs_cells`: the cell is row-major inside the destination tile, 128 cells a row.
All inputs are finite; a program needn't handle non-finite values.
Results may differ from a plain program's by a relative error of at most 0.015.
Values may be sent and summed in bfloat16 or wider, within the bound.
A program may use at most 128 MiB of HBM per device.

v0:
```python
import jax
import jax.numpy as jnp
from jax import lax
from jax.sharding import PartitionSpec as P

B = 8
LOC = 16
NS = 5
CAP = 768


exact = lax.Precision.HIGHEST


def padded_2(block, sides, width):
    for axis, dim in sides:
        count = lax.axis_size(axis)
        forward = [(i, i + 1) for i in range(count - 1)]
        backward = [(target, source) for source, target in forward]
        low = lax.ppermute(
            lax.slice_in_dim(block, block.shape[dim] - width, None, axis=dim), axis, forward
        )
        high = lax.ppermute(lax.slice_in_dim(block, 0, width, axis=dim), axis, backward)
        block = jnp.concatenate([low, block, high], axis=dim)
    return block


def taper_table(cell_ids, width_x, width_y, spacing):
    pos_x = (cell_ids // width_y).astype(jnp.float32)
    pos_y = (cell_ids % width_y).astype(jnp.float32)
    nodes_x = width_x // spacing
    nodes_y = width_y // spacing
    centre_x = jnp.repeat(
        jnp.arange(nodes_x, dtype=jnp.float32) * spacing + (spacing - 1) * 0.5, nodes_y
    )
    centre_y = jnp.tile(
        jnp.arange(nodes_y, dtype=jnp.float32) * spacing + (spacing - 1) * 0.5, nodes_x
    )
    square = (pos_x[None, :] - centre_x[:, None]) ** 2 + (pos_y[None, :] - centre_y[:, None]) ** 2
    return jnp.exp(-square / (2.0 * LOC * LOC))


def tent_table(length, nodes, spacing):
    position = jnp.arange(length, dtype=jnp.float32)[:, None]
    centre = (jnp.arange(nodes, dtype=jnp.float32)[None, :] - 1.0) * spacing + (spacing - 1) * 0.5
    return jnp.maximum(0.0, 1.0 - jnp.abs(position - centre) / spacing)


def coarse_weights(gram, inform):
    members = inform.shape[1]
    identity = jnp.eye(members, dtype=jnp.float32)
    amat = identity + gram.reshape(-1, members, members) / (members - 1)
    scale = jnp.sqrt(jnp.sum(amat * amat, axis=(1, 2)))[:, None, None]
    upper = amat / scale
    lower = jnp.broadcast_to(identity, amat.shape)
    for sweep in range(NS):
        middle = 1.5 * identity - 0.5 * jnp.einsum("cij,cjk->cik", lower, upper, precision=exact)
        upper = jnp.einsum("cij,cjk->cik", upper, middle, precision=exact)
        lower = jnp.einsum("cij,cjk->cik", middle, lower, precision=exact)
    inv_half = lower / jnp.sqrt(scale)
    step_one = jnp.einsum("cij,cj->ci", inv_half, inform, precision=exact)
    mean_shift = jnp.einsum("cij,cj->ci", inv_half, step_one, precision=exact) / (members - 1)
    shift = mean_shift - jnp.mean(mean_shift, axis=1, keepdims=True)
    spread = inv_half - jnp.mean(inv_half, axis=1, keepdims=True)
    trans = 1.0 / members + shift[:, :, None] + spread
    return trans.reshape(trans.shape[0], members * members)


def window_rows(blocked, pick_low, pick_high, offsets_in, precision_used):
    low_part = jnp.einsum(
        "tb,kbs->kts",
        pick_low,
        blocked,
        precision=precision_used,
        preferred_element_type=jnp.float32,
    )
    high_part = jnp.einsum(
        "tb,kbs->kts",
        pick_high,
        blocked,
        precision=precision_used,
        preferred_element_type=jnp.float32,
    )
    window = jnp.concatenate([low_part, high_part], axis=2)
    for bit_id in range((CAP - 1).bit_length()):
        step_len = 1 << bit_id
        moved = jnp.concatenate(
            [window[:, :, step_len:], jnp.zeros_like(window[:, :, :step_len])], axis=2
        )
        taken = offsets_in >> bit_id & 1 == 1
        window = jnp.where(taken[None, :, None], moved, window)
    return window[:, :, :CAP]


def per_device(volume, super_matrix, observed, error_var, obs_cells, counts, state):
    count_tx = lax.axis_size("tx")
    count_ty = lax.axis_size("ty")
    tiles = count_tx * count_ty
    half_members = volume.shape[1]
    members = half_members * lax.axis_size("mem")
    project = jnp.einsum(
        "kbg,bgs->kbs", volume[0], super_matrix[0], preferred_element_type=jnp.float32
    )
    radar_obs = project.reshape(half_members, -1).astype(jnp.bfloat16)
    inverse = (1.0 / error_var[0]).astype(jnp.bfloat16)
    radar_total = radar_obs.shape[1]
    block_count = radar_total // CAP + 1
    slot_ids = jnp.arange(CAP, dtype=jnp.int32)
    amounts = counts[0]
    offsets = jnp.cumsum(amounts) - amounts
    used = slot_ids[None, :] < amounts[:, None]
    first_block = offsets // CAP
    inner_offset = offsets % CAP
    block_ids = jnp.arange(block_count, dtype=jnp.int32)
    pick_low = first_block[:, None] == block_ids[None, :]
    pick_high = first_block[:, None] + 1 == block_ids[None, :]
    obs_blocks = jnp.concatenate(
        [radar_obs, jnp.zeros((half_members, CAP), jnp.bfloat16)], axis=1
    ).reshape(half_members, block_count, CAP)
    extra_rows = jnp.stack(
        [
            observed[0].astype(jnp.float32),
            inverse.astype(jnp.float32),
            obs_cells[0].astype(jnp.float32),
        ]
    )
    extra_blocks = jnp.concatenate([extra_rows, jnp.zeros((3, CAP), jnp.float32)], axis=1).reshape(
        3, block_count, CAP
    )
    obs_window = window_rows(
        obs_blocks,
        pick_low.astype(jnp.bfloat16),
        pick_high.astype(jnp.bfloat16),
        inner_offset,
        None,
    )
    extra_window = window_rows(
        extra_blocks,
        pick_low.astype(jnp.float32),
        pick_high.astype(jnp.float32),
        inner_offset,
        exact,
    )
    send_obs = jnp.where(used[None], obs_window, 0.0).astype(jnp.bfloat16)
    send_extra = jnp.where(used[None], extra_window[:2], 0.0).astype(jnp.bfloat16)
    send_cells = jnp.where(used, extra_window[2], 0.0).astype(jnp.int32)[None]
    got_obs, got_extra, got_cells = (
        lax.all_to_all(send_obs, ("tx", "ty"), split_axis=1, concat_axis=1, tiled=True),
        lax.all_to_all(send_extra, ("tx", "ty"), split_axis=1, concat_axis=1, tiled=True),
        lax.all_to_all(send_cells, ("tx", "ty"), split_axis=1, concat_axis=1, tiled=True),
    )
    slot_total = tiles * CAP
    flat_obs = got_obs.reshape(half_members, slot_total)
    ensemble = lax.all_to_all(flat_obs, "mem", split_axis=1, concat_axis=0, tiled=True)
    my_share = ensemble.shape[1]
    my_start = lax.axis_index("mem") * my_share
    my_extra = lax.dynamic_slice_in_dim(got_extra.reshape(2, slot_total), my_start, my_share, 1)
    my_cells = lax.dynamic_slice_in_dim(got_cells.reshape(slot_total), my_start, my_share, 0)
    ens_mean = jnp.sum(ensemble.astype(jnp.float32), axis=0) / members
    anomaly = lax.optimization_barrier(
        (ensemble.astype(jnp.float32) - ens_mean).astype(jnp.bfloat16)
    )
    innovation = my_extra[0].astype(jnp.float32) - ens_mean
    width_x = state.shape[2]
    width_y = state.shape[3]
    nodes_x = width_x // B
    nodes_y = width_y // B
    taper = taper_table(my_cells, width_x, width_y, B)
    weight_in = my_extra[1].astype(jnp.float32)
    weight = (taper * weight_in).astype(jnp.bfloat16)
    weight_innov = (taper * weight_in * innovation).astype(jnp.bfloat16)
    inform = jnp.einsum("cq,kq->ck", weight_innov, anomaly, preferred_element_type=jnp.float32)
    width_block = min(my_share, 2048)
    while my_share % width_block:
        width_block = width_block // 2

    def add_block(running, block_id):
        columns = lax.dynamic_slice_in_dim(anomaly, block_id * width_block, width_block, 1).astype(
            jnp.float32
        )
        weights_here = lax.dynamic_slice_in_dim(weight, block_id * width_block, width_block, 1)
        pairs = (
            (columns[:, None, :] * columns[None, :, :])
            .reshape(members * members, width_block)
            .astype(jnp.bfloat16)
        )
        return (
            running
            + jnp.einsum("cq,nq->cn", weights_here, pairs, preferred_element_type=jnp.float32),
            None,
        )

    gram_start = jnp.zeros((weight.shape[0], members * members), jnp.float32)
    gram = lax.scan(add_block, gram_start, jnp.arange(my_share // width_block, dtype=jnp.int32))[0]
    gram, inform = (
        lax.psum(gram.astype(jnp.bfloat16), "mem").astype(jnp.float32),
        lax.psum(inform.astype(jnp.bfloat16), "mem").astype(jnp.float32),
    )
    trans = coarse_weights(gram, inform).reshape(nodes_x, nodes_y, members * members)
    padded = padded_2(trans.astype(jnp.bfloat16), (("tx", 0), ("ty", 1)), 1).astype(trans.dtype)
    index_tx = lax.axis_index("tx")
    index_ty = lax.axis_index("ty")
    padded = padded.at[0].set(jnp.where(index_tx == 0, padded[1], padded[0]))
    padded = padded.at[-1].set(jnp.where(index_tx == count_tx - 1, padded[-2], padded[-1]))
    padded = padded.at[:, 0].set(jnp.where(index_ty == 0, padded[:, 1], padded[:, 0]))
    padded = padded.at[:, -1].set(jnp.where(index_ty == count_ty - 1, padded[:, -2], padded[:, -1]))
    flat = padded.reshape(nodes_x + 2, -1)
    table_x = tent_table(width_x, nodes_x + 2, B)
    table_y = tent_table(width_y, nodes_y + 2, B)

    def fine_rows(band_id):
        rows = lax.dynamic_slice_in_dim(table_x, band_id * B, B, 0)
        along = jnp.dot(rows, flat, precision=exact, preferred_element_type=jnp.float32).reshape(
            B, nodes_y + 2, members * members
        )
        return jnp.einsum("yb,xbn->xyn", table_y, along, precision=exact).astype(jnp.bfloat16)

    fine_weights = lax.map(fine_rows, jnp.arange(nodes_x, dtype=jnp.int32))
    fine_weights = fine_weights.reshape(width_x, width_y, members, members)
    own_first = lax.axis_index("mem") * half_members
    selected = lax.dynamic_slice(
        fine_weights,
        (0, 0, own_first, 0),
        (width_x, width_y, half_members, half_members * lax.axis_size("mem")),
    )
    return lax.psum_scatter(
        jnp.einsum("klxy,xykj->jlxy", state, selected, preferred_element_type=jnp.float32).astype(
            jnp.bfloat16
        ),
        "mem",
        scatter_dimension=0,
        tiled=True,
    )


def solution(mesh):
    placed = (
        P(("tx", "ty"), "mem", None, None),
        P(("tx", "ty"), None, None, None),
        P(("tx", "ty"), None),
        P(("tx", "ty"), None),
        P(("tx", "ty"), None),
        P(("tx", "ty"), None),
        P("mem", None, "tx", "ty"),
    )
    return jax.shard_map(
        per_device,
        mesh=mesh,
        in_specs=placed,
        out_specs=P("mem", None, "tx", "ty"),
        check_vma=False,
    )
```

profile of v0, /device:TPU:1, one launch (start us, length us, event | category | flops | bytes accessed | tf_op | source)
XLA Modules:
  0.0 378.8 jit_solution(10177609309626796589)
XLA Ops:
  20.5 12.5 %all-to-all-start = ((s32[1,64,768]{2,0,1:T(1,128)}), s32[1,64,768]{2,0,1:T(1,128)S(1)}, u32[]{:S(2)}, u32[]{:S(2)}) async-start(s32[1,64,768]{2,0,1:T(1,128)} %copy.42), calls=%async_computation | async-start | bytes 393216 | tf_op jit(solution)/shard_map/all_to_all | solution.py:150
  33.8 4.5 %fusion.39 = bf16[20,192,128]{2,0,1:T(8,128)(2,1)S(1)} fusion(bf16[1,192,128,128]{3,2,1,0:T(8,128)(2,1)} %param.20, bf16[20,192,128]{2,1,0:T(8,128)(2,1)S(1)} %bitcast.117), kind=kOutput, calls=%fused_computation.64 | convolution fusion | flops 126320640 | bytes 8257536 | tf_op jit(solution)/shard_map/kbg,bgs->kbs/dot_general | solution.py:101
  41.3 2.1 convolution_bitcast_fusion
  43.4 2.0 convolution_bitcast_fusion.1
  47.7 3.5 fusion.21
  79.0 2.9 copy.46
  82.5 9.9 %all-to-all-start.1 = ((bf16[2,64,768]{2,0,1:T(2,128)(2,1)}), bf16[2,64,768]{2,0,1:T(2,128)(2,1)S(1)}, u32[]{:S(2)}, u32[]{:S(2)}) async-start(bf16[2,64,768]{2,0,1:T(2,128)(2,1)} %copy.43), calls=%async_computation.1 | async-start | bytes 393216 | tf_op jit(solution)/shard_map/all_to_all | solution.py:149
  92.5 8.8 %all-to-all-done.1 = bf16[2,64,768]{2,0,1:T(2,128)(2,1)S(1)} async-done(((bf16[2,64,768]{2,0,1:T(2,128)(2,1)}), bf16[2,64,768]{2,0,1:T(2,128)(2,1)S(1)}, u32[]{:S(2)}, u32[]{:S(2)}) %all-to-all-start.1) | async-done | bytes 196640 | tf_op jit(solution)/shard_map/all_to_all | solution.py:149
  101.3 5.0 %all-to-all-start.2 = ((bf16[20,64,768]{2,0,1:T(8,128)(2,1)}), bf16[20,64,768]{2,0,1:T(8,128)(2,1)S(1)}, u32[]{:S(2)}, u32[]{:S(2)}) async-start(bf16[20,64,768]{2,0,1:T(8,128)(2,1)} %copy.46), calls=%async_computation.2 | async-start | bytes 4718592 | tf_op jit(solution)/shard_map/all_to_all | solution.py:148
  106.6 2.2 fusion.27
  108.8 25.8 %all-to-all-done.2 = bf16[20,64,768]{2,0,1:T(8,128)(2,1)S(1)} async-done(((bf16[20,64,768]{2,0,1:T(8,128)(2,1)}), bf16[20,64,768]{2,0,1:T(8,128)(2,1)S(1)}, u32[]{:S(2)}, u32[]{:S(2)}) %all-to-all-start.2) | async-done | bytes 1966112 | tf_op jit(solution)/shard_map/all_to_all | solution.py:148
  136.3 2.5 all_to_all.22
  139.9 10.4 %all_to_all.28 = bf16[20,2,24576]{2,0,1:T(8,128)(2,1)S(1)} all-to-all(bf16[20,2,24576]{2,0,1:T(8,128)(2,1)S(1)} %copy.48), channel_id=1, replica_groups=mesh['tx'=4,'ty'=16,'mem'=2] {'mem'}, dimensions={1} | all-to-all | bytes 3932160 | tf_op jit(solution)/shard_map/all_to_all | solution.py:154
  150.9 2.5 convert_bitcast_fusion
  153.4 4.7 %reshape.429 = f32[40,24576]{1,0:T(8,128)} reshape(f32[2,20,24576]{2,1,0:T(8,128)} %convert_bitcast_fusion) | data formatting | bytes 7864320 | tf_op jit(solution)/shard_map/convert_element_type | solution.py:161
  158.1 2.3 subtract_convert_fusion
  160.5 73.6 %while.27 = (s32[]{:T(128)}, f32[32,1600]{1,0:T(8,128)S(1)}, s32[12]{0:T(128)S(1)}, bf16[32,24576]{1,0:T(8,128)(2,1)}, bf16[40,24576]{1,0:T(8,128)(2,1)S(1)}, /*...) while((s32[]{:T(128)}, f32[32,1600]{1,0:T(8,128)S(1)}, s32[12]{0:T(128)S(1)}, ...), condition=%wide.region_3.4_spmd.clone, body=%wide.region_2.3_spmd.clone.sunk | while | flops 216453120 | bytes 14467249 | solution.py:194
  161.8 1.9 multiply_convert_fusion.6
  163.6 2.9 convolution_add_fusion.2
  167.9 1.9 multiply_convert_fusion.6
  169.8 2.9 convolution_add_fusion.2
  175.9 2.9 convolution_add_fusion.2
  182.0 2.9 convolution_add_fusion.2
  186.3 1.9 multiply_convert_fusion.6
  188.2 2.9 convolution_add_fusion.2
  194.3 2.9 convolution_add_fusion.2
  200.4 2.9 convolution_add_fusion.2
  204.7 1.9 multiply_convert_fusion.6
  206.6 2.9 convolution_add_fusion.2
  210.8 1.9 multiply_convert_fusion.6
  212.7 2.9 convolution_add_fusion.2
  218.8 2.9 convolution_add_fusion.2
  224.9 2.9 convolution_add_fusion.2
  231.1 2.9 convolution_add_fusion.2
  236.1 2.7 psum.15
  238.8 16.9 %all-reduce.24.cloned.1.call-done = bf16[32,1600]{1,0:T(8,128)(2,1)} async-done(((bf16[32,1600]{1,0:T(8,128)(2,1)}), bf16[32,1600]{1,0:T(8,128)(2,1)}) %all-reduce.24.cloned.1.call-update) | async-done | bytes 102416 | tf_op jit(solution)/shard_map/psum | solution.py:196
  276.3 3.2 collective-permute-start
  281.4 3.5 collective-permute-done.1
  284.9 3.2 collective-permute-start.2
  289.5 3.6 copy.50
  294.2 29.5 %while.26 = (s32[]{:T(128)}, bf16[2,8,128,1600]{2,3,1,0:T(8,128)(2,1)}, s32[2]{0:T(128)S(1)}, f32[16,4]{0,1:T(4,128)S(1)}, f32[4,28800]{1,0:T(4,128)S(1)}, /*ind...) while((s32[]{:T(128)}, bf16[2,8,128,1600]{2,3,1,0:T(8,128)(2,1)}, ...), condition=%wide.region_10.11_spmd.clone, body=%wide.region_9.10_spmd.clone.sunk | while | flops 366603520 | bytes 7424503 | solution.py:218
  297.3 11.8 %bitcast_dynamic-update-slice_fusion.2 = bf16[2,8,128,1600]{2,3,1,0:T(8,128)(2,1)} fusion(bf16[2,8,128,1600]{2,3,1,0:T(8,128)(2,1)} %get-tuple-element.302, s32[]{:T(128)S(6)} %copy.78, f32[8,18,1600]{2,1,0:T(8,128)S(1)} %reshape.441, f32[18]{0:T(128)S(1)} %get-tuple-element.316), kind=kOutput, calls=%fused_computation.2.clone.1 | convolution fusion | flops 355544320 | bytes 4198476 | tf_op jit(solution)/shard_map/while/body/eval_jaxpr/yb,xbn->xyn/dot_general | solution.py:216
  311.9 11.8 %bitcast_dynamic-update-slice_fusion.2 = bf16[2,8,128,1600]{2,3,1,0:T(8,128)(2,1)} fusion(bf16[2,8,128,1600]{2,3,1,0:T(8,128)(2,1)} %get-tuple-element.302, s32[]{:T(128)S(6)} %copy.78, f32[8,18,1600]{2,1,0:T(8,128)S(1)} %reshape.441, f32[18]{0:T(128)S(1)} %get-tuple-element.316), kind=kOutput, calls=%fused_computation.2.clone.1 | convolution fusion | flops 355544320 | bytes 4198476 | tf_op jit(solution)/shard_map/while/body/eval_jaxpr/yb,xbn->xyn/dot_general | solution.py:216
  323.7 4.2 %constant_dynamic-slice_fusion = bf16[16,128,20,40]{1,3,2,0:T(8,128)(2,1)} fusion(bf16[16,128,40,40]{1,3,2,0:T(8,128)(2,1)} %bitcast.121, s32[]{:T(128)S(6)} %select_n.218), kind=kLoop, calls=%fused_computation.153 | loop fusion | bytes 6553604 | tf_op jit(solution)/shard_map/dynamic_slice | solution.py:221
  327.9 11.9 %copy.56 = bf16[16,128,20,40]{3,2,1,0:T(8,128)(2,1)} copy(bf16[16,128,20,40]{1,3,2,0:T(8,128)(2,1)} %constant_dynamic-slice_fusion) | data formatting | bytes 6553600
  339.8 9.2 %convert_bitcast_fusion.1 = bf16[40,8,16,128]{0,1,3,2:T(8,128)(2,1)} fusion(bf16[16,128,20,40]{3,2,1,0:T(8,128)(2,1)} %copy.56, bf16[20,8,16,128]{0,1,3,2:T(8,128)(2,1)} %copy.50), kind=kOutput, calls=%fused_computation.42 | convolution fusion | flops 26869760 | bytes 5242880 | tf_op jit(solution)/shard_map/klxy,xykj->jlxy/dot_general | solution.py:227
  349.0 6.3 %copy.51 = bf16[40,8,16,128]{3,2,1,0:T(8,128)(2,1)} copy(bf16[40,8,16,128]{0,1,3,2:T(8,128)(2,1)} %convert_bitcast_fusion.1) | data formatting | bytes 2621440 | tf_op jit(solution)/shard_map/convert_element_type | solution.py:227
  355.3 16.3 %reduce-scatter.2.cloned.1.call-done = bf16[20,8,16,128]{3,2,1,0:T(8,128)(2,1)} async-done(((bf16[40,8,16,128]{3,2,1,0:T(8,128)(2,1)}), bf16[20,8,16,128]{3,2,1,0:T(8,128)(2,1)}) %reduce-scatter.2.cloned.1.call-update) | async-done | bytes 655376 | tf_op jit(solution)/shard_map/reduce_scatter | solution.py:226
  (238 shorter events, 102.9 us)
Async XLA Ops:
  6.5 27.3 %copy-start = (bf16[1,20,192,128]{3,2,1,0:T(8,128)(2,1)S(1)}, bf16[1,20,192,128]{3,2,1,0:T(8,128)(2,1)}, u32[]{:S(2)}) copy-start(bf16[1,20,192,128]{3,2,1,0:T(8,128)(2,1)} %param.19) | copy-start | bytes 2949124
  8.9 9.4 %copy-start.28 = (pred[64]{0:T(512)(128)(4,1)}, pred[64]{0:T(512)(128)(4,1)S(1)}, u32[]{:S(2)}) copy-start(pred[64]{0:T(512)(128)(4,1)S(1)} %get-tuple-element.171) | copy-start | bytes 196
  9.0 4.9 %copy-start.26 = (pred[64]{0:T(512)(128)(4,1)}, pred[64]{0:T(512)(128)(4,1)S(1)}, u32[]{:S(2)}) copy-start(pred[64]{0:T(512)(128)(4,1)S(1)} %get-tuple-element.191) | copy-start | bytes 196
  9.0 5.5 %copy-start.24 = (pred[64]{0:T(512)(128)(4,1)}, pred[64]{0:T(512)(128)(4,1)S(1)}, u32[]{:S(2)}) copy-start(pred[64]{0:T(512)(128)(4,1)S(1)} %get-tuple-element.184) | copy-start | bytes 196
  9.0 6.1 %copy-start.22 = (pred[64]{0:T(512)(128)(4,1)}, pred[64]{0:T(512)(128)(4,1)S(1)}, u32[]{:S(2)}) copy-start(pred[64]{0:T(512)(128)(4,1)S(1)} %get-tuple-element.185) | copy-start | bytes 196
  9.0 6.6 %copy-start.20 = (pred[64]{0:T(512)(128)(4,1)}, pred[64]{0:T(512)(128)(4,1)S(1)}, u32[]{:S(2)}) copy-start(pred[64]{0:T(512)(128)(4,1)S(1)} %get-tuple-element.186) | copy-start | bytes 196
  9.0 7.2 %copy-start.18 = (pred[64]{0:T(512)(128)(4,1)}, pred[64]{0:T(512)(128)(4,1)S(1)}, u32[]{:S(2)}) copy-start(pred[64]{0:T(512)(128)(4,1)S(1)} %get-tuple-element.187) | copy-start | bytes 196
  9.0 7.8 %copy-start.16 = (pred[64]{0:T(512)(128)(4,1)}, pred[64]{0:T(512)(128)(4,1)S(1)}, u32[]{:S(2)}) copy-start(pred[64]{0:T(512)(128)(4,1)S(1)} %get-tuple-element.188) | copy-start | bytes 196
  9.0 8.4 %copy-start.14 = (pred[64]{0:T(512)(128)(4,1)}, pred[64]{0:T(512)(128)(4,1)S(1)}, u32[]{:S(2)}) copy-start(pred[64]{0:T(512)(128)(4,1)S(1)} %get-tuple-element.189) | copy-start | bytes 196
  9.0 8.7 %copy-start.10 = (pred[64]{0:T(512)(128)(4,1)}, pred[64]{0:T(512)(128)(4,1)S(1)}, u32[]{:S(2)}) copy-start(pred[64]{0:T(512)(128)(4,1)S(1)} %get-tuple-element.190) | copy-start | bytes 196
  9.0 9.0 %copy-start.12 = (pred[64]{0:T(512)(128)(4,1)}, pred[64]{0:T(512)(128)(4,1)S(1)}, u32[]{:S(2)}) copy-start(pred[64]{0:T(512)(128)(4,1)S(1)} %get-tuple-element.183) | copy-start | bytes 196
  18.2 1.3 copy-start.9
  18.5 1.0 copy-start.4
  20.5 61.9 %all-to-all-start = ((s32[1,64,768]{2,0,1:T(1,128)}), s32[1,64,768]{2,0,1:T(1,128)S(1)}, u32[]{:S(2)}, u32[]{:S(2)}) async-start(s32[1,64,768]{2,0,1:T(1,128)} %copy.42), calls=%async_computation | async-start | bytes 393216 | tf_op jit(solution)/shard_map/all_to_all | solution.py:150
  33.1 12.6 %copy-start.7 = (f32[40,40]{1,0:T(8,128)}, f32[40,40]{1,0:T(8,128)S(1)}, u32[]{:S(2)}) copy-start(f32[40,40]{1,0:T(8,128)S(1)} %fusion.64) | copy-start | bytes 19204
  41.3 2.1 copy-start.3
  41.3 4.5 %copy-start.6 = (pred[64,768]{1,0:T(8,128)(4,1)S(1)}, pred[64,768]{1,0:T(8,128)(4,1)}, u32[]{:S(2)}) copy-start(pred[64,768]{1,0:T(8,128)(4,1)} %iota_compare_fusion.1) | copy-start | bytes 147460
  47.7 3.5 copy-start.2
  47.7 3.5 copy-start.27
  52.9 1.9 copy-start.25
  56.3 1.9 copy-start.23
  59.7 1.9 copy-start.21
  63.1 1.9 copy-start.19
  66.7 1.9 copy-start.17
  70.1 1.9 copy-start.15
  73.5 0.7 copy-start.11
  75.4 0.7 copy-start.13
  77.4 0.6 copy-start.29
  82.5 18.9 %all-to-all-start.1 = ((bf16[2,64,768]{2,0,1:T(2,128)(2,1)}), bf16[2,64,768]{2,0,1:T(2,128)(2,1)S(1)}, u32[]{:S(2)}, u32[]{:S(2)}) async-start(bf16[2,64,768]{2,0,1:T(2,128)(2,1)} %copy.43), calls=%async_computation.1 | async-start | bytes 393216 | tf_op jit(solution)/shard_map/all_to_all | solution.py:149
  101.3 33.2 %all-to-all-start.2 = ((bf16[20,64,768]{2,0,1:T(8,128)(2,1)}), bf16[20,64,768]{2,0,1:T(8,128)(2,1)S(1)}, u32[]{:S(2)}, u32[]{:S(2)}) async-start(bf16[20,64,768]{2,0,1:T(8,128)(2,1)} %copy.46), calls=%async_computation.2 | async-start | bytes 4718592 | tf_op jit(solution)/shard_map/all_to_all | solution.py:148
  106.4 149.3 %all-reduce.24.cloned.1.call-start = ((), (), s32[]{:S(2)}) async-start(), calls=%async_computation.5 | async-start | bytes 212992 | tf_op jit(solution)/shard_map/psum | solution.py:196
  234.7 136.8 %reduce-scatter.2.cloned.1.call-start = ((), (), s32[]{:S(2)}) async-start(), calls=%async_computation.6 | async-start | bytes 1966080 | tf_op jit(solution)/shard_map/reduce_scatter | solution.py:226
  234.8 22.3 %copy-start.8 = (f32[40,40]{1,0:T(8,128)S(1)}, f32[40,40]{1,0:T(8,128)}, u32[]{:S(2)}) copy-start(f32[40,40]{1,0:T(8,128)} %copy-done.7) | copy-start | bytes 19204
  272.7 6.8 %copy-start.30 = (f32[4]{0:T(128)S(1)}, f32[4]{0:T(128)}, u32[]{:S(2)}) copy-start(f32[4]{0:T(128)} %multiply_add_fusion.3) | copy-start | bytes 52
  272.7 16.8 %copy-start.5 = (bf16[20,8,16,128]{3,2,1,0:T(8,128)(2,1)S(1)}, bf16[20,8,16,128]{3,2,1,0:T(8,128)(2,1)}, u32[]{:S(2)}) copy-start(bf16[20,8,16,128]{3,2,1,0:T(8,128)(2,1)} %param.25) | copy-start | bytes 1966084
  276.3 5.0 %collective-permute-start = (bf16[1,16,1600]{2,1,0:T(8,128)(2,1)S(1)}, bf16[1,16,1600]{2,1,0:T(8,128)(2,1)S(1)}, u32[]{:S(2)}, u32[]{:S(2)}) collective-permute-start(bf16[1,16,1600]{2,1,0:T(8,128)(2,1)S(1)} %slice.226), channel_id=1, source_target_pairs={{0,32},{32,64},{64,96},{1,33},{33,65},{65,97},{2,34},{34,66},{66,9... | collective-permute-start | bytes 153608 | tf_op jit(solution)/shard_map/ppermute | solution.py:20
  280.0 4.9 %collective-permute-start.1 = (bf16[1,16,1600]{2,1,0:T(8,128)(2,1)S(1)}, bf16[1,16,1600]{2,1,0:T(8,128)(2,1)S(1)}, u32[]{:S(2)}, u32[]{:S(2)}) collective-permute-start(bf16[1,16,1600]{2,1,0:T(8,128)(2,1)S(1)} %slice.228), channel_id=1, source_target_pairs={{32,0},{64,32},{96,64},{33,1},{65,33},{97,65},{34,2},{66,34},{98,6... | collective-permute-start | bytes 153608 | tf_op jit(solution)/shard_map/ppermute | solution.py:23
  284.9 8.2 %collective-permute-start.2 = (bf16[4,1,1600]{2,1,0:T(2,128)(2,1)S(1)}, bf16[4,1,1600]{2,1,0:T(2,128)(2,1)S(1)}, u32[]{:S(2)}, u32[]{:S(2)}) collective-permute-start(bf16[4,1,1600]{2,1,0:T(2,128)(2,1)S(1)} %get-tuple-element.177), channel_id=1, source_target_pairs={{0,2},{2,4},{4,6},{6,8},{8,10},{10,12},{12,14},{14,16},{16,18},{18... | collective-permute-start | bytes 38408 | tf_op jit(solution)/shard_map/ppermute | solution.py:20
  288.1 5.0 %collective-permute-start.3 = (bf16[4,1,1600]{2,1,0:T(2,128)(2,1)S(1)}, bf16[4,1,1600]{2,1,0:T(2,128)(2,1)S(1)}, u32[]{:S(2)}, u32[]{:S(2)}) collective-permute-start(bf16[4,1,1600]{2,1,0:T(2,128)(2,1)S(1)} %get-tuple-element.178), channel_id=1, source_target_pairs={{2,0},{4,2},{6,4},{8,6},{10,8},{12,10},{14,12},{16,14},{18,16},{20... | collective-permute-start | bytes 38408 | tf_op jit(solution)/shard_map/ppermute | solution.py:23
  339.8 31.8 %copy-start.1 = (bf16[1,20,192,128]{3,2,1,0:T(8,128)(2,1)S(1)}, bf16[1,20,192,128]{3,2,1,0:T(8,128)(2,1)}, u32[]{:S(2)}) copy-start(bf16[1,20,192,128]{3,2,1,0:T(8,128)(2,1)} %param.19) | copy-start | bytes 2949124
Sparse Core Ops, SparseCore 0:
  234.8 20.8 all-reduce.23
  355.4 16.1 reduce-scatter.1
where the time goes:
time: 386 us; the launch traced here: 379 us
  matrix products  99.9 us (26%)
  local copies, waits for them, and re-layouts  72.2 us (19%)
  waiting for transfers between devices  71.4 us (18%)
  other arithmetic  60.9 us (16%)
  starting transfers between devices  36.5 us (9%)
  between operations  15 us (4%)
  blocking collectives  13.1 us (3%)
  loops' own time  9.9 us (3%)
    dot_general x12, matrix products, add_block(): jnp.einsum('cq,nq->cn', weights_here, pairs, preferred_element_type=jnp.f...  35.3 us
    all_to_all x1, waiting for transfers between devices, per_device(): lax.all_to_all(send_obs, ('tx', 'ty'), split_axis=1, concat_axis=1, tiled...  25.8 us
    dot_general x2, matrix products, fine_rows(): jnp.einsum('yb,xbn->xyn', table_y, along, precision=exact)  23.6 us
    convert_element_type x12, other arithmetic, add_block(): pairs = (columns[:, None, :] * columns[None, :, :]).reshape(members * mem...  22.5 us
    unnamed x68, local copies, waits for them, and re-layouts  18.5 us
    psum x1, waiting for transfers between devices, per_device(): lax.psum(gram.astype(jnp.bfloat16), 'mem').astype(jnp.float32)  16.9 us
    reduce_scatter x1, waiting for transfers between devices, per_device(): lax.psum_scatter(jnp.einsum('klxy,xykj->jlxy', state, selected, preferred...  16.3 us
    select_n x19, other arithmetic, window_rows(): window = jnp.where(taken[None, :, None], moved, window)  15.5 us
  transfers between devices with their start and end apart: 9, of which 5 were waited for; matrix products, arithmetic and copies ran while one was open for 15% of the time, Pallas kernels for 0%

commit v1 on v0

v1 whole, which is shorter than its diff:
```python
import numpy as np
import jax
import jax.numpy as jnp
from jax import lax
from jax.experimental import pallas as pl
from jax.experimental.pallas import tpu as pltpu
from jax.sharding import PartitionSpec as P

B = 8
LOC = 16
NS = 5
STEP = 512
SUB = 128
CHUNKS = 16


def pair_list():
    pairs = []
    for low in range(5):
        for high in range(low, 5):
            for turn in range(5 if low == high else 8):
                pairs.append((low, high, turn))
    for low in range(5):
        pairs.append((low, -1, 0))
    return pairs


def gram_kernel(
    count_ref, volume_ref, matrix_hbm, value_ref, error_ref, cell_ref, out_ref,
    wide, matrix, lhs, rhs, total, offsets, sems,
):
    radar_blocks = matrix.shape[0]
    tiles = count_ref.shape[1]
    chunk = radar_blocks // CHUNKS
    steps = radar_blocks * SUB // STEP
    per_step = STEP // SUB
    rows = total.shape[1]

    def fetch(index):
        part = pl.ds(index * chunk, chunk)
        return pltpu.make_async_copy(matrix_hbm.at[part], matrix.at[part], sems.at[index])

    for index in range(CHUNKS):
        fetch(index).start()

    offsets[0] = 0

    def add_count(tile, running):
        running = running + count_ref[0, tile]
        offsets[tile + 1] = running
        return running

    everything = lax.fori_loop(0, tiles, add_count, jnp.int32(0))
    for extra in range(8):
        offsets[tiles + 1 + extra] = everything

    def widen(member, carry):
        start = pl.multiple_of(member * radar_blocks, 8)
        wide[pl.ds(start, radar_blocks), :] = volume_ref[member].astype(jnp.float32)
        return carry

    lax.fori_loop(0, volume_ref.shape[0], widen, 0)
    total[...] = jnp.zeros_like(total)
    lhs[...] = jnp.zeros_like(lhs)

    centre_y = lax.broadcasted_iota(jnp.int32, (16, STEP), 0).astype(jnp.float32) * B + (B - 1) / 2
    lane = lax.broadcasted_iota(jnp.int32, (1, STEP), 1)
    chosen = pair_list()
    half = len(chosen) // 2

    def one_step(step, group, products):
        base = pl.multiple_of(step * STEP, STEP)
        here = pl.ds(base, STEP)
        cells = cell_ref[:, here]
        pos_x = (cells >> 7).astype(jnp.float32)
        pos_y = (cells & 127).astype(jnp.float32)
        inverse = (1.0 / error_ref[:, here]).astype(jnp.bfloat16).astype(jnp.float32)
        near_y = jnp.exp((pos_y - centre_y) ** 2 * (-0.5 / LOC**2)) * inverse
        weight = []
        for i in range(2):
            near_x = jnp.exp((pos_x - (i * B + (B - 1) / 2)) ** 2 * (-0.5 / LOC**2))
            weight.append((near_x * near_y).astype(jnp.bfloat16).astype(jnp.float32))
        weight = jnp.concatenate(weight, axis=0)
        values = value_ref[:, here].astype(jnp.float32)
        for sub in range(per_step):
            block = step * per_step + sub
            gates = wide[pl.ds(block, 40, stride=radar_blocks), :].astype(jnp.bfloat16)
            obs = jnp.dot(gates, matrix[block], preferred_element_type=jnp.float32)
            obs = obs.astype(jnp.bfloat16).astype(jnp.float32)
            mean = jnp.sum(obs, axis=0, keepdims=True) * (1.0 / 40)
            anomaly = (obs - mean).astype(jnp.bfloat16).astype(jnp.float32)
            innovation = values[:, sub * SUB:(sub + 1) * SUB] - mean
            part = [anomaly[8 * i:8 * i + 8] for i in range(5)]
            turned = {}
            made = []
            for low, high, turn in products:
                if high < 0:
                    made.append(part[low] * innovation)
                    continue
                if (high, turn) not in turned:
                    turned[high, turn] = part[high] if turn == 0 else pltpu.roll(part[high], turn, 0)
                made.append(part[low] * turned[high, turn])
            lanes = slice(sub * SUB, (sub + 1) * SUB)
            for index in range(0, len(made), 2):
                both = jnp.concatenate(
                    [made[index], made[index + 1] if index + 1 < len(made) else jnp.zeros_like(made[0])], axis=0
                )
                lhs[index * 8:index * 8 + 16, lanes] = both.astype(jnp.bfloat16)

        slot = lane + base

        def window(group):
            for i in range(8):
                first = offsets[group * 4 + i]
                last = offsets[group * 4 + i + 1]
                inside = (slot >= first) & (slot < last)
                rhs[i * 32:i * 32 + 32, :] = jnp.where(inside, weight, 0.0).astype(jnp.bfloat16)
            added = lax.dot_general(
                lhs[...], rhs[...], (((1,), (1,)), ((), ())), preferred_element_type=jnp.float32
            )
            total[group] += added[:, :128]
            total[group + 1] += added[:, 128:]

        group = lax.while_loop(lambda g: offsets[g * 4 + 4] <= base, lambda g: g + 1, group)

        def more(g):
            return (g < tiles // 4) & (offsets[jnp.minimum(g, tiles // 4) * 4] < base + STEP)

        def do(g):
            window(g)
            return g + 2

        lax.while_loop(more, do, group)
        return group

    mem = lax.axis_index("mem")
    for core in range(2):
        products = chosen[core * half:core * half + half]

        @pl.when(mem == core)
        def _():
            def chunk_loop(index, group):
                fetch(index).wait()
                count = steps // CHUNKS
                for inner in range(count):
                    group = one_step(index * count + inner, group, products)
                return group

            lax.fori_loop(0, CHUNKS, chunk_loop, jnp.int32(0))

    for group in range(tiles // 4):
        out_ref[group] = total[group].astype(jnp.bfloat16)


def gram(counts, volume, matrix, values, errors, cells):
    blocks = matrix.shape[0]
    tiles = counts.shape[1]
    rows = 448
    return pl.pallas_call(
        gram_kernel,
        out_shape=jax.ShapeDtypeStruct((tiles // 4, rows, 128), jnp.bfloat16),
        in_specs=[
            pl.BlockSpec(memory_space=pltpu.SMEM),
            pl.BlockSpec(memory_space=pltpu.VMEM),
            pl.BlockSpec(memory_space=pl.ANY),
            pl.BlockSpec(memory_space=pltpu.VMEM),
            pl.BlockSpec(memory_space=pltpu.VMEM),
            pl.BlockSpec(memory_space=pltpu.VMEM),
        ],
        out_specs=pl.BlockSpec(memory_space=pltpu.VMEM),
        scratch_shapes=[
            pltpu.VMEM((40 * blocks, 128), jnp.float32),
            pltpu.VMEM((blocks, 128, 128), jnp.bfloat16),
            pltpu.VMEM((rows, STEP), jnp.bfloat16),
            pltpu.VMEM((256, STEP), jnp.bfloat16),
            pltpu.VMEM((tiles // 4 + 1, rows, 128), jnp.float32),
            pltpu.SMEM((tiles + 9,), jnp.int32),
            pltpu.SemaphoreType.DMA((CHUNKS,)),
        ],
        compiler_params=pltpu.CompilerParams(vmem_limit_bytes=56 * 1024 * 1024),
        name="gram",
    )(counts, volume, matrix, values, errors, cells)


def apply_kernel(points_ref, tent_x_ref, tent_y_ref, state_ref, out_ref, fine, flat, result):
    levels, width_x, width_y = state_ref.shape[1:]
    members = state_ref.shape[0]
    own = out_ref.shape[0]
    points = points_ref[...].astype(jnp.float32).T.astype(jnp.bfloat16)

    def widen(member, carry):
        start = pl.multiple_of(member * levels * width_x, 8)
        flat[pl.ds(start, levels * width_x), :] = (
            state_ref[member].astype(jnp.float32).reshape(levels * width_x, width_y)
        )
        return carry

    lax.fori_loop(0, members, widen, 0)
    for x in range(0, width_x, 2):
        tent = jnp.concatenate(
            [tent_x_ref[:, x + i:x + i + 1] * tent_y_ref[...] for i in range(2)], axis=1
        ).astype(jnp.bfloat16)
        made = jnp.dot(points, tent, preferred_element_type=jnp.float32)
        made = made.astype(jnp.bfloat16).astype(jnp.float32)
        fine[x] = made[:, :128]
        fine[x + 1] = made[:, 128:]

    def column(x, carry):
        def add(k4, sums):
            sums = list(sums)
            for i in range(4):
                k = k4 * 4 + i
                field = flat[pl.ds(k * (levels * width_x) + x, levels, stride=width_x), :]
                for j in range(own):
                    row = fine[x, pl.ds(k * 32 + j, 8, stride=0), :]
                    sums[j] = sums[j] + row * field
            return tuple(sums)

        zero = jnp.zeros((levels, width_y), jnp.float32)
        sums = lax.fori_loop(0, members // 4, add, (zero,) * own)
        for j in range(own):
            result[pl.ds(j * (levels * width_x) + x, levels, stride=width_x), :] = sums[j]
        return carry

    lax.fori_loop(0, width_x, column, 0)

    def narrow(j, carry):
        start = pl.multiple_of(j * levels * width_x, 8)
        out_ref[j] = (
            result[pl.ds(start, levels * width_x), :]
            .reshape(levels, width_x, width_y)
            .astype(jnp.bfloat16)
        )
        return carry

    lax.fori_loop(0, own, narrow, 0)


def apply(points, tent_x, tent_y, state):
    members, levels, width_x, width_y = state.shape
    own = members // 2
    return pl.pallas_call(
        apply_kernel,
        out_shape=jax.ShapeDtypeStruct((own, levels, width_x, width_y), jnp.bfloat16),
        in_specs=[pl.BlockSpec(memory_space=pltpu.VMEM)] * 4,
        out_specs=pl.BlockSpec(memory_space=pltpu.VMEM),
        scratch_shapes=[
            pltpu.VMEM((width_x, points.shape[1], width_y), jnp.float32),
            pltpu.VMEM((members * levels * width_x, width_y), jnp.float32),
            pltpu.VMEM((own * levels * width_x, width_y), jnp.float32),
        ],
        compiler_params=pltpu.CompilerParams(vmem_limit_bytes=48 * 1024 * 1024),
        name="apply",
    )(points, tent_x, tent_y, state)


exact = lax.Precision.HIGHEST


def padded_2(block, sides, width):
    for axis, dim in sides:
        count = lax.axis_size(axis)
        forward = [(i, i + 1) for i in range(count - 1)]
        backward = [(target, source) for source, target in forward]
        low = lax.ppermute(
            lax.slice_in_dim(block, block.shape[dim] - width, None, axis=dim), axis, forward
        )
        high = lax.ppermute(lax.slice_in_dim(block, 0, width, axis=dim), axis, backward)
        block = jnp.concatenate([low, block, high], axis=dim)
    return block


def tent_table(length, nodes, spacing):
    position = jnp.arange(length, dtype=jnp.float32)[:, None]
    centre = (jnp.arange(nodes, dtype=jnp.float32)[None, :] - 1.0) * spacing + (spacing - 1) * 0.5
    return jnp.maximum(0.0, 1.0 - jnp.abs(position - centre) / spacing)


def coarse_weights(gram, inform):
    members = inform.shape[1]
    identity = jnp.eye(members, dtype=jnp.float32)
    amat = identity + gram.reshape(-1, members, members) / (members - 1)
    scale = jnp.sqrt(jnp.sum(amat * amat, axis=(1, 2)))[:, None, None]
    upper = amat / scale
    lower = jnp.broadcast_to(identity, amat.shape)
    for sweep in range(NS):
        middle = 1.5 * identity - 0.5 * jnp.einsum("cij,cjk->cik", lower, upper, precision=exact)
        upper = jnp.einsum("cij,cjk->cik", upper, middle, precision=exact)
        lower = jnp.einsum("cij,cjk->cik", middle, lower, precision=exact)
    inv_half = lower / jnp.sqrt(scale)
    step_one = jnp.einsum("cij,cj->ci", inv_half, inform, precision=exact)
    mean_shift = jnp.einsum("cij,cj->ci", inv_half, step_one, precision=exact) / (members - 1)
    shift = mean_shift - jnp.mean(mean_shift, axis=1, keepdims=True)
    spread = inv_half - jnp.mean(inv_half, axis=1, keepdims=True)
    trans = 1.0 / members + shift[:, :, None] + spread
    return trans.reshape(trans.shape[0], members * members)


def pair_table():
    table = np.zeros((880, 40, 40), np.float32)
    for index, (low, high, turn) in enumerate(pair_list()):
        if high < 0:
            continue
        for s in range(8):
            k, j = 8 * low + s, 8 * high + (s - turn) % 8
            if low == high and turn == 4 and s >= 4:
                continue
            table[index * 8 + s, k, j] = 1
            table[index * 8 + s, j, k] = 1
    return table.reshape(880, 1600).astype(jnp.bfloat16)


def per_device(volume, super_matrix, observed, error_var, obs_cells, counts, state):
    all_volume = lax.all_gather(volume[0], "mem", axis=0, tiled=True)
    all_state = lax.all_gather(state, "mem", axis=0, tiled=True)
    partial = gram(counts, all_volume, super_matrix[0], observed, error_var, obs_cells)
    by_tile = partial[:, :440].reshape(16, 440, 4, 32).transpose(0, 2, 1, 3).reshape(64, 440, 32)
    mine = lax.psum_scatter(by_tile, ("tx", "ty"), scatter_dimension=0, tiled=True)[0]
    rows = lax.all_gather(mine, "mem", axis=0, tiled=True)
    full = jnp.einsum("rc,rn->cn", rows, jnp.asarray(pair_table()), preferred_element_type=jnp.float32)
    inform = rows[840:].astype(jnp.float32).T
    trans = coarse_weights(full, inform).reshape(2, 16, 1600)
    padded = padded_2(trans.astype(jnp.bfloat16), (("tx", 0), ("ty", 1)), 1)
    index_tx, index_ty = lax.axis_index("tx"), lax.axis_index("ty")
    count_tx, count_ty = lax.axis_size("tx"), lax.axis_size("ty")
    padded = padded.at[0].set(jnp.where(index_tx == 0, padded[1], padded[0]))
    padded = padded.at[-1].set(jnp.where(index_tx == count_tx - 1, padded[-2], padded[-1]))
    padded = padded.at[:, 0].set(jnp.where(index_ty == 0, padded[:, 1], padded[:, 0]))
    padded = padded.at[:, -1].set(jnp.where(index_ty == count_ty - 1, padded[:, -2], padded[:, -1]))
    own = lax.dynamic_slice_in_dim(padded.reshape(72, 40, 40), lax.axis_index("mem") * 20, 20, 2)
    points = jnp.pad(own, ((0, 56), (0, 0), (0, 12))).reshape(128, 1280)
    tent_x = jnp.pad(jnp.repeat(tent_table(16, 4, B), 18, axis=1).T, ((0, 56), (0, 0)))
    tent_y = jnp.pad(jnp.tile(tent_table(128, 18, B), (1, 4)).T, ((0, 56), (0, 0)))
    return apply(points, tent_x, tent_y, all_state)


def solution(mesh):
    placed = (
        P(("tx", "ty"), "mem", None, None),
        P(("tx", "ty"), None, None, None),
        P(("tx", "ty"), None),
        P(("tx", "ty"), None),
        P(("tx", "ty"), None),
        P(("tx", "ty"), None),
        P("mem", None, "tx", "ty"),
    )
    return jax.shard_map(
        per_device,
        mesh=mesh,
        in_specs=placed,
        out_specs=P("mem", None, "tx", "ty"),
        check_vma=False,
    )
```

time: 386 us -> 490 us (1.27); the launches traced: 379 us -> 488 us
  waiting for transfers between devices: 71.4 us -> 329 us
  matrix products: 99.9 us -> 19.3 us
  other arithmetic: 60.9 us -> 4.66 us
  local copies, waits for them, and re-layouts: 72.2 us -> 19.8 us
  Pallas kernels: 0 us -> 42.1 us
  blocking collectives: 13.1 us -> 54.1 us
  starting transfers between devices: 36.5 us -> 5.25 us
  loops' own time: 9.9 us -> 0 us
    reduce_scatter x1, waiting for transfers between devices: 16.3 us -> 303 us  [per_device(): lax.psum_scatter(by_tile, ('tx', 'ty'), scatter_dimension=0, tiled=True)[0]]
    dot_general x23 -> x1, matrix products: 81.4 us -> 0.73 us  [per_device(): jnp.einsum('rc,rn->cn', rows, jnp.asarray(pair_table()), preferred_elemen...]
    all_gather x0 -> x1, blocking collectives: none -> 54.1 us  [per_device(): rows = lax.all_gather(mine, 'mem', axis=0, tiled=True)]
    pallas_call x0 -> x2, Pallas kernels: none -> 42.1 us  [the longest x1 33.1 us: gram(): pl.pallas_call(gram_kernel, out_shape=jax.ShapeDtypeStruct((tiles // 4, r...]
    convert_element_type x38 -> x1, other arithmetic: 36.1 us -> 0.25 us  [per_device(): padded = padded_2(trans.astype(jnp.bfloat16), (('tx', 0), ('ty', 1)), 1)]
    all_to_all x3 -> x0, waiting for transfers between devices: 34.6 us -> none  [the longest x1 25.8 us: per_device(): lax.all_to_all(send_obs, ('tx', 'ty'), split_axis=1, concat_axis=1, tiled...]
    all_to_all x3 -> x0, starting transfers between devices: 27.4 us -> none  [the longest x1 12.5 us: per_device(): lax.all_to_all(send_cells, ('tx', 'ty'), split_axis=1, concat_axis=1, til...]
    all_gather x0 -> x2, waiting for transfers between devices: none -> 18.5 us  [the longest x1 18.5 us: per_device(): all_volume = lax.all_gather(volume[0], 'mem', axis=0, tiled=True)]
  transfers between devices with their start and end apart: 9 -> 7, of which waited for: 5 -> 4; matrix products, arithmetic and copies ran while one was open for 15% -> 5% of each run, Pallas kernels for 0% -> 0%
where the time goes in v1:
time: 490 us; the launch traced here: 488 us
  waiting for transfers between devices  329 us (67%)
  blocking collectives  54.1 us (11%)
  Pallas kernels  42.1 us (9%)
  local copies, waits for them, and re-layouts  19.8 us (4%)
  matrix products  19.3 us (4%)
  between operations  13.5 us (3%)
  starting transfers between devices  5.25 us (1%)
    reduce_scatter x1, waiting for transfers between devices, per_device(): lax.psum_scatter(by_tile, ('tx', 'ty'), scatter_dimension=0, tiled=True)[0]  303 us
    all_gather x1, blocking collectives, per_device(): rows = lax.all_gather(mine, 'mem', axis=0, tiled=True)  54.1 us
    pallas_call x1, Pallas kernels, gram(): pl.pallas_call(gram_kernel, out_shape=jax.ShapeDtypeStruct((tiles // 4, r...  33.1 us
    all_gather x1, waiting for transfers between devices, per_device(): all_volume = lax.all_gather(volume[0], 'mem', axis=0, tiled=True)  18.5 us
  transfers between devices with their start and end apart: 7, of which 4 were waited for; matrix products, arithmetic and copies ran while one was open for 5% of the time, Pallas kernels for 0%

profile of v1, /device:TPU:1, one launch (start us, length us, event | category | flops | bytes accessed | tf_op | source)
XLA Modules:
  0.0 488.1 jit_solution(3044772283983692146)
XLA Ops:
  6.5 0.7 all-gather.7.cloned.1.call-update
  7.3 18.5 %all-gather.7.cloned.1.call-done = bf16[1,40,192,128]{3,2,0,1:T(8,128)(2,1)} async-done(((bf16[1,20,192,128]{3,2,0,1:T(8,128)(2,1)}), bf16[1,40,192,128]{3,2,0,1:T(8,128)(2,1)}) %all-gather.7.cloned.1.call-update) | async-done | bytes 1966096 | tf_op jit(solution)/shard_map/all_gather | solution.py:314
  25.8 33.1 %gram.1 = bf16[16,448,128]{2,1,0:T(8,128)(2,1)} custom-call(s32[1,64]{1,0:T(1,128)} %count_ref.1, bf16[40,192,128]{2,1,0:T(8,128)(2,1)} %bitcast.58, bf16[192,128,128]{2,1,0:T(8,128)(2,1)} %bitcast.57, bf16[1,24576]{1,0:T(2,128)(2,1)} %value_ref.1, f32[1,24576]{1,0:T(1,128)} %error_ref.1, s32[1,24576]{1,0:T(1,128)} %cell_ref.1), custom_call_target="tpu_custom_call" | custom-call | tf_op jit(solution)/shard_map/gram/pallas_call | solution.py:159
  58.9 5.0 %fusion.15 = (bf16[16,440,32]{2,1,0:T(8,128)(2,1)S(1)}, bf16[16,440,32]{2,1,0:T(8,128)(2,1)S(1)}, bf16[16,440,32]{2,1,0:T(8,128)(2,1)S(1)}, bf16[16,440,32]{2,1,0:T(8,128)(2,1)S(1)}) fusion(bf16[16,448,128]{2,1,0:T(8,128)(2,1)} %gram.1), kind=kLoop, calls=%fused_computation.47 | loop fusion | bytes 3604480 | tf_op jit(solution)/shard_map/slice.90
  63.9 3.8 pad_maximum_fusion
  67.7 7.6 %copy.56 = bf16[64,440,32]{1,2,0:T(8,128)(2,1)} copy(bf16[64,440,32]{2,1,0:T(8,128)(2,1)} %bitcast.56) | data formatting | bytes 3604480 | tf_op jit(solution)/shard_map/reshape | solution.py:317
  75.4 0.7 all-gather.5.cloned.1.call-update
  76.3 303.0 %reduce-scatter.2.cloned.1.call-done = bf16[1,440,32]{1,2,0:T(8,128)(2,1)} async-done(((bf16[64,440,32]{1,2,0:T(8,128)(2,1)}), bf16[1,440,32]{1,2,0:T(8,128)(2,1)}) %reduce-scatter.2.cloned.1.call-update) | async-done | bytes 28176 | tf_op jit(solution)/shard_map/reduce_scatter | solution.py:318
  379.2 1.6 copy.57
  380.9 54.1 %all-gather.1 = bf16[1,880,32]{2,0,1:T(2,128)(2,1)S(1)} all-gather(bf16[1,440,32]{2,0,1:T(2,128)(2,1)} %copy.57), channel_id=3, replica_groups=mesh['tx'=4,'ty'=16,'mem'=2] {'mem'}, dimensions={1}, use_global_device_ids=true | all-gather | bytes 84480 | tf_op jit(solution)/shard_map/all_gather | solution.py:319
  435.0 0.8 copy.58
  435.7 0.7 multiply_reduce_fusion
  436.5 0.3 div.54
  436.8 1.2 fusion.4
  438.0 1.3 fusion.10
  439.3 1.2 fusion.5
  440.5 1.2 fusion.3
  441.7 1.2 fusion.20
  442.8 1.2 fusion.19
  444.0 1.2 fusion.2
  445.2 1.2 fusion.22
  446.4 1.2 fusion.21
  447.5 1.4 fusion.1
  449.0 1.2 fusion.24
  450.1 1.2 fusion.23
  451.4 1.2 fusion
  452.6 1.2 fusion.18
  453.8 0.6 convolution_bitcast_fusion
  454.4 1.1 fusion.25
  455.7 0.2 add_convert_fusion
  456.0 0.1 slice.148
  456.2 1.3 collective-permute-start
  457.5 0.2 convert_element_type.34
  457.7 0.1 slice.150
  457.9 1.3 collective-permute-start.1
  459.2 3.5 collective-permute-done.1
  462.8 1.3 collective-permute-start.2
  464.1 1.3 collective-permute-start.3
  465.8 2.9 collective-permute-done.3
  468.7 0.1 pad_maximum_fusion.1
  469.0 0.2 scatter.16
  469.3 0.2 scatter.19
  469.4 0.7 reshape.215
  470.2 0.3 constant_dynamic-slice_fusion
  470.4 0.5 copy.69
  471.1 0.2 copy.62.points_ref
  471.3 1.3 copy-done
  472.6 9.0 %apply.1 = bf16[20,8,16,128]{3,2,1,0:T(8,128)(2,1)} custom-call(bf16[128,1280]{1,0:T(8,128)(2,1)S(1)} %copy.62.points_ref, f32[128,16]{1,0:T(8,128)S(1)} %pad.21.tent_x_ref, f32[128,128]{1,0:T(8,128)S(1)} %pad.22.tent_y_ref, bf16[40,8,16,128]{3,2,1,0:T(8,128)(2,1)S(1)} %copy-done), custom_call_target="tpu_custom_call" | custom-call | tf_op jit(solution)/shard_map/apply/pallas_call | solution.py:242
  (41 shorter events, 1.3 us)
Async XLA Ops:
  6.5 19.2 %all-gather.7.cloned.1.call-start = ((), (), s32[]{:S(2)}) async-start(), calls=%async_computation.3 | async-start | bytes 2949120 | tf_op jit(solution)/shard_map/all_gather | solution.py:314
  7.3 372.0 %reduce-scatter.2.cloned.1.call-start = ((), (), s32[]{:S(2)}) async-start(), calls=%async_computation.1 | async-start | bytes 2129920 | tf_op jit(solution)/shard_map/reduce_scatter | solution.py:318
  75.3 360.4 %copy-start.1 = (bf16[880,1600]{1,0:T(8,128)(2,1)S(1)}, bf16[880,1600]{1,0:T(8,128)(2,1)}, u32[]{:S(2)}) copy-start(bf16[880,1600]{1,0:T(8,128)(2,1)} %constant.174.clone) | copy-start | bytes 8448004
  75.3 395.9 %all-gather.5.cloned.1.call-start = ((), (), s32[]{:S(2)}) async-start(), calls=%async_computation.2 | async-start | bytes 1966080 | tf_op jit(solution)/shard_map/all_gather | solution.py:315
  456.2 3.0 collective-permute-start
  457.9 4.9 collective-permute-start.1
  462.8 2.9 collective-permute-start.2
  464.1 4.6 collective-permute-start.3
  471.3 1.3 copy-start
Sparse Core Ops, SparseCore 0:
  9.0 16.7 all-gather.6
  75.4 303.7 reduce-scatter.1
  381.0 58.7 all-gather.4

commit v2 on v1

--- a/solution.py
+++ b/solution.py
@@ -26,7 +26,7 @@
 
 
 def gram_kernel(
-    count_ref, volume_ref, matrix_hbm, value_ref, error_ref, cell_ref, out_ref,
+    count_ref, volume_ref, other_ref, matrix_hbm, value_ref, error_ref, cell_ref, ab_ref, c_ref,
     wide, matrix, lhs, rhs, total, offsets, sems,
 ):
     radar_blocks = matrix.shape[0]
@@ -54,12 +54,17 @@
     for extra in range(8):
         offsets[tiles + 1 + extra] = everything
 
+    mem = lax.axis_index("mem")
+    held = volume_ref.shape[0]
+
     def widen(member, carry):
-        start = pl.multiple_of(member * radar_blocks, 8)
+        start = pl.multiple_of((mem * held + member) * radar_blocks, 8)
         wide[pl.ds(start, radar_blocks), :] = volume_ref[member].astype(jnp.float32)
+        start = pl.multiple_of(((1 - mem) * held + member) * radar_blocks, 8)
+        wide[pl.ds(start, radar_blocks), :] = other_ref[member].astype(jnp.float32)
         return carry
 
-    lax.fori_loop(0, volume_ref.shape[0], widen, 0)
+    lax.fori_loop(0, held, widen, 0)
     total[...] = jnp.zeros_like(total)
     lhs[...] = jnp.zeros_like(lhs)
 
@@ -133,7 +138,6 @@
         lax.while_loop(more, do, group)
         return group
 
-    mem = lax.axis_index("mem")
     for core in range(2):
         products = chosen[core * half:core * half + half]
 
@@ -148,26 +152,33 @@
 
             lax.fori_loop(0, CHUNKS, chunk_loop, jnp.int32(0))
 
-    for group in range(tiles // 4):
-        out_ref[group] = total[group].astype(jnp.bfloat16)
-
-
-def gram(counts, volume, matrix, values, errors, cells):
+    for x in range(4):
+        for y in range(4):
+            ab_ref[x, y] = total[x * 4 + y, :PART_A + PART_B].astype(jnp.bfloat16)
+        for z, value in enumerate(block_swap([total[x * 4 + y, PART_A + PART_B:] for y in range(4)])):
+            c_ref[z, x] = value.astype(jnp.bfloat16)
+
+
+def gram(counts, volume, other, matrix, values, errors, cells):
     blocks = matrix.shape[0]
     tiles = counts.shape[1]
     rows = 448
     return pl.pallas_call(
         gram_kernel,
-        out_shape=jax.ShapeDtypeStruct((tiles // 4, rows, 128), jnp.bfloat16),
+        out_shape=(
+            jax.ShapeDtypeStruct((4, 4, PART_A + PART_B, 128), jnp.bfloat16),
+            jax.ShapeDtypeStruct((4, 4, PART_C, 128), jnp.bfloat16),
+        ),
         in_specs=[
             pl.BlockSpec(memory_space=pltpu.SMEM),
+            pl.BlockSpec(memory_space=pltpu.VMEM),
             pl.BlockSpec(memory_space=pltpu.VMEM),
             pl.BlockSpec(memory_space=pl.ANY),
             pl.BlockSpec(memory_space=pltpu.VMEM),
             pl.BlockSpec(memory_space=pltpu.VMEM),
             pl.BlockSpec(memory_space=pltpu.VMEM),
         ],
-        out_specs=pl.BlockSpec(memory_space=pltpu.VMEM),
+        out_specs=(pl.BlockSpec(memory_space=pltpu.VMEM), pl.BlockSpec(memory_space=pltpu.VMEM)),
         scratch_shapes=[
             pltpu.VMEM((40 * blocks, 128), jnp.float32),
             pltpu.VMEM((blocks, 128, 128), jnp.bfloat16),
@@ -179,26 +190,33 @@
         ],
         compiler_params=pltpu.CompilerParams(vmem_limit_bytes=56 * 1024 * 1024),
         name="gram",
-    )(counts, volume, matrix, values, errors, cells)
-
-
-def apply_kernel(points_ref, tent_x_ref, tent_y_ref, state_ref, out_ref, fine, flat, result):
+    )(counts, volume, other, matrix, values, errors, cells)
+
+
+def apply_kernel(points_ref, tent_x_ref, tent_y_ref, state_ref, other_ref, out_ref, fine, flat, result):
     levels, width_x, width_y = state_ref.shape[1:]
-    members = state_ref.shape[0]
     own = out_ref.shape[0]
-    points = points_ref[...].astype(jnp.float32).T.astype(jnp.bfloat16)
+    members = 2 * own
+    mem, tx, ty = lax.axis_index("mem"), lax.axis_index("tx"), lax.axis_index("ty")
+    kind_x = jnp.where(tx == 0, 0, jnp.where(tx == lax.axis_size("tx") - 1, 2, 1))
+    kind_y = jnp.where(ty == 0, 0, jnp.where(ty == lax.axis_size("ty") - 1, 2, 1))
+    tent_x, tent_y = tent_x_ref[kind_x], tent_y_ref[kind_y]
+    points = points_ref[...].astype(jnp.float32)
+    points = jnp.concatenate([points, jnp.zeros((48, points.shape[1]), jnp.float32)], axis=0).T
+    points = points[:, :80].astype(jnp.bfloat16)
 
     def widen(member, carry):
-        start = pl.multiple_of(member * levels * width_x, 8)
-        flat[pl.ds(start, levels * width_x), :] = (
-            state_ref[member].astype(jnp.float32).reshape(levels * width_x, width_y)
-        )
+        for source, first in ((state_ref, mem * own), (other_ref, (1 - mem) * own)):
+            start = pl.multiple_of((first + member) * levels * width_x, 8)
+            flat[pl.ds(start, levels * width_x), :] = (
+                source[member].astype(jnp.float32).reshape(levels * width_x, width_y)
+            )
         return carry
 
-    lax.fori_loop(0, members, widen, 0)
+    lax.fori_loop(0, own, widen, 0)
     for x in range(0, width_x, 2):
         tent = jnp.concatenate(
-            [tent_x_ref[:, x + i:x + i + 1] * tent_y_ref[...] for i in range(2)], axis=1
+            [tent_x[:, x + i:x + i + 1] * tent_y for i in range(2)], axis=1
         ).astype(jnp.bfloat16)
         made = jnp.dot(points, tent, preferred_element_type=jnp.float32)
         made = made.astype(jnp.bfloat16).astype(jnp.float32)
@@ -236,13 +254,13 @@
     lax.fori_loop(0, own, narrow, 0)
 
 
-def apply(points, tent_x, tent_y, state):
-    members, levels, width_x, width_y = state.shape
-    own = members // 2
+def apply(points, tent_x, tent_y, state, other):
+    own, levels, width_x, width_y = state.shape
+    members = 2 * own
     return pl.pallas_call(
         apply_kernel,
         out_shape=jax.ShapeDtypeStruct((own, levels, width_x, width_y), jnp.bfloat16),
-        in_specs=[pl.BlockSpec(memory_space=pltpu.VMEM)] * 4,
+        in_specs=[pl.BlockSpec(memory_space=pltpu.VMEM)] * 5,
         out_specs=pl.BlockSpec(memory_space=pltpu.VMEM),
         scratch_shapes=[
             pltpu.VMEM((width_x, points.shape[1], width_y), jnp.float32),
@@ -251,87 +269,458 @@
         ],
         compiler_params=pltpu.CompilerParams(vmem_limit_bytes=48 * 1024 * 1024),
         name="apply",
-    )(points, tent_x, tent_y, state)
-
-
-exact = lax.Precision.HIGHEST
-
-
-def padded_2(block, sides, width):
-    for axis, dim in sides:
-        count = lax.axis_size(axis)
-        forward = [(i, i + 1) for i in range(count - 1)]
-        backward = [(target, source) for source, target in forward]
-        low = lax.ppermute(
-            lax.slice_in_dim(block, block.shape[dim] - width, None, axis=dim), axis, forward
+    )(points, tent_x, tent_y, state, other)
+
+
+MESH = pl.DeviceIdType.MESH
+PART_A, PART_B, PART_C = 160, 160, 128
+GROUPS = 6
+WIDE = 256
+LINK_LANES = 1280
+
+
+def place_of(row):
+    if row < PART_A:
+        return row % (PART_A // 4), row // (PART_A // 4)
+    row -= PART_A
+    if row < PART_B:
+        return PART_A // 4 + row % (PART_B // 4), row // (PART_B // 4)
+    row -= PART_B
+    return (PART_A + PART_B) // 4 + row % (PART_C // 4), row // (PART_C // 4)
+
+
+def pick_tables():
+    rows = np.zeros((1648, WIDE), np.float32)
+    quarters = np.zeros((1648, 128), np.float32)
+
+    def put(target, product, s):
+        core, local = divmod(product * 8 + s, 440)
+        row, quarter = place_of(local)
+        rows[target] = 0
+        quarters[target] = 0
+        rows[target, core * 112 + row] = 1
+        quarters[target, quarter * 32:quarter * 32 + 32] = 1
+
+    for product, (low, high, turn) in enumerate(pair_list()):
+        for s in range(8):
+            if high < 0:
+                put(1600 + 8 * low + s, product, s)
+                continue
+            k, j = 8 * low + s, 8 * high + (s - turn) % 8
+            put(j * 40 + k, product, s)
+            put(k * 40 + j, product, s)
+    return rows.astype(jnp.bfloat16), quarters
+
+
+def lane_table():
+    lanes = np.arange(WIDE)
+    table = np.full((8, WIDE), -1, np.int32)
+    table[0] = np.where(lanes < 240, lanes // 40, 7)
+    table[1] = np.where(lanes < 240, lanes % 40, -1)
+    return table
+
+
+def block_swap(arrays):
+    lane = lax.broadcasted_iota(jnp.int32, arrays[0].shape, 1)
+    for step, mask in ((2, lane < 64), (1, (lane & 32) == 0)):
+        turned = list(arrays)
+        for low in range(4):
+            if low & step:
+                continue
+            first, second = arrays[low], arrays[low + step]
+            turned[low] = jnp.where(mask, first, pltpu.roll(second, 32 * step, 1))
+            turned[low + step] = jnp.where(mask, pltpu.roll(first, 128 - 32 * step, 1), second)
+        arrays = turned
+    return arrays
+
+
+def split(value):
+    high = value.astype(jnp.bfloat16)
+    return high, (value - high.astype(jnp.float32)).astype(jnp.bfloat16)
+
+
+def bdot(left, right):
+    return jnp.dot(left, right, preferred_element_type=jnp.float32)
+
+
+def coarse_points(summed, pick_ref, quarter_ref, lane_ref, picked, spread_rows, rows, mem):
+    lane_i, lane_j = lane_ref[0:1], lane_ref[1:2]
+    high, low = split(summed)
+    both = jnp.concatenate(
+        [jnp.concatenate([high, low], axis=1).astype(jnp.float32), jnp.zeros((32, WIDE), jnp.float32)], axis=0
+    ).astype(jnp.bfloat16)
+    quarters = quarter_ref[...]
+    found = bdot(pick_ref[...], both)
+    picked[...] = jnp.concatenate(
+        [found[:, :128] * quarters, found[:, 128:] * quarters], axis=1
+    ).astype(jnp.bfloat16)
+    row_c = lax.broadcasted_iota(jnp.int32, (WIDE, WIDE), 0) & 31
+    eye = (lax.broadcasted_iota(jnp.int32, (40, WIDE), 0) == lane_j).astype(jnp.float32)
+    real = lane_j >= 0
+    same = (
+        (jnp.concatenate(
+            [jnp.full((40, WIDE), i, jnp.int32) for i in range(6)] + [jnp.full((16, WIDE), 9, jnp.int32)], axis=0
+        ) == lane_i)
+        .astype(jnp.float32)
+        .astype(jnp.bfloat16)
+    )
+
+    def blocks(value):
+        parts = [jnp.where(lane_i == i, value, 0.0) for i in range(6)] + [jnp.zeros((16, WIDE), jnp.float32)]
+        return split(jnp.concatenate(parts, axis=0))
+
+    def times(values, right):
+        right_high, right_low = right
+        highs, lows = zip(*[split(value) for value in values])
+        count = len(values) * 40
+        stack = jnp.concatenate([part.astype(jnp.float32) for part in highs + lows], axis=0).astype(jnp.bfloat16)
+        main = bdot(stack, right_high)
+        rest = bdot(stack[:count], right_low)
+        return [
+            main[40 * i:40 * i + 40] + (main[count + 40 * i:count + 40 * i + 40] + rest[40 * i:40 * i + 40])
+            for i in range(len(values))
+        ]
+
+    uppers, lowers, scales, informs = [], [], [], []
+    for group in range(GROUPS):
+        expand = (row_c == lane_i + 6 * group).astype(jnp.float32) * real.astype(jnp.float32)
+        spread_rows[...] = bdot(picked[...], expand.astype(jnp.bfloat16))
+        gram = jnp.zeros((40, WIDE), jnp.float32)
+        for j in range(40):
+            gram = jnp.where(lane_j == j, spread_rows[40 * j:40 * j + 40], gram)
+        informs.append(spread_rows[1600:1640])
+        amat = eye + gram * (1.0 / 39)
+        square = jnp.sum(amat * amat, axis=0, keepdims=True)
+        first = square.astype(jnp.bfloat16).astype(jnp.float32)
+        second = (square - first).astype(jnp.bfloat16).astype(jnp.float32)
+        third = square - first - second
+        parts = jnp.concatenate(
+            [jnp.broadcast_to(part, (8, WIDE)) for part in (first, second, third, jnp.zeros_like(third))], axis=0
         )
-        high = lax.ppermute(lax.slice_in_dim(block, 0, width, axis=dim), axis, backward)
-        block = jnp.concatenate([low, block, high], axis=dim)
-    return block
-
-
-def tent_table(length, nodes, spacing):
-    position = jnp.arange(length, dtype=jnp.float32)[:, None]
-    centre = (jnp.arange(nodes, dtype=jnp.float32)[None, :] - 1.0) * spacing + (spacing - 1) * 0.5
-    return jnp.maximum(0.0, 1.0 - jnp.abs(position - centre) / spacing)
-
-
-def coarse_weights(gram, inform):
-    members = inform.shape[1]
-    identity = jnp.eye(members, dtype=jnp.float32)
-    amat = identity + gram.reshape(-1, members, members) / (members - 1)
-    scale = jnp.sqrt(jnp.sum(amat * amat, axis=(1, 2)))[:, None, None]
-    upper = amat / scale
-    lower = jnp.broadcast_to(identity, amat.shape)
-    for sweep in range(NS):
-        middle = 1.5 * identity - 0.5 * jnp.einsum("cij,cjk->cik", lower, upper, precision=exact)
-        upper = jnp.einsum("cij,cjk->cik", upper, middle, precision=exact)
-        lower = jnp.einsum("cij,cjk->cik", middle, lower, precision=exact)
-    inv_half = lower / jnp.sqrt(scale)
-    step_one = jnp.einsum("cij,cj->ci", inv_half, inform, precision=exact)
-    mean_shift = jnp.einsum("cij,cj->ci", inv_half, step_one, precision=exact) / (members - 1)
-    shift = mean_shift - jnp.mean(mean_shift, axis=1, keepdims=True)
-    spread = inv_half - jnp.mean(inv_half, axis=1, keepdims=True)
-    trans = 1.0 / members + shift[:, :, None] + spread
-    return trans.reshape(trans.shape[0], members * members)
-
-
-def pair_table():
-    table = np.zeros((880, 40, 40), np.float32)
-    for index, (low, high, turn) in enumerate(pair_list()):
-        if high < 0:
-            continue
-        for s in range(8):
-            k, j = 8 * low + s, 8 * high + (s - turn) % 8
-            if low == high and turn == 4 and s >= 4:
-                continue
-            table[index * 8 + s, k, j] = 1
-            table[index * 8 + s, j, k] = 1
-    return table.reshape(880, 1600).astype(jnp.bfloat16)
+        norm = bdot(parts.astype(jnp.bfloat16), same)
+        norm = norm[0:1] + norm[8:9] + norm[16:17]
+        scale = jnp.sqrt(jnp.where(real, norm, 1.0))
+        scales.append(scale)
+        uppers.append(amat / scale)
+    for group in range(GROUPS):
+        middle = 1.5 * eye - 0.5 * uppers[group]
+        lowers.append(middle)
+        uppers[group] = times([uppers[group]], blocks(middle))[0]
+    for sweep in range(1, NS):
+        middles = []
+        for group in range(GROUPS):
+            product = times([lowers[group]], blocks(uppers[group]))[0]
+            middles.append(blocks(1.5 * eye - 0.5 * product))
+        for group in range(GROUPS):
+            if sweep < NS - 1:
+                uppers[group], lowers[group] = times([uppers[group], lowers[group]], middles[group])
+            else:
+                lowers[group] = times([lowers[group]], middles[group])[0]
+    target = lax.broadcasted_iota(jnp.int32, (WIDE, 768), 1)
+    source = lax.broadcasted_iota(jnp.int32, (WIDE, 768), 0)
+    own = target & 31
+    wanted = (target >> 7) * 40 + mem * 20 + own
+    choose = ((source == wanted) & (own < 20)).astype(jnp.float32).astype(jnp.bfloat16)
+    for group in range(GROUPS):
+        inv_half = lowers[group] / jnp.sqrt(scales[group])
+        step_one = jnp.sum(inv_half * informs[group], axis=0, keepdims=True)
+        product = inv_half * step_one
+        high, low = split(product)
+        stack = jnp.concatenate([high.astype(jnp.float32), low.astype(jnp.float32)], axis=0).astype(jnp.bfloat16)
+        moved = bdot(stack, same)
+        shift = (moved[:40] + moved[40:]) * (1.0 / 39)
+        shift = shift - jnp.sum(shift, axis=0, keepdims=True) * (1.0 / 40)
+        spread = inv_half - jnp.sum(inv_half, axis=0, keepdims=True) * (1.0 / 40)
+        trans = (1.0 / 40 + shift + spread).astype(jnp.bfloat16)
+        chosen = bdot(trans, choose)
+        for i in range(6):
+            point = group * 6 + i
+            if point < 32:
+                rows[point * 40:point * 40 + 40, :] = chosen[:, i * 128:i * 128 + 128]
+
+
+def gather_members(rows, lane):
+    quarter = lane >> 5
+    pieces = []
+    for q in range(10):
+        piece = rows[pl.ds(4 * q, 32, stride=40), :]
+        for p in range(1, 4):
+            piece = jnp.where(quarter == p, rows[pl.ds(4 * q + p, 32, stride=40), :], piece)
+        pieces.append(piece)
+    return jnp.concatenate(pieces, axis=1)
+
+
+def swap_kernel(volume_ref, other_ref, send, recv):
+    mem = lax.axis_index("mem")
+    mate = (lax.axis_index("tx"), lax.axis_index("ty"), 1 - mem)
+    barrier = pltpu.get_barrier_semaphore()
+    pl.semaphore_signal(barrier, inc=1, device_id=mate, device_id_type=MESH)
+    pl.semaphore_wait(barrier, 1)
+    count = send.shape[0]
+    share = volume_ref.shape[0] // count
+    copies = []
+    for index in range(count):
+        part = pl.ds(index * share, share)
+        copies.append(
+            pltpu.make_async_remote_copy(
+                src_ref=volume_ref.at[part], dst_ref=other_ref.at[part], send_sem=send.at[index],
+                recv_sem=recv.at[index], device_id=mate, device_id_type=MESH,
+            )
+        )
+    for copy in copies:
+        copy.start()
+    for copy in copies:
+        copy.wait()
+
+
+def swap(volume):
+    return pl.pallas_call(
+        swap_kernel,
+        out_shape=jax.ShapeDtypeStruct(volume.shape, volume.dtype),
+        in_specs=[pl.BlockSpec(memory_space=pl.ANY)],
+        out_specs=pl.BlockSpec(memory_space=pl.ANY),
+        scratch_shapes=[pltpu.SemaphoreType.DMA((4,)), pltpu.SemaphoreType.DMA((4,))],
+        compiler_params=pltpu.CompilerParams(collective_id=0, has_side_effects=True),
+        name="swap",
+    )(volume)
+
+
+def coarse_kernel(
+    ab_ref, c_ref, pick_ref, quarter_ref, lane_ref, state_ref, points_ref, other_ref,
+    own_a, own_b, own_c, got_a, got_b, got_c, next_a, next_b, next_c, got_a2, got_b2, got_c2,
+    last_a, last_b, last_c, got_a3, got_b3, got_c3, summed, picked, spread_rows, rows, edges, columns, halo,
+    send, recv, local,
+):
+    x, ty, mem = lax.axis_index("tx"), lax.axis_index("ty"), lax.axis_index("mem")
+    y, z = ty // 4, ty % 4
+    mate = (x, ty, 1 - mem)
+
+    def along(axis, turn):
+        if axis == 0:
+            return ((x + turn) % 4, ty, mem)
+        if axis == 1:
+            return (x, ((y + turn) % 4) * 4 + z, mem)
+        return (x, y * 4 + (z + turn) % 4, mem)
+
+    around = []
+    for side, step in ((0, 1), (1, 15)):
+        for turn in range(3):
+            around.append((side, turn, ((x + 5 - turn) % 4, (ty + step) % 16, mem)))
+    peers = [along(axis, turn) for axis in range(3) for turn in range(1, 4)] + [mate]
+    peers += [along(0, 1), along(0, 3)] + [device for _, _, device in around]
+    barrier = pltpu.get_barrier_semaphore()
+    for device in peers:
+        pl.semaphore_signal(barrier, inc=1, device_id=device, device_id_type=MESH)
+
+    mine = [
+        pltpu.make_async_copy(ab_ref.at[x, :, pl.ds(0, PART_A)], own_a, local.at[0]),
+        pltpu.make_async_copy(ab_ref.at[:, y, pl.ds(PART_A, PART_B)], own_b, local.at[1]),
+        pltpu.make_async_copy(c_ref.at[z], own_c, local.at[2]),
+    ]
+    for copy in mine:
+        copy.start()
+    pl.semaphore_wait(barrier, len(peers))
+
+    def link(source, target, index, device):
+        copy = pltpu.make_async_remote_copy(
+            src_ref=source, dst_ref=target, send_sem=send.at[index], recv_sem=recv.at[index],
+            device_id=device, device_id_type=MESH,
+        )
+        copy.start()
+        return copy
+
+    started = []
+
+    def stage(number, axis, source, target):
+        copies = []
+        for turn in (2, 1, 3):
+            place = ((x, y, z)[axis] + turn) % 4
+            copies.append(link(source(place), target.at[turn - 1], number * 3 + turn - 1, along(axis, turn)))
+        started.extend(copies)
+        return copies
+
+    first = [
+        stage(0, 0, lambda place: ab_ref.at[place, :, pl.ds(0, PART_A)], got_a),
+        stage(1, 1, lambda place: ab_ref.at[:, place, pl.ds(PART_A, PART_B)], got_b),
+        stage(2, 2, lambda place: c_ref.at[place], got_c),
+    ]
+    state_copy = link(state_ref, other_ref, 27, mate)
+
+    def wait_all(copies):
+        for copy in copies:
+            copy.wait_recv()
+
+    def add_up(own, got, index):
+        value = own[index].astype(jnp.float32)
+        for turn in range(3):
+            value = value + got[turn, index].astype(jnp.float32)
+        return value
+
+    def add_last(own, got):
+        value = own.astype(jnp.float32)
+        for turn in range(3):
+            value = value + got[turn].astype(jnp.float32)
+        return value
+
+    mine[0].wait()
+    wait_all(first[0])
+    for index in range(4):
+        next_a[index] = add_up(own_a, got_a, index).astype(jnp.bfloat16)
+    second_a = stage(3, 1, lambda place: next_a.at[place], got_a2)
+    mine[1].wait()
+    wait_all(first[1])
+    for index, value in enumerate(block_swap([add_up(own_b, got_b, index) for index in range(4)])):
+        next_b[index] = value.astype(jnp.bfloat16)
+    second_b = stage(4, 2, lambda place: next_b.at[place], got_b2)
+    mine[2].wait()
+    wait_all(first[2])
+    for index in range(4):
+        next_c[index] = add_up(own_c, got_c, index).astype(jnp.bfloat16)
+    second_c = stage(5, 0, lambda place: next_c.at[place], got_c2)
+
+    def quarter_rows(value, target):
+        size = value.shape[0] // 4
+        for index, part in enumerate(block_swap([value[i * size:(i + 1) * size] for i in range(4)])):
+            target[index] = part
+
+    wait_all(second_a)
+    quarter_rows(add_last(next_a[y], got_a2), last_a)
+    third_a = stage(6, 2, lambda place: last_a.at[place], got_a3)
+    wait_all(second_b)
+    quarter_rows(add_last(next_b[z], got_b2), last_b)
+    third_b = stage(7, 0, lambda place: last_b.at[place], got_b3)
+    wait_all(second_c)
+    quarter_rows(add_last(next_c[x], got_c2), last_c)
+    third_c = stage(8, 1, lambda place: last_c.at[place], got_c3)
+
+    wait_all(third_a)
+    summed[mem, 0:40] = add_last(last_a[z], got_a3)
+    wait_all(third_b)
+    summed[mem, 40:80] = add_last(last_b[x], got_b3)
+    wait_all(third_c)
+    summed[mem, 80:112] = add_last(last_c[y], got_c3)
+    halves = link(summed.at[mem], summed.at[mem], 28, mate)
+    halves.wait_recv()
+
+    coarse_points(
+        summed[...].reshape(224, 128), pick_ref, quarter_ref, lane_ref, picked, spread_rows, rows, mem
+    )
+    lane = lax.broadcasted_iota(jnp.int32, (32, 128), 1)
+    points = gather_members(rows, lane)
+    edges[...] = points.astype(jnp.bfloat16)
+    line = lax.broadcasted_iota(jnp.int32, (16, LINK_LANES), 0)
+    copies = [
+        link(edges.at[pl.ds(16, 16)], halo.at[0], 29, along(0, 1)),
+        link(edges.at[pl.ds(0, 16)], halo.at[1], 30, along(0, 3)),
+    ]
+    for side, turn, device in around:
+        index = side * 3 + turn
+        column = 15 if side == 0 else 0
+        value = jnp.where(
+            line == 2 * index, points[column:column + 1],
+            jnp.where(line == 2 * index + 1, points[16 + column:17 + column], 0.0),
+        )
+        columns[index] = value.astype(jnp.bfloat16)
+        copies.append(link(columns.at[index], halo.at[2 + index], 31 + index, device))
+    points_ref[0:32, :] = edges[...]
+    wait_all(copies)
+    points_ref[32:48, :] = halo[0]
+    points_ref[48:64, :] = halo[1]
+    total = halo[2].astype(jnp.float32)
+    for index in range(1, 6):
+        total = total + halo[2 + index].astype(jnp.float32)
+    points_ref[64:80, :] = total.astype(jnp.bfloat16)
+    for copy in started + copies + [halves]:
+        copy.wait_send()
+    state_copy.wait()
+
+
+def coarse(partial_ab, partial_c, state):
+    pick, quarter = pick_tables()
+    bf16, f32 = jnp.bfloat16, jnp.float32
+    part = ((PART_A, bf16), (PART_B, bf16), (PART_C, bf16))
+    return pl.pallas_call(
+        coarse_kernel,
+        out_shape=(
+            jax.ShapeDtypeStruct((80, LINK_LANES), bf16),
+            jax.ShapeDtypeStruct(state.shape, state.dtype),
+        ),
+        in_specs=[
+            pl.BlockSpec(memory_space=pl.ANY),
+            pl.BlockSpec(memory_space=pl.ANY),
+            pl.BlockSpec(memory_space=pltpu.VMEM),
+            pl.BlockSpec(memory_space=pltpu.VMEM),
+            pl.BlockSpec(memory_space=pltpu.VMEM),
+            pl.BlockSpec(memory_space=pl.ANY),
+        ],
+        out_specs=(pl.BlockSpec(memory_space=pltpu.VMEM), pl.BlockSpec(memory_space=pl.ANY)),
+        scratch_shapes=[pltpu.VMEM((4, size, 128), kind) for size, kind in part]
+        + [pltpu.VMEM((3, 4, size, 128), kind) for size, kind in part]
+        + [pltpu.VMEM((4, size, 128), kind) for size, kind in part]
+        + [pltpu.VMEM((3, size, 128), kind) for size, kind in part]
+        + [pltpu.VMEM((4, size // 4, 128), f32) for size, kind in part]
+        + [pltpu.VMEM((3, size // 4, 128), f32) for size, kind in part]
+        + [
+            pltpu.VMEM((2, 112, 128), f32),
+            pltpu.VMEM((1648, WIDE), bf16),
+            pltpu.VMEM((1648, WIDE), f32),
+            pltpu.VMEM((1280, 128), f32),
+            pltpu.VMEM((32, LINK_LANES), bf16),
+            pltpu.VMEM((6, 16, LINK_LANES), bf16),
+            pltpu.VMEM((8, 16, LINK_LANES), bf16),
+            pltpu.SemaphoreType.DMA((37,)),
+            pltpu.SemaphoreType.DMA((37,)),
+            pltpu.SemaphoreType.DMA((3,)),
+        ],
+        compiler_params=pltpu.CompilerParams(
+            collective_id=1, has_side_effects=True, vmem_limit_bytes=48 * 1024 * 1024
+        ),
+        name="coarse",
+    )(partial_ab, partial_c, jnp.asarray(pick), jnp.asarray(quarter), jnp.asarray(lane_table()), state)
+
+
+def tent(length, nodes):
+    position = np.arange(length, dtype=np.float32)[:, None]
+    centre = (np.arange(nodes, dtype=np.float32)[None, :] - 1.0) * B + (B - 1) * 0.5
+    return np.maximum(0.0, 1.0 - np.abs(position - centre) / B)
+
+
+def tent_tables():
+    place_x, place_y = np.full(80, -1), np.full(80, -1)
+    for i in range(2):
+        for j in range(16):
+            place_x[i * 16 + j], place_y[i * 16 + j] = i + 1, j + 1
+            place_x[32 + i * 16 + j], place_y[32 + i * 16 + j] = 3 * i, j + 1
+    for side in range(2):
+        for turn in range(3):
+            for i in range(2):
+                row = 64 + (side * 3 + turn) * 2 + i
+                place_y[row] = 17 * side
+                place_x[row] = {1: i + 1, 0: 0 if i == 1 else -1, 2: 3 if i == 0 else -1}[turn]
+    tables = []
+    for length, nodes, place in ((16, 4, place_x), (128, 18, place_y)):
+        table = np.zeros((3, 80, length), np.float32)
+        for kind in range(3):
+            weights = tent(length, nodes)
+            if kind == 0:
+                weights[:, 1] += weights[:, 0]
+                weights[:, 0] = 0
+            if kind == 2:
+                weights[:, -2] += weights[:, -1]
+                weights[:, -1] = 0
+            for row in range(80):
+                if place[row] >= 0:
+                    table[kind, row] = weights[:, place[row]]
+        tables.append(table)
+    return tables
 
 
 def per_device(volume, super_matrix, observed, error_var, obs_cells, counts, state):
-    all_volume = lax.all_gather(volume[0], "mem", axis=0, tiled=True)
-    all_state = lax.all_gather(state, "mem", axis=0, tiled=True)
-    partial = gram(counts, all_volume, super_matrix[0], observed, error_var, obs_cells)
-    by_tile = partial[:, :440].reshape(16, 440, 4, 32).transpose(0, 2, 1, 3).reshape(64, 440, 32)
-    mine = lax.psum_scatter(by_tile, ("tx", "ty"), scatter_dimension=0, tiled=True)[0]
-    rows = lax.all_gather(mine, "mem", axis=0, tiled=True)
-    full = jnp.einsum("rc,rn->cn", rows, jnp.asarray(pair_table()), preferred_element_type=jnp.float32)
-    inform = rows[840:].astype(jnp.float32).T
-    trans = coarse_weights(full, inform).reshape(2, 16, 1600)
-    padded = padded_2(trans.astype(jnp.bfloat16), (("tx", 0), ("ty", 1)), 1)
-    index_tx, index_ty = lax.axis_index("tx"), lax.axis_index("ty")
-    count_tx, count_ty = lax.axis_size("tx"), lax.axis_size("ty")
-    padded = padded.at[0].set(jnp.where(index_tx == 0, padded[1], padded[0]))
-    padded = padded.at[-1].set(jnp.where(index_tx == count_tx - 1, padded[-2], padded[-1]))
-    padded = padded.at[:, 0].set(jnp.where(index_ty == 0, padded[:, 1], padded[:, 0]))
-    padded = padded.at[:, -1].set(jnp.where(index_ty == count_ty - 1, padded[:, -2], padded[:, -1]))
-    own = lax.dynamic_slice_in_dim(padded.reshape(72, 40, 40), lax.axis_index("mem") * 20, 20, 2)
-    points = jnp.pad(own, ((0, 56), (0, 0), (0, 12))).reshape(128, 1280)
-    tent_x = jnp.pad(jnp.repeat(tent_table(16, 4, B), 18, axis=1).T, ((0, 56), (0, 0)))
-    tent_y = jnp.pad(jnp.tile(tent_table(128, 18, B), (1, 4)).T, ((0, 56), (0, 0)))
-    return apply(points, tent_x, tent_y, all_state)
+    other_volume = swap(volume[0])
+    partial_ab, partial_c = gram(counts, volume[0], other_volume, super_matrix[0], observed, error_var, obs_cells)
+    points, other_state = coarse(partial_ab, partial_c, state)
+    tent_x, tent_y = tent_tables()
+    return apply(points, jnp.asarray(tent_x), jnp.asarray(tent_y), state, other_state)
 
 
 def solution(mesh):

time: 490 us -> 90.1 us (0.18)
  waiting for transfers between devices: 329 us -> 0 us
  blocking collectives: 54.1 us -> 0 us
  Pallas kernels: 42.1 us -> 87.4 us
  matrix products: 19.3 us -> 0 us
  local copies, waits for them, and re-layouts: 19.8 us -> 2.38 us
  between operations: 13.5 us -> 0.11 us
  starting transfers between devices: 5.25 us -> 0 us
    reduce_scatter x1 -> x0, waiting for transfers between devices: 303 us -> none  [per_device(): lax.psum_scatter(by_tile, ('tx', 'ty'), scatter_dimension=0, tiled=True)[0]]
    all_gather x1 -> x0, blocking collectives: 54.1 us -> none  [per_device(): rows = lax.all_gather(mine, 'mem', axis=0, tiled=True)]
    pallas_call x1 -> x3, Pallas kernels: 33.1 us -> 78.5 us  [the longest x1 40.7 us: coarse(): pl.pallas_call(coarse_kernel, out_shape=(jax.ShapeDtypeStruct((80, LINK_L...]
    dot_general x17 -> x0, matrix products: 19.3 us -> none  [the longest x5 6.17 us: coarse_weights(): jnp.einsum('cij,cjk->cik', lower, upper, precision=exact)]
    all_gather x2 -> x0, waiting for transfers between devices: 18.5 us -> none  [the longest x1 18.5 us: per_device(): all_volume = lax.all_gather(volume[0], 'mem', axis=0, tiled=True)]
    reshape x5 -> x0, local copies, waits for them, and re-layouts: 8.7 us -> none  [the longest x1 7.61 us: per_device(): partial[:, :440].reshape(16, 440, 4, 32).transpose(0, 2, 1, 3)]
    ppermute x4 -> x0, waiting for transfers between devices: 6.48 us -> none  [the longest x2 6.48 us: padded_2(): lax.ppermute(lax.slice_in_dim(block, 0, width, axis=dim), axis, backward)]
    ppermute x4 -> x0, starting transfers between devices: 5.17 us -> none  [the longest x2 2.58 us: padded_2(): lax.ppermute(lax.slice_in_dim(block, 0, width, axis=dim), axis, backward)]
  transfers between devices with their start and end apart: 7 -> 0, of which waited for: 4 -> 0; matrix products, arithmetic and copies ran while one was open for 5% -> 0% of each run, Pallas kernels for 0% -> 0%
where the time goes in v2:
time: 90.1 us; the launch traced here: 89.9 us
  Pallas kernels  87.4 us (97%)
  local copies, waits for them, and re-layouts  2.38 us (3%)
    pallas_call x1, Pallas kernels, coarse(): pl.pallas_call(coarse_kernel, out_shape=(jax.ShapeDtypeStruct((80, LINK_L...  40.7 us
    pallas_call x1, Pallas kernels, gram(): pl.pallas_call(gram_kernel, out_shape=(jax.ShapeDtypeStruct((4, 4, PART_A...  33.7 us
    pallas_call x1, Pallas kernels, apply(): pl.pallas_call(apply_kernel, out_shape=jax.ShapeDtypeStruct((own, levels,...  8.92 us
    pallas_call x1, Pallas kernels, swap(): pl.pallas_call(swap_kernel, out_shape=jax.ShapeDtypeStruct(volume.shape,...  4.1 us
    unnamed x16, local copies, waits for them, and re-layouts  2.38 us

profile of v2, /device:TPU:1, one launch (start us, length us, event | category | flops | bytes accessed | tf_op | source)
XLA Modules:
  0.0 89.9 jit_solution(4133268067982159267)
XLA Ops:
  0.0 0.0 copy-start.7
  0.0 0.0 copy-start.2
  0.0 0.0 copy-start.3
  0.0 0.0 copy-start
  0.0 4.1 %swap.1.other_ref = bf16[20,192,128]{2,1,0:T(8,128)(2,1)} custom-call(bf16[20,192,128]{2,1,0:T(8,128)(2,1)} %bitcast.3), custom_call_target="tpu_custom_call" | custom-call | tf_op jit(solution)/shard_map/swap/pallas_call | solution.py:477
  4.1 0.0 copy-start.5
  4.1 0.0 copy-start.6
  4.2 33.7 %gram.1 = (bf16[4,4,320,128]{3,2,1,0:T(8,128)(2,1)}, bf16[4,4,128,128]{3,2,1,0:T(8,128)(2,1)}) custom-call(s32[1,64]{1,0:T(1,128)} %count_ref.1, bf16[20,192,128]{2,1,0:T(8,128)(2,1)} %bitcast.4, bf16[20,192,128]{2,1,0:T(8,128)(2,1)} %swap.1.other_ref, bf16[192,128,128]{2,1,0:T(8,128)(2,1)} %bitcast.2, bf16[1,24576]{1,0:T(2,128)(2,1)} %value_ref.1, ...), custom_call_target="tpu_custom_call" | custom-call | tf_op jit(solution)/shard_map/gram/pallas_call | solution.py:166
  37.8 0.0 copy-done.7
  37.8 0.0 copy-done.2
  37.9 0.0 copy-done.3
  37.9 0.0 copy-done
  37.9 0.0 copy-start.1
  37.9 1.3 %copy-done.1 = bf16[4,4,320,128]{3,2,1,0:T(8,128)(2,1)S(1)} copy-done((bf16[4,4,320,128]{3,2,1,0:T(8,128)(2,1)S(1)}, bf16[4,4,320,128]{3,2,1,0:T(8,128)(2,1)}, u32[]{:S(2)}) %copy-start.1) | copy-done | bytes 1310744
  39.2 0.0 copy-start.4
  39.2 1.0 %copy-done.4 = bf16[4,4,128,128]{3,2,1,0:T(8,128)(2,1)S(1)} copy-done((bf16[4,4,128,128]{3,2,1,0:T(8,128)(2,1)S(1)}, bf16[4,4,128,128]{3,2,1,0:T(8,128)(2,1)}, u32[]{:S(2)}) %copy-start.4) | copy-done | bytes 524312
  40.2 40.7 %coarse.1 = (bf16[80,1280]{1,0:T(8,128)(2,1)S(1)}, bf16[20,8,16,128]{3,2,1,0:T(8,128)(2,1)S(1)}) custom-call(bf16[4,4,320,128]{3,2,1,0:T(8,128)(2,1)S(1)} %copy-done.1, bf16[4,4,128,128]{3,2,1,0:T(8,128)(2,1)S(1)} %copy-done.4, bf16[1648,256]{1,0:T(8,128)(2,1)S(1)} %copy-done.3, f32[1648,128]{1,0:T(8,128)S(1)} %copy-done.2, s32[8,256]{1,0:T(8,128)S(1)} %copy-done.7, ...), custom_call_target="tpu_custom_call" | custom-call | tf_op jit(solution)/shard_map/coarse/pallas_call | solution.py:642
  81.0 0.0 copy-done.5
  81.0 0.0 copy-done.6
  81.0 8.9 %apply.1 = bf16[20,8,16,128]{3,2,1,0:T(8,128)(2,1)} custom-call(bf16[80,1280]{1,0:T(8,128)(2,1)S(1)} %get-tuple-element.11.points_ref, f32[3,80,16]{2,1,0:T(8,128)S(1)} %copy-done.6, f32[3,80,128]{2,1,0:T(8,128)S(1)} %copy-done.5, bf16[20,8,16,128]{3,2,1,0:T(8,128)(2,1)S(1)} %copy-done, bf16[20,8,16,128]{3,2,1,0:T(8,128)(2,1)S(1)} %get-tuple-element.12.other_ref), custom_call_target="tpu_custom_call" | custom-call | tf_op jit(solution)/shard_map/apply/pallas_call | solution.py:260
Async XLA Ops:
  0.0 37.8 %copy-start.7 = (s32[8,256]{1,0:T(8,128)S(1)}, s32[8,256]{1,0:T(8,128)}, u32[]{:S(2)}) copy-start(s32[8,256]{1,0:T(8,128)} %constant.12.clone.lane_ref) | copy-start | bytes 24580
  0.0 37.8 %copy-start.2 = (f32[1648,128]{1,0:T(8,128)S(1)}, f32[1648,128]{1,0:T(8,128)}, u32[]{:S(2)}) copy-start(f32[1648,128]{1,0:T(8,128)} %constant.11.clone.quarter_ref) | copy-start | bytes 2531332
  0.0 37.8 %copy-start.3 = (bf16[1648,256]{1,0:T(8,128)(2,1)S(1)}, bf16[1648,256]{1,0:T(8,128)(2,1)}, u32[]{:S(2)}) copy-start(bf16[1648,256]{1,0:T(8,128)(2,1)} %constant.10.clone.pick_ref) | copy-start | bytes 2531332
  0.0 37.9 %copy-start = (bf16[20,8,16,128]{3,2,1,0:T(8,128)(2,1)S(1)}, bf16[20,8,16,128]{3,2,1,0:T(8,128)(2,1)}, u32[]{:S(2)}) copy-start(bf16[20,8,16,128]{3,2,1,0:T(8,128)(2,1)} %state_ref.3) | copy-start | bytes 1966084
  4.1 76.9 %copy-start.5 = (f32[3,80,128]{2,1,0:T(8,128)S(1)}, f32[3,80,128]{2,1,0:T(8,128)}, u32[]{:S(2)}) copy-start(f32[3,80,128]{2,1,0:T(8,128)} %constant.14.clone.tent_y_ref) | copy-start | bytes 368644
  4.1 76.9 %copy-start.6 = (f32[3,80,16]{2,1,0:T(8,128)S(1)}, f32[3,80,16]{2,1,0:T(8,128)}, u32[]{:S(2)}) copy-start(f32[3,80,16]{2,1,0:T(8,128)} %constant.13.clone.tent_x_ref) | copy-start | bytes 46084
  37.9 1.3 %copy-start.1 = (bf16[4,4,320,128]{3,2,1,0:T(8,128)(2,1)S(1)}, bf16[4,4,320,128]{3,2,1,0:T(8,128)(2,1)}, u32[]{:S(2)}) copy-start(bf16[4,4,320,128]{3,2,1,0:T(8,128)(2,1)} %get-tuple-element.9.ab_ref) | copy-start | bytes 3932164
  39.2 1.0 %copy-start.4 = (bf16[4,4,128,128]{3,2,1,0:T(8,128)(2,1)S(1)}, bf16[4,4,128,128]{3,2,1,0:T(8,128)(2,1)}, u32[]{:S(2)}) copy-start(bf16[4,4,128,128]{3,2,1,0:T(8,128)(2,1)} %get-tuple-element.10.c_ref) | copy-start | bytes 1572868

commit v3 on v1

v3 whole, which is shorter than its diff:
```python
import numpy as np
import jax
import jax.numpy as jnp
from jax import lax
from jax.experimental import pallas as pl
from jax.experimental.pallas import tpu as pltpu
from jax.sharding import PartitionSpec as P

B = 8
LOC = 16
NS = 5
STEP = 512
SUB = 128
CHUNKS = 12


MESH = pl.DeviceIdType.MESH
PART_A, PART_B, PART_C = 160, 160, 128
GROUPS = 3
WIDE = 256
LINK_LANES = 1280


def place_of(row):
    if row < PART_A:
        return row % (PART_A // 8), row // (PART_A // 8)
    row -= PART_A
    if row < PART_B:
        return PART_A // 8 + row % (PART_B // 8), row // (PART_B // 8)
    row -= PART_B
    return (PART_A + PART_B) // 8 + row % (PART_C // 8), row // (PART_C // 8)


def pick_tables():
    rows = np.zeros((1648, 128), np.float32)
    eighths = np.zeros((1648, 128), np.float32)

    def put(target, core, local):
        row, eighth = place_of(local)
        rows[target] = 0
        eighths[target] = 0
        rows[target, core * 56 + row] = 1
        eighths[target, eighth * 16:eighth * 16 + 16] = 1

    for core, products in enumerate(core_products()):
        for index, entry in enumerate([entry for both in products for entry in both]):
            if entry is None:
                continue
            low, high, turn = entry
            for s in range(8):
                if high < 0:
                    put(1600 + 8 * low + s, core, index * 8 + s)
                    continue
                k, j = 8 * low + s, 8 * high + (s - turn) % 8
                put(j * 40 + k, core, index * 8 + s)
                put(k * 40 + j, core, index * 8 + s)
    return rows.astype(jnp.bfloat16), eighths.astype(jnp.bfloat16)


def lane_table():
    lanes = np.arange(WIDE)
    table = np.full((8, WIDE), -1, np.int32)
    table[0] = np.where(lanes < 240, lanes // 40, 7)
    table[1] = np.where(lanes < 240, lanes % 40, -1)
    return table


def block_swap(arrays):
    lane = lax.broadcasted_iota(jnp.int32, arrays[0].shape, 1)
    count = len(arrays)
    step = count // 2
    while step:
        width = step * (128 // count)
        mask = (lane & width) == 0
        turned = list(arrays)
        for low in range(count):
            if low & step:
                continue
            first, second = arrays[low], arrays[low + step]
            turned[low] = jnp.where(mask, first, pltpu.roll(second, width, 1))
            turned[low + step] = jnp.where(mask, pltpu.roll(first, 128 - width, 1), second)
        arrays = turned
        step //= 2
    return arrays


def split(value):
    high = value.astype(jnp.bfloat16)
    return high, (value - high.astype(jnp.float32)).astype(jnp.bfloat16)


def bdot(left, right):
    return jnp.dot(left, right, preferred_element_type=jnp.float32)


def coarse_points(summed, pick_ref, eighth_ref, lane_ref, picked, spread_rows, rows):
    lane_i, lane_j = lane_ref[0:1], lane_ref[1:2]
    high, low = split(summed)
    both = jnp.concatenate([high, low], axis=1)
    both = jnp.concatenate([both, jnp.zeros((16, WIDE), jnp.bfloat16)], axis=0)
    eighths = eighth_ref[...].astype(jnp.float32)
    found = bdot(pick_ref[...], both)
    picked[...] = jnp.concatenate(
        [found[:, :128] * eighths, found[:, 128:] * eighths], axis=1
    ).astype(jnp.bfloat16)
    row_c = lax.broadcasted_iota(jnp.int32, (WIDE, WIDE), 0) & 15
    eye = (lax.broadcasted_iota(jnp.int32, (40, WIDE), 0) == lane_j).astype(jnp.float32)
    real = lane_j >= 0
    same = (
        (jnp.concatenate(
            [jnp.full((40, WIDE), i, jnp.int32) for i in range(6)] + [jnp.full((16, WIDE), 9, jnp.int32)], axis=0
        ) == lane_i)
        .astype(jnp.float32)
        .astype(jnp.bfloat16)
    )

    def blocks(value):
        parts = [jnp.where(lane_i == i, value, 0.0) for i in range(6)] + [jnp.zeros((16, WIDE), jnp.float32)]
        return split(jnp.concatenate(parts, axis=0))

    def times(values, right):
        right_high, right_low = right
        highs, lows = zip(*[split(value) for value in values])
        count = len(values) * 40
        stack = jnp.concatenate([part.astype(jnp.float32) for part in highs + lows], axis=0).astype(jnp.bfloat16)
        main = bdot(stack, right_high)
        rest = bdot(stack[:count], right_low)
        return [
            main[40 * i:40 * i + 40] + (main[count + 40 * i:count + 40 * i + 40] + rest[40 * i:40 * i + 40])
            for i in range(len(values))
        ]

    uppers, lowers, scales, informs = [], [], [], []
    for group in range(GROUPS):
        expand = (row_c == lane_i + 6 * group).astype(jnp.float32) * real.astype(jnp.float32)
        spread_rows[...] = bdot(picked[...], expand.astype(jnp.bfloat16))
        gram = jnp.zeros((40, WIDE), jnp.float32)
        for j in range(40):
            gram = jnp.where(lane_j == j, spread_rows[40 * j:40 * j + 40], gram)
        informs.append(spread_rows[1600:1640])
        amat = eye + gram * (1.0 / 39)
        square = jnp.sum(amat * amat, axis=0, keepdims=True)
        first = square.astype(jnp.bfloat16).astype(jnp.float32)
        second = (square - first).astype(jnp.bfloat16).astype(jnp.float32)
        third = square - first - second
        parts = jnp.concatenate(
            [jnp.broadcast_to(part, (8, WIDE)) for part in (first, second, third, jnp.zeros_like(third))], axis=0
        )
        norm = bdot(parts.astype(jnp.bfloat16), same)
        norm = norm[0:1] + norm[8:9] + norm[16:17]
        scale = jnp.sqrt(jnp.where(real, norm, 1.0))
        scales.append(scale)
        uppers.append(amat / scale)
    for group in range(GROUPS):
        middle = 1.5 * eye - 0.5 * uppers[group]
        lowers.append(middle)
        uppers[group] = times([uppers[group]], blocks(middle))[0]
    for sweep in range(1, NS):
        middles = []
        for group in range(GROUPS):
            product = times([lowers[group]], blocks(uppers[group]))[0]
            middles.append(blocks(1.5 * eye - 0.5 * product))
        for group in range(GROUPS):
            if sweep < NS - 1:
                uppers[group], lowers[group] = times([uppers[group], lowers[group]], middles[group])
            else:
                lowers[group] = times([lowers[group]], middles[group])[0]
    target = lax.broadcasted_iota(jnp.int32, (WIDE, 768), 1)
    source = lax.broadcasted_iota(jnp.int32, (WIDE, 768), 0)
    own = target & 31
    chooses = []
    for core in range(2):
        wanted = (target >> 7) * 40 + core * 20 + own
        chooses.append(((source == wanted) & (own < 20)).astype(jnp.float32).astype(jnp.bfloat16))
    for group in range(GROUPS):
        inv_half = lowers[group] / jnp.sqrt(scales[group])
        step_one = jnp.sum(inv_half * informs[group], axis=0, keepdims=True)
        product = inv_half * step_one
        high, low = split(product)
        stack = jnp.concatenate([high.astype(jnp.float32), low.astype(jnp.float32)], axis=0).astype(jnp.bfloat16)
        moved = bdot(stack, same)
        shift = (moved[:40] + moved[40:]) * (1.0 / 39)
        shift = shift - jnp.sum(shift, axis=0, keepdims=True) * (1.0 / 40)
        spread = inv_half - jnp.sum(inv_half, axis=0, keepdims=True) * (1.0 / 40)
        trans = (1.0 / 40 + shift + spread).astype(jnp.bfloat16)
        for core in range(2):
            chosen = bdot(trans, chooses[core])
            for i in range(6):
                point = group * 6 + i
                if point < 16:
                    rows[core, point * 40:point * 40 + 40, :] = chosen[:, i * 128:i * 128 + 128]


def gather_members(rows, lane):
    quarter = lane >> 5
    pieces = []
    for q in range(10):
        piece = rows[pl.ds(4 * q, 16, stride=40), :]
        for p in range(1, 4):
            piece = jnp.where(quarter == p, rows[pl.ds(4 * q + p, 16, stride=40), :], piece)
        pieces.append(piece)
    return jnp.concatenate(pieces, axis=1)


UNROLL = 4


def core_products():
    first, second = [], []
    for high in (4, 3, 2, 1):
        for low in range(high):
            for turn in range(0, 8, 2):
                both = ((low, high, turn), (low, high, turn + 1))
                (first if high > 2 else second).append(both)
    for low in range(5):
        second.append(((low, low, 0), (low, low, 1)))
        second.append(((low, low, 2), (low, low, 3)))
    second.append(((0, 0, 4), (1, 1, 4)))
    second.append(((2, 2, 4), (3, 3, 4)))
    second.append(((0, -1, 0), (1, -1, 0)))
    second.append(((2, -1, 0), (3, -1, 0)))
    second.append(((4, 4, 4), (4, -1, 0)))
    second.append((None, None))
    return first, second


def gram_kernel(
    count_ref, volume_hbm, other_hbm, matrix_hbm, value_ref, error_ref, cell_ref, ab_ref, c_ref,
    volume, matrix, wide, anomalies, surprises, weights, lhs0, lhs1, rhs0, rhs1, total, offsets, sems,
):
    mem = lax.axis_index("mem")
    chunks = sems.shape[0]
    radar_blocks = matrix.shape[0]
    held = volume_hbm.shape[0]
    tiles = count_ref.shape[1]
    chunk = radar_blocks // chunks
    steps = radar_blocks * SUB // STEP
    per_step = STEP // SUB

    def fetch(index):
        part = pl.ds(index * chunk, chunk)
        return (
            pltpu.make_async_copy(volume_hbm.at[:, part], volume.at[pl.ds(mem * held, held), part], sems.at[index, 0]),
            pltpu.make_async_copy(
                other_hbm.at[:, part], volume.at[pl.ds((1 - mem) * held, held), part], sems.at[index, 1]
            ),
            pltpu.make_async_copy(matrix_hbm.at[part], matrix.at[part], sems.at[index, 2]),
        )

    for index in range(chunks):
        for copy in fetch(index):
            copy.start()

    offsets[0] = 0
    running = jnp.int32(0)
    for tile in range(tiles):
        running = running + count_ref[0, tile]
        offsets[tile + 1] = running
    for extra in range(12):
        offsets[tiles + 1 + extra] = running
    total[...] = jnp.zeros_like(total)
    centre_y = lax.broadcasted_iota(jnp.int32, (16, STEP), 0).astype(jnp.float32) * B + (B - 1) / 2

    def project(index, carry):
        for copy in fetch(index):
            copy.wait()
        part = pl.ds(pl.multiple_of(index * chunk, chunk), chunk)
        for member in range(2 * held):
            wide[member * chunk:member * chunk + chunk, :] = volume[member, part].astype(jnp.float32)
        for inner in range(chunk // per_step):
            step = index * (chunk // per_step) + inner
            here = pl.ds(pl.multiple_of(step * STEP, STEP), STEP)
            cells = cell_ref[:, here]
            pos_x = (cells >> 7).astype(jnp.float32)
            pos_y = (cells & 127).astype(jnp.float32)
            inverse = (1.0 / error_ref[:, here]).astype(jnp.bfloat16).astype(jnp.float32)
            near_y = jnp.exp((pos_y - centre_y) ** 2 * (-0.5 / LOC**2)) * inverse
            for i in range(2):
                near_x = jnp.exp((pos_x - (i * B + (B - 1) / 2)) ** 2 * (-0.5 / LOC**2))
                weights[step, i * 16:i * 16 + 16, :] = (near_x * near_y).astype(jnp.bfloat16)
            values = value_ref[:, here].astype(jnp.float32)
            for sub in range(per_step):
                local = inner * per_step + sub
                block = index * chunk + local
                gates = wide[pl.ds(local, 2 * held, stride=chunk), :].astype(jnp.bfloat16)
                obs = jnp.dot(gates, matrix[block], preferred_element_type=jnp.float32)
                obs = obs.astype(jnp.bfloat16).astype(jnp.float32)
                mean = jnp.sum(obs, axis=0, keepdims=True) * (1.0 / 40)
                anomalies[block] = obs - mean
                surprises[block] = jnp.broadcast_to(values[:, sub * SUB:(sub + 1) * SUB] - mean, (8, SUB))
        return carry

    lax.fori_loop(0, chunks, project, 0)

    lane = lax.broadcasted_iota(jnp.int32, (8, STEP), 1)

    def build(item, lhs, rhs, products):
        step, group = item
        step = jnp.minimum(step, steps - 1)
        for sub in range(per_step):
            block = step * per_step + sub
            lanes = slice(sub * SUB, (sub + 1) * SUB)
            part = [
                anomalies[block, 8 * i:8 * i + 8, :].astype(jnp.bfloat16).astype(jnp.float32) for i in range(5)
            ]
            made = {}

            def operand(kind, entry):
                low, high, turn = entry
                if kind == 0:
                    return part[low]
                if high < 0:
                    return surprises[block]
                if (high, turn) not in made:
                    made[high, turn] = part[high] if turn == 0 else pltpu.roll(part[high], turn, 0)
                return made[high, turn]

            packed = {}

            def pack(kind, both):
                key = tuple((kind, entry[0]) if kind == 0 else (kind, entry[1:]) for entry in both)
                if key not in packed:
                    packed[key] = jnp.concatenate([operand(kind, entry) for entry in both], axis=0).astype(jnp.bfloat16)
                return packed[key]

            for index, both in enumerate(products):
                if both[0] is None:
                    continue
                lhs[index * 16:index * 16 + 16, lanes] = pack(0, both) * pack(1, both)
        slot = lane + step * STEP
        reached = [jnp.where(slot >= offsets[group * 4 + i], 1.0, 0.0) for i in range(9)]
        weight = weights[step]
        for i in range(8):
            inside = reached[i] - reached[i + 1]
            inside = jnp.concatenate([inside, inside], axis=0).astype(jnp.bfloat16)
            for half in range(2):
                rhs[i * 32 + half * 16:i * 32 + half * 16 + 16, :] = weight[half * 16:half * 16 + 16] * inside

    def use(group, lhs, rhs):
        added = lax.dot_general(
            lhs[...], rhs[...], (((1,), (1,)), ((), ())), preferred_element_type=jnp.float32
        )
        total[group] += added[:, :128]
        total[group + 1] += added[:, 128:]

    def follow(item):
        step, group = item
        end = (step + 1) * STEP
        again = (group + 2 < tiles // 4) & (offsets[group * 4 + 8] < end)
        ahead = (offsets[group * 4 + 4] <= end).astype(jnp.int32) + (offsets[group * 4 + 8] <= end).astype(jnp.int32)
        next_step = jnp.where(again, step, step + 1)
        next_group = jnp.where(again, group + 2, group + ahead)
        return next_step, jnp.where(next_step >= steps, tiles // 4, next_group)

    for core, products in enumerate(core_products()):

        @pl.when(mem == core)
        def _():
            if products[-1][0] is None:
                lhs0[len(products) * 16 - 16:, :] = jnp.zeros((16, STEP), jnp.bfloat16)
                lhs1[len(products) * 16 - 16:, :] = jnp.zeros((16, STEP), jnp.bfloat16)
            start = (jnp.int32(0), jnp.int32(0))
            build(start, lhs0, rhs0, products)

            def body(item):
                for turn in range(UNROLL):
                    lhs, rhs = (lhs0, rhs0) if turn % 2 == 0 else (lhs1, rhs1)
                    other_lhs, other_rhs = (lhs1, rhs1) if turn % 2 == 0 else (lhs0, rhs0)
                    following = follow(item)
                    use(item[1], lhs, rhs)
                    build(following, other_lhs, other_rhs, products)
                    item = following
                return item

            lax.while_loop(lambda item: item[0] < steps, body, start)

    for x in range(4):
        for y in range(4):
            ab_ref[x, y] = total[x * 4 + y, :PART_A + PART_B].astype(jnp.bfloat16)
        for z, value in enumerate(block_swap([total[x * 4 + y, PART_A + PART_B:] for y in range(4)])):
            c_ref[z, x] = value.astype(jnp.bfloat16)


def gram(counts, volume, other, matrix, values, errors, cells):
    blocks = matrix.shape[0]
    tiles = counts.shape[1]
    members = 2 * volume.shape[0]
    rows = PART_A + PART_B + PART_C
    steps = blocks * SUB // STEP
    vmem = pl.BlockSpec(memory_space=pltpu.VMEM)
    hbm = pl.BlockSpec(memory_space=pl.ANY)
    return pl.pallas_call(
        gram_kernel,
        out_shape=(
            jax.ShapeDtypeStruct((4, 4, PART_A + PART_B, 128), jnp.bfloat16),
            jax.ShapeDtypeStruct((4, 4, PART_C, 128), jnp.bfloat16),
        ),
        in_specs=[pl.BlockSpec(memory_space=pltpu.SMEM), hbm, hbm, hbm, vmem, vmem, vmem],
        out_specs=(vmem, vmem),
        scratch_shapes=[
            pltpu.VMEM((members, blocks, 128), jnp.bfloat16),
            pltpu.VMEM((blocks, 128, 128), jnp.bfloat16),
            pltpu.VMEM((members * (blocks // CHUNKS), 128), jnp.float32),
            pltpu.VMEM((blocks, members, 128), jnp.float32),
            pltpu.VMEM((blocks, 8, 128), jnp.float32),
            pltpu.VMEM((steps, 32, STEP), jnp.bfloat16),
            pltpu.VMEM((rows, STEP), jnp.bfloat16),
            pltpu.VMEM((rows, STEP), jnp.bfloat16),
            pltpu.VMEM((256, STEP), jnp.bfloat16),
            pltpu.VMEM((256, STEP), jnp.bfloat16),
            pltpu.VMEM((tiles // 4 + 2, rows, 128), jnp.float32),
            pltpu.SMEM((tiles + 13,), jnp.int32),
            pltpu.SemaphoreType.DMA((CHUNKS, 3)),
        ],
        compiler_params=pltpu.CompilerParams(vmem_limit_bytes=56 * 1024 * 1024),
        name="gram",
    )(counts, volume, other, matrix, values, errors, cells)


def apply_kernel(points_ref, tent_x_ref, tent_y_ref, state_ref, other_ref, out_ref, fine, flat, result):
    levels, width_x, width_y = state_ref.shape[1:]
    own = out_ref.shape[0]
    members = 2 * own
    mem, tx, ty = lax.axis_index("mem"), lax.axis_index("tx"), lax.axis_index("ty")
    kind_x = jnp.where(tx == 0, 0, jnp.where(tx == lax.axis_size("tx") - 1, 2, 1))
    kind_y = jnp.where(ty == 0, 0, jnp.where(ty == lax.axis_size("ty") - 1, 2, 1))
    tent_x, tent_y = tent_x_ref[kind_x], tent_y_ref[kind_y]
    points = points_ref[...].astype(jnp.float32)
    points = jnp.concatenate([points, jnp.zeros((48, points.shape[1]), jnp.float32)], axis=0).T
    points = points[:, :80].astype(jnp.bfloat16)

    def widen(member, carry):
        for source, first in ((state_ref, mem * own), (other_ref, (1 - mem) * own)):
            start = pl.multiple_of((first + member) * levels * width_x, 8)
            flat[pl.ds(start, levels * width_x), :] = (
                source[member].astype(jnp.float32).reshape(levels * width_x, width_y)
            )
        return carry

    lax.fori_loop(0, own, widen, 0)
    for x in range(0, width_x, 2):
        tent = jnp.concatenate(
            [tent_x[:, x + i:x + i + 1] * tent_y for i in range(2)], axis=1
        ).astype(jnp.bfloat16)
        made = jnp.dot(points, tent, preferred_element_type=jnp.float32)
        made = made.astype(jnp.bfloat16).astype(jnp.float32)
        fine[x] = made[:, :128]
        fine[x + 1] = made[:, 128:]

    def column(x, carry):
        def add(k4, sums):
            sums = list(sums)
            for i in range(4):
                k = k4 * 4 + i
                field = flat[pl.ds(k * (levels * width_x) + x, levels, stride=width_x), :]
                for j in range(own):
                    row = fine[x, pl.ds(k * 32 + j, 8, stride=0), :]
                    sums[j] = sums[j] + row * field
            return tuple(sums)

        zero = jnp.zeros((levels, width_y), jnp.float32)
        sums = lax.fori_loop(0, members // 4, add, (zero,) * own)
        for j in range(own):
            result[pl.ds(j * (levels * width_x) + x, levels, stride=width_x), :] = sums[j]
        return carry

    lax.fori_loop(0, width_x, column, 0)

    def narrow(j, carry):
        start = pl.multiple_of(j * levels * width_x, 8)
        out_ref[j] = (
            result[pl.ds(start, levels * width_x), :]
            .reshape(levels, width_x, width_y)
            .astype(jnp.bfloat16)
        )
        return carry

    lax.fori_loop(0, own, narrow, 0)


def apply(points, tent_x, tent_y, state, other):
    own, levels, width_x, width_y = state.shape
    members = 2 * own
    return pl.pallas_call(
        apply_kernel,
        out_shape=jax.ShapeDtypeStruct((own, levels, width_x, width_y), jnp.bfloat16),
        in_specs=[pl.BlockSpec(memory_space=pltpu.VMEM)] * 5,
        out_specs=pl.BlockSpec(memory_space=pltpu.VMEM),
        scratch_shapes=[
            pltpu.VMEM((width_x, points.shape[1], width_y), jnp.float32),
            pltpu.VMEM((members * levels * width_x, width_y), jnp.float32),
            pltpu.VMEM((own * levels * width_x, width_y), jnp.float32),
        ],
        compiler_params=pltpu.CompilerParams(vmem_limit_bytes=48 * 1024 * 1024),
        name="apply",
    )(points, tent_x, tent_y, state, other)


def swap_kernel(volume_ref, other_ref, send, recv):
    mem = lax.axis_index("mem")
    mate = (lax.axis_index("tx"), lax.axis_index("ty"), 1 - mem)
    barrier = pltpu.get_barrier_semaphore()
    pl.semaphore_signal(barrier, inc=1, device_id=mate, device_id_type=MESH)
    pl.semaphore_wait(barrier, 1)
    count = send.shape[0]
    share = volume_ref.shape[0] // count
    copies = []
    for index in range(count):
        part = pl.ds(index * share, share)
        copies.append(
            pltpu.make_async_remote_copy(
                src_ref=volume_ref.at[part], dst_ref=other_ref.at[part], send_sem=send.at[index],
                recv_sem=recv.at[index], device_id=mate, device_id_type=MESH,
            )
        )
    for copy in copies:
        copy.start()
    for copy in copies:
        copy.wait()


def swap(volume):
    return pl.pallas_call(
        swap_kernel,
        out_shape=jax.ShapeDtypeStruct(volume.shape, volume.dtype),
        in_specs=[pl.BlockSpec(memory_space=pl.ANY)],
        out_specs=pl.BlockSpec(memory_space=pl.ANY),
        scratch_shapes=[pltpu.SemaphoreType.DMA((4,)), pltpu.SemaphoreType.DMA((4,))],
        compiler_params=pltpu.CompilerParams(collective_id=0, has_side_effects=True),
        name="swap",
    )(volume)


def coarse_kernel(
    ab_ref, c_ref, pick_ref, eighth_ref, lane_ref, state_ref, points_ref, other_ref,
    own_a, own_b, own_c, pass_a, pass_b, pass_c, via_a, via_b, via_c, got_a, got_b, got_c,
    next_a, next_b, next_c, got_a2, got_b2, got_c2, last_a, last_b, last_c, got_a3, got_b3, got_c3,
    folded, summed, pick, eighth, picked, spread_rows, rows, edges, columns, halo, corners,
    send, recv, local,
):
    x, ty, mem = lax.axis_index("tx"), lax.axis_index("ty"), lax.axis_index("mem")
    y, z = ty // 4, ty % 4
    spot = (x, y, z)

    def along(axis, turn, core=None):
        core = mem if core is None else core
        if axis == 0:
            return ((x + turn) % 4, ty, core)
        if axis == 1:
            return (x, ((y + turn) % 4) * 4 + z, core)
        return (x, y * 4 + (z + turn) % 4, core)

    mate = (x, ty, 1 - mem)
    ahead = 2 * mem - 1
    around = []
    for step in (1, 15):
        for core in range(2):
            around.append(((x, (ty + step) % 16, core), (((x + ahead) + 4) % 4, (ty + step) % 16, core)))
    peers = [along(axis, turn, core) for axis in range(3) for turn in range(1, 4) for core in (mem, 1 - mem)]
    peers += [mate] + [device for pair in around for device in pair]
    peers += [(((x - ahead) + 4) % 4, (ty + step) % 16, mem) for step in (1, 15)]
    barrier = pltpu.get_barrier_semaphore()
    for device in peers:
        pl.semaphore_signal(barrier, inc=1, device_id=device, device_id_type=MESH)

    parts = (
        (0, lambda place, first, size: ab_ref.at[place, :, pl.ds(first, size)], PART_A),
        (1, lambda place, first, size: ab_ref.at[:, place, pl.ds(PART_A + first, size)], PART_B),
        (2, lambda place, first, size: c_ref.at[place, :, pl.ds(first, size)], PART_C),
    )
    owns, passes, vias, gots = (own_a, own_b, own_c), (pass_a, pass_b, pass_c), (via_a, via_b, via_c), (got_a, got_b, got_c)
    fetched = []
    for index, (axis, piece, size) in enumerate(parts):
        half = size // 2
        up, down = (spot[axis] + 1) % 4, (spot[axis] + 3) % 4
        fetched.append(
            [
                pltpu.make_async_copy(piece(up, 0, half), passes[index].at[0], local.at[3 * index]),
                pltpu.make_async_copy(piece(down, half, half), passes[index].at[1], local.at[3 * index + 1]),
                pltpu.make_async_copy(piece(spot[axis], 0, size), owns[index], local.at[3 * index + 2]),
            ]
        )
        for copy in fetched[index]:
            copy.start()
    tables = [
        pltpu.make_async_copy(pick_ref, pick, local.at[9]),
        pltpu.make_async_copy(eighth_ref, eighth, local.at[10]),
    ]
    for copy in tables:
        copy.start()
    for index in (0, 5, 6, 11):
        corners[index * 16:index * 16 + 16, :] = jnp.zeros((16, 128), jnp.float32)
    corners[192:256, :] = jnp.zeros((64, 128), jnp.float32)
    for core in range(2):
        rows[core, 640:, :] = jnp.zeros((rows.shape[1] - 640, 128), jnp.float32)
    pl.semaphore_wait(barrier, len(peers))

    started = []

    def link(source, target, index, device, landing=None):
        copy = pltpu.make_async_remote_copy(
            src_ref=source, dst_ref=target, send_sem=send.at[index],
            recv_sem=recv.at[index if landing is None else landing], device_id=device, device_id_type=MESH,
        )
        copy.start()
        started.append(copy)
        return copy

    relays, plains, finals = [], [], []
    for index, (axis, piece, size) in enumerate(parts):
        half = size // 2
        opposite = (spot[axis] + 2) % 4
        relays.append(
            [
                link(piece(opposite, 0, half), vias[index].at[0], 6 * index, along(axis, 1)),
                link(piece(opposite, half, half), vias[index].at[1], 6 * index + 1, along(axis, 3)),
            ]
        )
    for index, (axis, piece, size) in enumerate(parts):
        half = size // 2
        up, down = (spot[axis] + 1) % 4, (spot[axis] + 3) % 4
        plains.append(
            [
                link(piece(up, half, half), gots[index].at[0, :, pl.ds(half, half)], 6 * index + 2, along(axis, 1)),
                link(piece(down, 0, half), gots[index].at[1, :, pl.ds(0, half)], 6 * index + 3, along(axis, 3)),
            ]
        )
    state_copy = link(state_ref, other_ref, 18, mate)
    for index, (axis, piece, size) in enumerate(parts):
        half = size // 2
        finals.append([])
        for way in range(2):
            fetched[index][way].wait()
            relays[index][way].wait_recv()
            for block in range(4):
                passes[index][way, block] = (
                    passes[index][way, block].astype(jnp.float32) + vias[index][way, block].astype(jnp.float32)
                ).astype(jnp.bfloat16)
            target = gots[index].at[way, :, pl.ds(way * half, half)]
            finals[index].append(
                link(passes[index].at[way], target, 6 * index + 4 + way, along(axis, 1 + 2 * way))
            )

    def arrive(index):
        fetched[index][2].wait()
        for copy in plains[index] + finals[index]:
            copy.wait_recv()

    def add_up(index, block):
        value = owns[index][block].astype(jnp.float32)
        for way in range(2):
            value = value + gots[index][way, block].astype(jnp.float32)
        return value

    def stage(first, axis, source, target):
        copies = []
        for turn in (2, 1, 3):
            place = (spot[axis] + turn) % 4
            copies.append(link(source.at[place], target.at[turn - 1], first + turn - 1, along(axis, turn)))
        return copies

    def wait_all(copies):
        for copy in copies:
            copy.wait_recv()

    def add_last(own, got):
        value = own.astype(jnp.float32)
        for turn in range(3):
            value = value + got[turn].astype(jnp.float32)
        return value

    arrive(0)
    for block in range(4):
        next_a[block] = add_up(0, block).astype(jnp.bfloat16)
    second_a = stage(19, 1, next_a, got_a2)
    arrive(1)
    for block, value in enumerate(block_swap([add_up(1, block) for block in range(4)])):
        next_b[block] = value.astype(jnp.bfloat16)
    second_b = stage(22, 2, next_b, got_b2)
    arrive(2)
    for block in range(4):
        next_c[block] = add_up(2, block).astype(jnp.bfloat16)
    second_c = stage(25, 0, next_c, got_c2)

    def fold(value, target):
        size = value.shape[0] // 8
        folded[0:value.shape[0], :] = value
        pieces = [folded[i * size:(i + 1) * size, :] for i in range(8)]
        for index, part in enumerate(block_swap(pieces)):
            target[index] = part

    def third(number, axis, source, target):
        first = 28 + 8 * number
        for turn in (2, 1, 3, 0):
            place = (spot[axis] + turn) % 4
            for other in range(2):
                if turn == 0 and other == 0:
                    continue
                core = 1 - mem if other else mem
                link(
                    source.at[place * 2 + core], target.at[mem * 4 + turn], first + 2 * turn + other,
                    along(axis, turn, core), first + 2 * turn + mem,
                )
        target[mem * 4] = source[spot[axis] * 2 + mem]

    def sum_third(number, source, target, row):
        first = 28 + 8 * number

        def landed(core, turn):
            pltpu.make_async_remote_copy(
                src_ref=source.at[0], dst_ref=target.at[core * 4 + turn], send_sem=send.at[first],
                recv_sem=recv.at[first + 2 * turn + core], device_id=mate, device_id_type=MESH,
            ).wait_recv()

        landed(1 - mem, 0)
        for turn in range(1, 4):
            for core in range(2):
                landed(core, turn)
        size = source.shape[1]
        for core in range(2):
            value = target[core * 4]
            for turn in range(1, 4):
                value = value + target[core * 4 + turn]
            summed[core * 56 + row:core * 56 + row + size, :] = value

    wait_all(second_a)
    fold(add_last(next_a[y], got_a2), last_a)
    third(0, 2, last_a, got_a3)
    wait_all(second_b)
    fold(add_last(next_b[z], got_b2), last_b)
    third(1, 0, last_b, got_b3)
    wait_all(second_c)
    fold(add_last(next_c[x], got_c2), last_c)
    third(2, 1, last_c, got_c3)
    sum_third(0, last_a, got_a3, 0)
    sum_third(1, last_b, got_b3, 20)
    sum_third(2, last_c, got_c3, 40)

    for copy in tables:
        copy.wait()
    coarse_points(summed[...], pick, eighth, lane_ref, picked, spread_rows, rows)

    quarter_of = lax.broadcasted_iota(jnp.int32, (16, 128), 1) >> 5
    for core in range(2):
        for side in range(2):
            point = 15 * (1 - side)
            value = rows[core, pl.ds(point * 40, 16, stride=4), :]
            for p in range(1, 4):
                value = jnp.where(quarter_of == p, rows[core, pl.ds(point * 40 + p, 16, stride=4), :], value)
            columns[core, side] = value
    outer = jnp.where(mem == 1, 0, 2)
    for index, (straight, slanted) in enumerate(around):
        side, core = index // 2, index % 2
        for device, turn in ((straight, 1), (slanted, outer)):
            slot = (side * 3 + turn) * 2 + mem
            link(
                columns.at[core, side], corners.at[pl.ds(slot * 16, 16)],
                52 + 2 * index + (1 if device is slanted else 0), device, 52 + slot,
            )
    lane = lax.broadcasted_iota(jnp.int32, (16, 128), 1)
    for core in range(2):
        edges[core] = gather_members(rows.at[core], lane).astype(jnp.bfloat16)
    link(edges.at[1 - mem], halo.at[mem], 60, mate, 64 + mem)
    for other in range(2):
        core = 1 - mem if other else mem
        link(edges.at[core], halo.at[3 - mem], 61 + other, ((x + ahead + 4) % 4, ty, core), 64 + 3 - mem)
    points_ref[pl.ds(pl.multiple_of(mem * 16, 16), 16), :] = edges[mem]

    def landed(source, target, index):
        pltpu.make_async_remote_copy(
            src_ref=source, dst_ref=target, send_sem=send.at[0], recv_sem=recv.at[index],
            device_id=mate, device_id_type=MESH,
        ).wait_recv()

    for slot in (1, 2, 3, 4, 7, 8, 9, 10):
        landed(columns.at[0, 0], corners.at[pl.ds(slot * 16, 16)], 52 + slot)
    for q in range(10):
        points_ref[64:80, q * 128:q * 128 + 128] = corners[pl.ds(q, 16, stride=16), :].astype(jnp.bfloat16)
    landed(edges.at[0], halo.at[1 - mem], 64 + 1 - mem)
    points_ref[pl.ds(pl.multiple_of((1 - mem) * 16, 16), 16), :] = halo[1 - mem]
    for slot in (2, 3):
        landed(edges.at[0], halo.at[slot], 64 + slot)
        points_ref[slot * 16:slot * 16 + 16, :] = halo[slot]
    state_copy.wait_recv()
    for copy in started:
        copy.wait_send()


def coarse(partial_ab, partial_c, state):
    pick, eighth = pick_tables()
    bf16, f32 = jnp.bfloat16, jnp.float32
    sizes = (PART_A, PART_B, PART_C)
    hbm, vmem = pl.BlockSpec(memory_space=pl.ANY), pl.BlockSpec(memory_space=pltpu.VMEM)
    return pl.pallas_call(
        coarse_kernel,
        out_shape=(
            jax.ShapeDtypeStruct((80, LINK_LANES), bf16),
            jax.ShapeDtypeStruct(state.shape, state.dtype),
        ),
        in_specs=[hbm, hbm, hbm, hbm, vmem, hbm],
        out_specs=(vmem, hbm),
        scratch_shapes=[pltpu.VMEM((4, size, 128), bf16) for size in sizes]
        + [pltpu.VMEM((2, 4, size // 2, 128), bf16) for size in sizes]
        + [pltpu.VMEM((2, 4, size // 2, 128), bf16) for size in sizes]
        + [pltpu.VMEM((2, 4, size, 128), bf16) for size in sizes]
        + [pltpu.VMEM((4, size, 128), bf16) for size in sizes]
        + [pltpu.VMEM((3, size, 128), bf16) for size in sizes]
        + [pltpu.VMEM((8, size // 8, 128), f32) for size in sizes]
        + [pltpu.VMEM((8, size // 8, 128), f32) for size in sizes]
        + [
            pltpu.VMEM((PART_A, 128), f32),
            pltpu.VMEM((112, 128), f32),
            pltpu.VMEM((1648, 128), bf16),
            pltpu.VMEM((1648, 128), bf16),
            pltpu.VMEM((1648, WIDE), bf16),
            pltpu.VMEM((1648, WIDE), f32),
            pltpu.VMEM((2, 672, 128), f32),
            pltpu.VMEM((2, 16, LINK_LANES), bf16),
            pltpu.VMEM((2, 2, 16, 128), f32),
            pltpu.VMEM((4, 16, LINK_LANES), bf16),
            pltpu.VMEM((256, 128), f32),
            pltpu.SemaphoreType.DMA((68,)),
            pltpu.SemaphoreType.DMA((68,)),
            pltpu.SemaphoreType.DMA((11,)),
        ],
        compiler_params=pltpu.CompilerParams(
            collective_id=1, has_side_effects=True, vmem_limit_bytes=48 * 1024 * 1024
        ),
        name="coarse",
    )(partial_ab, partial_c, jnp.asarray(pick), jnp.asarray(eighth), jnp.asarray(lane_table()), state)


def tent(length, nodes):
    position = np.arange(length, dtype=np.float32)[:, None]
    centre = (np.arange(nodes, dtype=np.float32)[None, :] - 1.0) * B + (B - 1) * 0.5
    return np.maximum(0.0, 1.0 - np.abs(position - centre) / B)


def tent_tables():
    place_x, place_y = np.full(80, -1), np.full(80, -1)
    for i in range(2):
        for j in range(16):
            place_x[i * 16 + j], place_y[i * 16 + j] = i + 1, j + 1
            place_x[32 + i * 16 + j], place_y[32 + i * 16 + j] = 3 * i, j + 1
    for side in range(2):
        for turn in range(3):
            for i in range(2):
                row = 64 + (side * 3 + turn) * 2 + i
                place_y[row] = 17 * side
                place_x[row] = {1: i + 1, 0: 0 if i == 1 else -1, 2: 3 if i == 0 else -1}[turn]
    tables = []
    for length, nodes, place in ((16, 4, place_x), (128, 18, place_y)):
        table = np.zeros((3, 80, length), np.float32)
        for kind in range(3):
            weights = tent(length, nodes)
            if kind == 0:
                weights[:, 1] += weights[:, 0]
                weights[:, 0] = 0
            if kind == 2:
                weights[:, -2] += weights[:, -1]
                weights[:, -1] = 0
            for row in range(80):
                if place[row] >= 0:
                    table[kind, row] = weights[:, place[row]]
        tables.append(table)
    return tables


def per_device(volume, super_matrix, observed, error_var, obs_cells, counts, state):
    other_volume = swap(volume[0])
    partial_ab, partial_c = gram(counts, volume[0], other_volume, super_matrix[0], observed, error_var, obs_cells)
    points, other_state = coarse(partial_ab, partial_c, state)
    tent_x, tent_y = tent_tables()
    return apply(points, jnp.asarray(tent_x), jnp.asarray(tent_y), state, other_state)


def solution(mesh):
    placed = (
        P(("tx", "ty"), "mem", None, None),
        P(("tx", "ty"), None, None, None),
        P(("tx", "ty"), None),
        P(("tx", "ty"), None),
        P(("tx", "ty"), None),
        P(("tx", "ty"), None),
        P("mem", None, "tx", "ty"),
    )
    return jax.shard_map(
        per_device,
        mesh=mesh,
        in_specs=placed,
        out_specs=P("mem", None, "tx", "ty"),
        check_vma=False,
    )
```

time: 490 us -> 71.7 us (0.15)
  waiting for transfers between devices: 329 us -> 0 us
  blocking collectives: 54.1 us -> 0 us
  Pallas kernels: 42.1 us -> 69 us
  matrix products: 19.3 us -> 0 us
  local copies, waits for them, and re-layouts: 19.8 us -> 2.38 us
  between operations: 13.5 us -> 0.11 us
  starting transfers between devices: 5.25 us -> 0 us
    reduce_scatter x1 -> x0, waiting for transfers between devices: 303 us -> none  [per_device(): lax.psum_scatter(by_tile, ('tx', 'ty'), scatter_dimension=0, tiled=True)[0]]
    all_gather x1 -> x0, blocking collectives: 54.1 us -> none  [per_device(): rows = lax.all_gather(mine, 'mem', axis=0, tiled=True)]
    pallas_call x1 -> x3, Pallas kernels: 33.1 us -> 60.1 us  [the longest x1 36.3 us: coarse(): pl.pallas_call(coarse_kernel, out_shape=(jax.ShapeDtypeStruct((80, LINK_L...]
    dot_general x17 -> x0, matrix products: 19.3 us -> none  [the longest x5 6.17 us: coarse_weights(): jnp.einsum('cij,cjk->cik', lower, upper, precision=exact)]
    all_gather x2 -> x0, waiting for transfers between devices: 18.5 us -> none  [the longest x1 18.5 us: per_device(): all_volume = lax.all_gather(volume[0], 'mem', axis=0, tiled=True)]
    reshape x5 -> x0, local copies, waits for them, and re-layouts: 8.7 us -> none  [the longest x1 7.61 us: per_device(): partial[:, :440].reshape(16, 440, 4, 32).transpose(0, 2, 1, 3)]
    ppermute x4 -> x0, waiting for transfers between devices: 6.48 us -> none  [the longest x2 6.48 us: padded_2(): lax.ppermute(lax.slice_in_dim(block, 0, width, axis=dim), axis, backward)]
    ppermute x4 -> x0, starting transfers between devices: 5.17 us -> none  [the longest x2 2.58 us: padded_2(): lax.ppermute(lax.slice_in_dim(block, 0, width, axis=dim), axis, backward)]
  transfers between devices with their start and end apart: 7 -> 0, of which waited for: 4 -> 0; matrix products, arithmetic and copies ran while one was open for 5% -> 0% of each run, Pallas kernels for 0% -> 0%
where the time goes in v3:
time: 71.7 us; the launch traced here: 71.5 us
  Pallas kernels  69 us (96%)
  local copies, waits for them, and re-layouts  2.38 us (3%)
    pallas_call x1, Pallas kernels, coarse(): pl.pallas_call(coarse_kernel, out_shape=(jax.ShapeDtypeStruct((80, LINK_L...  36.3 us
    pallas_call x1, Pallas kernels, gram(): pl.pallas_call(gram_kernel, out_shape=(jax.ShapeDtypeStruct((4, 4, PART_A...  19.6 us
    pallas_call x1, Pallas kernels, apply(): pl.pallas_call(apply_kernel, out_shape=jax.ShapeDtypeStruct((own, levels,...  8.92 us
    pallas_call x1, Pallas kernels, swap(): pl.pallas_call(swap_kernel, out_shape=jax.ShapeDtypeStruct(volume.shape,...  4.1 us
    unnamed x16, local copies, waits for them, and re-layouts  2.38 us

profile of v3, /device:TPU:1, one launch (start us, length us, event | category | flops | bytes accessed | tf_op | source)
XLA Modules:
  0.0 71.5 jit_solution(10617796383765567865)
XLA Ops:
  0.0 0.0 copy-start.7
  0.0 0.0 copy-start.3
  0.0 0.0 copy-start.4
  0.0 0.0 copy-start
  0.0 4.1 %swap.1.other_hbm = bf16[20,192,128]{2,1,0:T(8,128)(2,1)} custom-call(bf16[20,192,128]{2,1,0:T(8,128)(2,1)} %bitcast.3), custom_call_target="tpu_custom_call" | custom-call | tf_op jit(solution)/shard_map/swap/pallas_call | solution.py:523
  4.1 0.0 copy-start.5
  4.1 0.0 copy-start.6
  4.2 19.6 %gram.1 = (bf16[4,4,320,128]{3,2,1,0:T(8,128)(2,1)}, bf16[4,4,128,128]{3,2,1,0:T(8,128)(2,1)}) custom-call(s32[1,64]{1,0:T(1,128)} %count_ref.1, bf16[20,192,128]{2,1,0:T(8,128)(2,1)} %bitcast.4, bf16[20,192,128]{2,1,0:T(8,128)(2,1)} %swap.1.other_hbm, bf16[192,128,128]{2,1,0:T(8,128)(2,1)} %bitcast.2, bf16[1,24576]{1,0:T(2,128)(2,1)} %value_ref.1, ...), custom_call_target="tpu_custom_call" | custom-call | tf_op jit(solution)/shard_map/gram/pallas_call | solution.py:392
  23.8 0.0 copy-done.7
  23.8 0.0 copy-done.3
  23.8 0.0 copy-done.4
  23.8 0.0 copy-done
  23.8 0.0 copy-start.1
  23.9 1.3 %copy-done.1 = bf16[4,4,320,128]{3,2,1,0:T(8,128)(2,1)S(1)} copy-done((bf16[4,4,320,128]{3,2,1,0:T(8,128)(2,1)S(1)}, bf16[4,4,320,128]{3,2,1,0:T(8,128)(2,1)}, u32[]{:S(2)}) %copy-start.1) | copy-done | bytes 1310744
  25.2 0.0 copy-start.2
  25.2 1.0 %copy-done.2 = bf16[4,4,128,128]{3,2,1,0:T(8,128)(2,1)S(1)} copy-done((bf16[4,4,128,128]{3,2,1,0:T(8,128)(2,1)S(1)}, bf16[4,4,128,128]{3,2,1,0:T(8,128)(2,1)}, u32[]{:S(2)}) %copy-start.2) | copy-done | bytes 524312
  26.2 36.3 %coarse.1 = (bf16[80,1280]{1,0:T(8,128)(2,1)S(1)}, bf16[20,8,16,128]{3,2,1,0:T(8,128)(2,1)S(1)}) custom-call(bf16[4,4,320,128]{3,2,1,0:T(8,128)(2,1)S(1)} %copy-done.1, bf16[4,4,128,128]{3,2,1,0:T(8,128)(2,1)S(1)} %copy-done.2, bf16[1648,128]{1,0:T(8,128)(2,1)S(1)} %copy-done.4, bf16[1648,128]{1,0:T(8,128)(2,1)S(1)} %copy-done.3, s32[8,256]{1,0:T(8,128)S(1)} %copy-done.7, ...), custom_call_target="tpu_custom_call" | custom-call | tf_op jit(solution)/shard_map/coarse/pallas_call | solution.py:794
  62.6 0.0 copy-done.5
  62.6 0.0 copy-done.6
  62.6 8.9 %apply.1 = bf16[20,8,16,128]{3,2,1,0:T(8,128)(2,1)} custom-call(bf16[80,1280]{1,0:T(8,128)(2,1)S(1)} %get-tuple-element.11.points_ref, f32[3,80,16]{2,1,0:T(8,128)S(1)} %copy-done.6, f32[3,80,128]{2,1,0:T(8,128)S(1)} %copy-done.5, bf16[20,8,16,128]{3,2,1,0:T(8,128)(2,1)S(1)} %copy-done, bf16[20,8,16,128]{3,2,1,0:T(8,128)(2,1)S(1)} %get-tuple-element.12.other_ref), custom_call_target="tpu_custom_call" | custom-call | tf_op jit(solution)/shard_map/apply/pallas_call | solution.py:484
Async XLA Ops:
  0.0 23.8 %copy-start.7 = (s32[8,256]{1,0:T(8,128)S(1)}, s32[8,256]{1,0:T(8,128)}, u32[]{:S(2)}) copy-start(s32[8,256]{1,0:T(8,128)} %constant.12.clone.lane_ref) | copy-start | bytes 24580
  0.0 23.8 %copy-start.3 = (bf16[1648,128]{1,0:T(8,128)(2,1)S(1)}, bf16[1648,128]{1,0:T(8,128)(2,1)}, u32[]{:S(2)}) copy-start(bf16[1648,128]{1,0:T(8,128)(2,1)} %constant.11.clone.eighth_ref) | copy-start | bytes 1265668
  0.0 23.8 %copy-start.4 = (bf16[1648,128]{1,0:T(8,128)(2,1)S(1)}, bf16[1648,128]{1,0:T(8,128)(2,1)}, u32[]{:S(2)}) copy-start(bf16[1648,128]{1,0:T(8,128)(2,1)} %constant.10.clone.pick_ref) | copy-start | bytes 1265668
  0.0 23.8 %copy-start = (bf16[20,8,16,128]{3,2,1,0:T(8,128)(2,1)S(1)}, bf16[20,8,16,128]{3,2,1,0:T(8,128)(2,1)}, u32[]{:S(2)}) copy-start(bf16[20,8,16,128]{3,2,1,0:T(8,128)(2,1)} %state_ref.3) | copy-start | bytes 1966084
  4.1 58.4 %copy-start.5 = (f32[3,80,128]{2,1,0:T(8,128)S(1)}, f32[3,80,128]{2,1,0:T(8,128)}, u32[]{:S(2)}) copy-start(f32[3,80,128]{2,1,0:T(8,128)} %constant.14.clone.tent_y_ref) | copy-start | bytes 368644
  4.1 58.4 %copy-start.6 = (f32[3,80,16]{2,1,0:T(8,128)S(1)}, f32[3,80,16]{2,1,0:T(8,128)}, u32[]{:S(2)}) copy-start(f32[3,80,16]{2,1,0:T(8,128)} %constant.13.clone.tent_x_ref) | copy-start | bytes 46084
  23.8 1.3 %copy-start.1 = (bf16[4,4,320,128]{3,2,1,0:T(8,128)(2,1)S(1)}, bf16[4,4,320,128]{3,2,1,0:T(8,128)(2,1)}, u32[]{:S(2)}) copy-start(bf16[4,4,320,128]{3,2,1,0:T(8,128)(2,1)} %get-tuple-element.9.ab_ref) | copy-start | bytes 3932164
  25.2 1.0 %copy-start.2 = (bf16[4,4,128,128]{3,2,1,0:T(8,128)(2,1)S(1)}, bf16[4,4,128,128]{3,2,1,0:T(8,128)(2,1)}, u32[]{:S(2)}) copy-start(bf16[4,4,128,128]{3,2,1,0:T(8,128)(2,1)} %get-tuple-element.10.c_ref) | copy-start | bytes 1572868

commit v4 on v3

--- a/solution.py
+++ b/solution.py
@@ -9,16 +9,16 @@
 B = 8
 LOC = 16
 NS = 5
-STEP = 512
+STEP = 768
 SUB = 128
-CHUNKS = 12
+CHUNKS = 4
 
 
 MESH = pl.DeviceIdType.MESH
 PART_A, PART_B, PART_C = 160, 160, 128
 GROUPS = 3
 WIDE = 256
-LINK_LANES = 1280
+LINK_LANES = 896
 
 
 def place_of(row):
@@ -167,11 +167,14 @@
                 lowers[group] = times([lowers[group]], middles[group])[0]
     target = lax.broadcasted_iota(jnp.int32, (WIDE, 768), 1)
     source = lax.broadcasted_iota(jnp.int32, (WIDE, 768), 0)
-    own = target & 31
+    own = target & 127
+    point = (target >> 7) * 40
+    for copy in range(1, 6):
+        own = jnp.where((target & 127) >= 20 * copy, (target & 127) - 20 * copy, own)
     chooses = []
     for core in range(2):
-        wanted = (target >> 7) * 40 + core * 20 + own
-        chooses.append(((source == wanted) & (own < 20)).astype(jnp.float32).astype(jnp.bfloat16))
+        chosen = (source == point + core * 20 + own) & ((target & 127) < 120)
+        chooses.append(chosen.astype(jnp.float32).astype(jnp.bfloat16))
     for group in range(GROUPS):
         inv_half = lowers[group] / jnp.sqrt(scales[group])
         step_one = jnp.sum(inv_half * informs[group], axis=0, keepdims=True)
@@ -191,18 +194,23 @@
                     rows[core, point * 40:point * 40 + 40, :] = chosen[:, i * 128:i * 128 + 128]
 
 
-def gather_members(rows, lane):
-    quarter = lane >> 5
+def sixths(shape):
+    lane = lax.broadcasted_iota(jnp.int32, shape, 1)
+    return [lane >= 20 * p for p in range(6)]
+
+
+def gather_members(rows):
+    after = sixths((16, 128))
     pieces = []
-    for q in range(10):
-        piece = rows[pl.ds(4 * q, 16, stride=40), :]
-        for p in range(1, 4):
-            piece = jnp.where(quarter == p, rows[pl.ds(4 * q + p, 16, stride=40), :], piece)
+    for q in range(7):
+        piece = rows[pl.ds(6 * q, 16, stride=40), :]
+        for p in range(1, 6):
+            piece = jnp.where(after[p], rows[pl.ds(6 * q + p, 16, stride=40), :], piece)
         pieces.append(piece)
     return jnp.concatenate(pieces, axis=1)
 
 
-UNROLL = 4
+UNROLL = 2
 
 
 def core_products():
@@ -225,8 +233,8 @@
 
 
 def gram_kernel(
-    count_ref, volume_hbm, other_hbm, matrix_hbm, value_ref, error_ref, cell_ref, ab_ref, c_ref,
-    volume, matrix, wide, anomalies, surprises, weights, lhs0, lhs1, rhs0, rhs1, total, offsets, sems,
+    count_ref, volume_hbm, other_hbm, matrix_hbm, value_ref, error_ref, cell_ref, ab_hbm, c_hbm,
+    ab_ref, c_ref,    volume, matrix, wide, anomalies, surprises, weights, lhs0, lhs1, rhs0, rhs1, total, offsets, sems, out_sems,
 ):
     mem = lax.axis_index("mem")
     chunks = sems.shape[0]
@@ -374,11 +382,18 @@
 
             lax.while_loop(lambda item: item[0] < steps, body, start)
 
+    results = []
     for x in range(4):
         for y in range(4):
             ab_ref[x, y] = total[x * 4 + y, :PART_A + PART_B].astype(jnp.bfloat16)
         for z, value in enumerate(block_swap([total[x * 4 + y, PART_A + PART_B:] for y in range(4)])):
             c_ref[z, x] = value.astype(jnp.bfloat16)
+        results.append(pltpu.make_async_copy(ab_ref.at[x], ab_hbm.at[x], out_sems.at[2 * x]))
+        results.append(pltpu.make_async_copy(c_ref.at[:, x], c_hbm.at[:, x], out_sems.at[2 * x + 1]))
+        for copy in results[-2:]:
+            copy.start()
+    for copy in results:
+        copy.wait()
 
 
 def gram(counts, volume, other, matrix, values, errors, cells):
@@ -396,8 +411,10 @@
             jax.ShapeDtypeStruct((4, 4, PART_C, 128), jnp.bfloat16),
         ),
         in_specs=[pl.BlockSpec(memory_space=pltpu.SMEM), hbm, hbm, hbm, vmem, vmem, vmem],
-        out_specs=(vmem, vmem),
+        out_specs=(hbm, hbm),
         scratch_shapes=[
+            pltpu.VMEM((4, 4, PART_A + PART_B, 128), jnp.bfloat16),
+            pltpu.VMEM((4, 4, PART_C, 128), jnp.bfloat16),
             pltpu.VMEM((members, blocks, 128), jnp.bfloat16),
             pltpu.VMEM((blocks, 128, 128), jnp.bfloat16),
             pltpu.VMEM((members * (blocks // CHUNKS), 128), jnp.float32),
@@ -411,17 +428,22 @@
             pltpu.VMEM((tiles // 4 + 2, rows, 128), jnp.float32),
             pltpu.SMEM((tiles + 13,), jnp.int32),
             pltpu.SemaphoreType.DMA((CHUNKS, 3)),
+            pltpu.SemaphoreType.DMA((8,)),
         ],
-        compiler_params=pltpu.CompilerParams(vmem_limit_bytes=56 * 1024 * 1024),
+        compiler_params=pltpu.CompilerParams(vmem_limit_bytes=60 * 1024 * 1024),
         name="gram",
     )(counts, volume, other, matrix, values, errors, cells)
 
 
-def apply_kernel(points_ref, tent_x_ref, tent_y_ref, state_ref, other_ref, out_ref, fine, flat, result):
-    levels, width_x, width_y = state_ref.shape[1:]
+def apply_kernel(points_ref, tent_x_ref, tent_y_ref, state_hbm, other_hbm, out_ref, states, fine, flat, result, sems):
+    levels, width_x, width_y = state_hbm.shape[1:]
     own = out_ref.shape[0]
     members = 2 * own
     mem, tx, ty = lax.axis_index("mem"), lax.axis_index("tx"), lax.axis_index("ty")
+    copies = []
+    for index, source in enumerate((state_hbm, other_hbm)):
+        copies.append(pltpu.make_async_copy(source, states.at[index], sems.at[index]))
+        copies[index].start()
     kind_x = jnp.where(tx == 0, 0, jnp.where(tx == lax.axis_size("tx") - 1, 2, 1))
     kind_y = jnp.where(ty == 0, 0, jnp.where(ty == lax.axis_size("ty") - 1, 2, 1))
     tent_x, tent_y = tent_x_ref[kind_x], tent_y_ref[kind_y]
@@ -429,37 +451,44 @@
     points = jnp.concatenate([points, jnp.zeros((48, points.shape[1]), jnp.float32)], axis=0).T
     points = points[:, :80].astype(jnp.bfloat16)
 
-    def widen(member, carry):
-        for source, first in ((state_ref, mem * own), (other_ref, (1 - mem) * own)):
-            start = pl.multiple_of((first + member) * levels * width_x, 8)
-            flat[pl.ds(start, levels * width_x), :] = (
-                source[member].astype(jnp.float32).reshape(levels * width_x, width_y)
-            )
-        return carry
-
-    lax.fori_loop(0, own, widen, 0)
     for x in range(0, width_x, 2):
         tent = jnp.concatenate(
             [tent_x[:, x + i:x + i + 1] * tent_y for i in range(2)], axis=1
         ).astype(jnp.bfloat16)
         made = jnp.dot(points, tent, preferred_element_type=jnp.float32)
-        made = made.astype(jnp.bfloat16).astype(jnp.float32)
         fine[x] = made[:, :128]
         fine[x + 1] = made[:, 128:]
 
+    for copy in copies:
+        copy.wait()
+
+    def widen(member, carry):
+        for index, first in enumerate((mem * own, (1 - mem) * own)):
+            start = pl.multiple_of((first + member) * levels * width_x, 8)
+            flat[pl.ds(start, levels * width_x), :] = (
+                states[index, member].astype(jnp.float32).reshape(levels * width_x, width_y)
+            )
+        return carry
+
+    lax.fori_loop(0, own, widen, 0)
+
     def column(x, carry):
-        def add(k4, sums):
+        def add(step, sums):
             sums = list(sums)
-            for i in range(4):
-                k = k4 * 4 + i
+            for inner in range(20):
+                k = step * 20 + inner
                 field = flat[pl.ds(k * (levels * width_x) + x, levels, stride=width_x), :]
+                place = sum(
+                    jnp.where(step == turn, (it // 6) * 128 + (it % 6) * 20, 0)
+                    for turn, it in enumerate(range(inner, members, 20))
+                )
                 for j in range(own):
-                    row = fine[x, pl.ds(k * 32 + j, 8, stride=0), :]
+                    row = fine[x, pl.ds(place + j, 8, stride=0), :]
                     sums[j] = sums[j] + row * field
             return tuple(sums)
 
         zero = jnp.zeros((levels, width_y), jnp.float32)
-        sums = lax.fori_loop(0, members // 4, add, (zero,) * own)
+        sums = lax.fori_loop(0, members // 20, add, (zero,) * own)
         for j in range(own):
             result[pl.ds(j * (levels * width_x) + x, levels, stride=width_x), :] = sums[j]
         return carry
@@ -484,14 +513,16 @@
     return pl.pallas_call(
         apply_kernel,
         out_shape=jax.ShapeDtypeStruct((own, levels, width_x, width_y), jnp.bfloat16),
-        in_specs=[pl.BlockSpec(memory_space=pltpu.VMEM)] * 5,
+        in_specs=[pl.BlockSpec(memory_space=pltpu.VMEM)] * 3 + [pl.BlockSpec(memory_space=pl.ANY)] * 2,
         out_specs=pl.BlockSpec(memory_space=pltpu.VMEM),
         scratch_shapes=[
+            pltpu.VMEM((2,) + state.shape, state.dtype),
             pltpu.VMEM((width_x, points.shape[1], width_y), jnp.float32),
             pltpu.VMEM((members * levels * width_x, width_y), jnp.float32),
             pltpu.VMEM((own * levels * width_x, width_y), jnp.float32),
+            pltpu.SemaphoreType.DMA((2,)),
         ],
-        compiler_params=pltpu.CompilerParams(vmem_limit_bytes=48 * 1024 * 1024),
+        compiler_params=pltpu.CompilerParams(vmem_limit_bytes=60 * 1024 * 1024),
         name="apply",
     )(points, tent_x, tent_y, state, other)
 
@@ -526,14 +557,16 @@
         in_specs=[pl.BlockSpec(memory_space=pl.ANY)],
         out_specs=pl.BlockSpec(memory_space=pl.ANY),
         scratch_shapes=[pltpu.SemaphoreType.DMA((4,)), pltpu.SemaphoreType.DMA((4,))],
-        compiler_params=pltpu.CompilerParams(collective_id=0, has_side_effects=True),
+        compiler_params=pltpu.CompilerParams(
+            collective_id=0, has_side_effects=True, vmem_limit_bytes=60 * 1024 * 1024
+        ),
         name="swap",
     )(volume)
 
 
 def coarse_kernel(
     ab_ref, c_ref, pick_ref, eighth_ref, lane_ref, state_ref, points_ref, other_ref,
-    own_a, own_b, own_c, pass_a, pass_b, pass_c, via_a, via_b, via_c, got_a, got_b, got_c,
+    whole_ab, whole_c, pass_a, pass_b, pass_c, via_a, via_b, via_c, got_a, got_b, got_c,
     next_a, next_b, next_c, got_a2, got_b2, got_c2, last_a, last_b, last_c, got_a3, got_b3, got_c3,
     folded, summed, pick, eighth, picked, spread_rows, rows, edges, columns, halo, corners,
     send, recv, local,
@@ -564,27 +597,20 @@
         pl.semaphore_signal(barrier, inc=1, device_id=device, device_id_type=MESH)
 
     parts = (
-        (0, lambda place, first, size: ab_ref.at[place, :, pl.ds(first, size)], PART_A),
-        (1, lambda place, first, size: ab_ref.at[:, place, pl.ds(PART_A + first, size)], PART_B),
-        (2, lambda place, first, size: c_ref.at[place, :, pl.ds(first, size)], PART_C),
+        (0, lambda place, blocks, first, size: whole_ab.at[place, blocks, pl.ds(first, size)], PART_A),
+        (1, lambda place, blocks, first, size: whole_ab.at[blocks, place, pl.ds(PART_A + first, size)], PART_B),
+        (2, lambda place, blocks, first, size: whole_c.at[place, blocks, pl.ds(first, size)], PART_C),
     )
-    owns, passes, vias, gots = (own_a, own_b, own_c), (pass_a, pass_b, pass_c), (via_a, via_b, via_c), (got_a, got_b, got_c)
-    fetched = []
-    for index, (axis, piece, size) in enumerate(parts):
-        half = size // 2
-        up, down = (spot[axis] + 1) % 4, (spot[axis] + 3) % 4
-        fetched.append(
-            [
-                pltpu.make_async_copy(piece(up, 0, half), passes[index].at[0], local.at[3 * index]),
-                pltpu.make_async_copy(piece(down, half, half), passes[index].at[1], local.at[3 * index + 1]),
-                pltpu.make_async_copy(piece(spot[axis], 0, size), owns[index], local.at[3 * index + 2]),
-            ]
-        )
-        for copy in fetched[index]:
-            copy.start()
+    passes, vias, gots = (pass_a, pass_b, pass_c), (via_a, via_b, via_c), (got_a, got_b, got_c)
+    fetched = [
+        pltpu.make_async_copy(ab_ref, whole_ab, local.at[0]),
+        pltpu.make_async_copy(c_ref, whole_c, local.at[1]),
+    ]
+    for copy in fetched:
+        copy.start()
     tables = [
-        pltpu.make_async_copy(pick_ref, pick, local.at[9]),
-        pltpu.make_async_copy(eighth_ref, eighth, local.at[10]),
+        pltpu.make_async_copy(pick_ref, pick, local.at[2]),
+        pltpu.make_async_copy(eighth_ref, eighth, local.at[3]),
     ]
     for copy in tables:
         copy.start()
@@ -593,6 +619,8 @@
     corners[192:256, :] = jnp.zeros((64, 128), jnp.float32)
     for core in range(2):
         rows[core, 640:, :] = jnp.zeros((rows.shape[1] - 640, 128), jnp.float32)
+    for copy in fetched:
+        copy.wait()
     pl.semaphore_wait(barrier, len(peers))
 
     started = []
@@ -606,48 +634,56 @@
         started.append(copy)
         return copy
 
-    relays, plains, finals = [], [], []
-    for index, (axis, piece, size) in enumerate(parts):
-        half = size // 2
-        opposite = (spot[axis] + 2) % 4
-        relays.append(
-            [
-                link(piece(opposite, 0, half), vias[index].at[0], 6 * index, along(axis, 1)),
-                link(piece(opposite, half, half), vias[index].at[1], 6 * index + 1, along(axis, 3)),
-            ]
-        )
+    relays, plains, finals = [[], [], []], [], [[], [], []]
+    every, halves = pl.ds(0, 4), (pl.ds(0, 2), pl.ds(2, 2))
+    for turn, blocks in enumerate(halves):
+        for index, (axis, piece, size) in enumerate(parts):
+            half = size // 2
+            opposite = (spot[axis] + 2) % 4
+            relays[index].append(
+                [
+                    link(
+                        piece(opposite, blocks, way * half, half), vias[index].at[way, blocks],
+                        68 + 4 * index + 2 * turn + way, along(axis, 1 + 2 * way),
+                    )
+                    for way in range(2)
+                ]
+            )
     for index, (axis, piece, size) in enumerate(parts):
         half = size // 2
         up, down = (spot[axis] + 1) % 4, (spot[axis] + 3) % 4
         plains.append(
             [
-                link(piece(up, half, half), gots[index].at[0, :, pl.ds(half, half)], 6 * index + 2, along(axis, 1)),
-                link(piece(down, 0, half), gots[index].at[1, :, pl.ds(0, half)], 6 * index + 3, along(axis, 3)),
+                link(piece(up, every, half, half), gots[index].at[0, :, pl.ds(half, half)], 2 * index, along(axis, 1)),
+                link(piece(down, every, 0, half), gots[index].at[1, :, pl.ds(0, half)], 2 * index + 1, along(axis, 3)),
             ]
         )
     state_copy = link(state_ref, other_ref, 18, mate)
-    for index, (axis, piece, size) in enumerate(parts):
-        half = size // 2
-        finals.append([])
-        for way in range(2):
-            fetched[index][way].wait()
-            relays[index][way].wait_recv()
-            for block in range(4):
-                passes[index][way, block] = (
-                    passes[index][way, block].astype(jnp.float32) + vias[index][way, block].astype(jnp.float32)
-                ).astype(jnp.bfloat16)
-            target = gots[index].at[way, :, pl.ds(way * half, half)]
-            finals[index].append(
-                link(passes[index].at[way], target, 6 * index + 4 + way, along(axis, 1 + 2 * way))
-            )
+    for turn, blocks in enumerate(halves):
+        for index, (axis, piece, size) in enumerate(parts):
+            half = size // 2
+            for way in range(2):
+                relays[index][turn][way].wait_recv()
+                own = piece((spot[axis] + 1 + 2 * way) % 4, every, way * half, half)
+                for block in (2 * turn, 2 * turn + 1):
+                    passes[index][way, block] = (
+                        own[block].astype(jnp.float32) + vias[index][way, block].astype(jnp.float32)
+                    ).astype(jnp.bfloat16)
+                target = gots[index].at[way, blocks, pl.ds(way * half, half)]
+                finals[index].append(
+                    link(
+                        passes[index].at[way, blocks], target, 6 + 4 * index + 2 * turn + way,
+                        along(axis, 1 + 2 * way),
+                    )
+                )
 
     def arrive(index):
-        fetched[index][2].wait()
         for copy in plains[index] + finals[index]:
             copy.wait_recv()
 
     def add_up(index, block):
-        value = owns[index][block].astype(jnp.float32)
+        axis, piece, size = parts[index]
+        value = piece(spot[axis], every, 0, size)[block].astype(jnp.float32)
         for way in range(2):
             value = value + gots[index][way, block].astype(jnp.float32)
         return value
@@ -740,13 +776,13 @@
         copy.wait()
     coarse_points(summed[...], pick, eighth, lane_ref, picked, spread_rows, rows)
 
-    quarter_of = lax.broadcasted_iota(jnp.int32, (16, 128), 1) >> 5
+    after = sixths((16, 128))
     for core in range(2):
         for side in range(2):
             point = 15 * (1 - side)
-            value = rows[core, pl.ds(point * 40, 16, stride=4), :]
-            for p in range(1, 4):
-                value = jnp.where(quarter_of == p, rows[core, pl.ds(point * 40 + p, 16, stride=4), :], value)
+            value = rows[core, pl.ds(point * 40, 16, stride=6), :]
+            for p in range(1, 6):
+                value = jnp.where(after[p], rows[core, pl.ds(point * 40 + p, 16, stride=6), :], value)
             columns[core, side] = value
     outer = jnp.where(mem == 1, 0, 2)
     for index, (straight, slanted) in enumerate(around):
@@ -757,9 +793,8 @@
                 columns.at[core, side], corners.at[pl.ds(slot * 16, 16)],
                 52 + 2 * index + (1 if device is slanted else 0), device, 52 + slot,
             )
-    lane = lax.broadcasted_iota(jnp.int32, (16, 128), 1)
     for core in range(2):
-        edges[core] = gather_members(rows.at[core], lane).astype(jnp.bfloat16)
+        edges[core] = gather_members(rows.at[core]).astype(jnp.bfloat16)
     link(edges.at[1 - mem], halo.at[mem], 60, mate, 64 + mem)
     for other in range(2):
         core = 1 - mem if other else mem
@@ -774,7 +809,7 @@
 
     for slot in (1, 2, 3, 4, 7, 8, 9, 10):
         landed(columns.at[0, 0], corners.at[pl.ds(slot * 16, 16)], 52 + slot)
-    for q in range(10):
+    for q in range(7):
         points_ref[64:80, q * 128:q * 128 + 128] = corners[pl.ds(q, 16, stride=16), :].astype(jnp.bfloat16)
     landed(edges.at[0], halo.at[1 - mem], 64 + 1 - mem)
     points_ref[pl.ds(pl.multiple_of((1 - mem) * 16, 16), 16), :] = halo[1 - mem]
@@ -799,7 +834,7 @@
         ),
         in_specs=[hbm, hbm, hbm, hbm, vmem, hbm],
         out_specs=(vmem, hbm),
-        scratch_shapes=[pltpu.VMEM((4, size, 128), bf16) for size in sizes]
+        scratch_shapes=[pltpu.VMEM((4, 4, PART_A + PART_B, 128), bf16), pltpu.VMEM((4, 4, PART_C, 128), bf16)]
         + [pltpu.VMEM((2, 4, size // 2, 128), bf16) for size in sizes]
         + [pltpu.VMEM((2, 4, size // 2, 128), bf16) for size in sizes]
         + [pltpu.VMEM((2, 4, size, 128), bf16) for size in sizes]
@@ -814,17 +849,17 @@
             pltpu.VMEM((1648, 128), bf16),
             pltpu.VMEM((1648, WIDE), bf16),
             pltpu.VMEM((1648, WIDE), f32),
-            pltpu.VMEM((2, 672, 128), f32),
+            pltpu.VMEM((2, 704, 128), f32),
             pltpu.VMEM((2, 16, LINK_LANES), bf16),
             pltpu.VMEM((2, 2, 16, 128), f32),
             pltpu.VMEM((4, 16, LINK_LANES), bf16),
             pltpu.VMEM((256, 128), f32),
-            pltpu.SemaphoreType.DMA((68,)),
-            pltpu.SemaphoreType.DMA((68,)),
-            pltpu.SemaphoreType.DMA((11,)),
+            pltpu.SemaphoreType.DMA((80,)),
+            pltpu.SemaphoreType.DMA((80,)),
+            pltpu.SemaphoreType.DMA((4,)),
         ],
         compiler_params=pltpu.CompilerParams(
-            collective_id=1, has_side_effects=True, vmem_limit_bytes=48 * 1024 * 1024
+            collective_id=1, has_side_effects=True, vmem_limit_bytes=60 * 1024 * 1024
         ),
         name="coarse",
     )(partial_ab, partial_c, jnp.asarray(pick), jnp.asarray(eighth), jnp.asarray(lane_table()), state)

time: 71.7 us -> 67.3 us (0.939)
  local copies, waits for them, and re-layouts: 2.38 us -> 0 us
  Pallas kernels: 69 us -> 67 us
    unnamed x16 -> x0, local copies, waits for them, and re-layouts: 2.38 us -> none
    pallas_call x1, Pallas kernels: 19.6 us -> 17.7 us  [gram(): pl.pallas_call(gram_kernel, out_shape=(jax.ShapeDtypeStruct((4, 4, PART_A...]
    pallas_call x1, Pallas kernels: 36.3 us -> 37.1 us  [coarse(): pl.pallas_call(coarse_kernel, out_shape=(jax.ShapeDtypeStruct((80, LINK_L...]
where the time goes in v4:
time: 67.3 us; the launch traced here: 67.1 us
  Pallas kernels  67 us (100%)
    pallas_call x1, Pallas kernels, coarse(): pl.pallas_call(coarse_kernel, out_shape=(jax.ShapeDtypeStruct((80, LINK_L...  37.1 us
    pallas_call x1, Pallas kernels, gram(): pl.pallas_call(gram_kernel, out_shape=(jax.ShapeDtypeStruct((4, 4, PART_A...  17.7 us
    pallas_call x1, Pallas kernels, apply(): pl.pallas_call(apply_kernel, out_shape=jax.ShapeDtypeStruct((own, levels,...  8.21 us
    pallas_call x1, Pallas kernels, swap(): pl.pallas_call(swap_kernel, out_shape=jax.ShapeDtypeStruct(volume.shape,...  4.03 us

profile of v4, /device:TPU:1, one launch (start us, length us, event | category | flops | bytes accessed | tf_op | source)
XLA Modules:
  0.0 67.1 jit_solution(2738346480072676092)
XLA Ops:
  0.0 4.0 %swap.1.other_hbm = bf16[20,192,128]{2,1,0:T(8,128)(2,1)} custom-call(bf16[20,192,128]{2,1,0:T(8,128)(2,1)} %bitcast.3), custom_call_target="tpu_custom_call" | custom-call | tf_op jit(solution)/shard_map/swap/pallas_call | solution.py:554
  4.0 17.7 %gram.1 = (bf16[4,4,320,128]{3,2,1,0:T(8,128)(2,1)}, bf16[4,4,128,128]{3,2,1,0:T(8,128)(2,1)}) custom-call(s32[1,64]{1,0:T(1,128)} %count_ref.1, bf16[20,192,128]{2,1,0:T(8,128)(2,1)} %bitcast.4, bf16[20,192,128]{2,1,0:T(8,128)(2,1)} %swap.1.other_hbm, bf16[192,128,128]{2,1,0:T(8,128)(2,1)} %bitcast.2, bf16[1,24576]{1,0:T(2,128)(2,1)} %value_ref.1, ...), custom_call_target="tpu_custom_call" | custom-call | tf_op jit(solution)/shard_map/gram/pallas_call | solution.py:407
  21.7 37.1 %coarse.1 = (bf16[80,896]{1,0:T(8,128)(2,1)}, bf16[20,8,16,128]{3,2,1,0:T(8,128)(2,1)}) custom-call(bf16[4,4,320,128]{3,2,1,0:T(8,128)(2,1)} %get-tuple-element.9.ab_ref, bf16[4,4,128,128]{3,2,1,0:T(8,128)(2,1)} %get-tuple-element.10.c_ref, bf16[1648,128]{1,0:T(8,128)(2,1)} %constant.10.clone.pick_ref, bf16[1648,128]{1,0:T(8,128)(2,1)} %constant.11.clone.eighth_ref, ...), custom_call_target="tpu_custom_call" | custom-call | tf_op jit(solution)/shard_map/coarse/pallas_call | solution.py:829
  58.8 8.2 %apply.1 = bf16[20,8,16,128]{3,2,1,0:T(8,128)(2,1)} custom-call(bf16[80,896]{1,0:T(8,128)(2,1)} %get-tuple-element.11.points_ref, f32[3,80,16]{2,1,0:T(8,128)} %constant.13.clone.tent_x_ref, f32[3,80,128]{2,1,0:T(8,128)} %constant.14.clone.tent_y_ref, bf16[20,8,16,128]{3,2,1,0:T(8,128)(2,1)} %state_hbm.1, bf16[20,8,16,128]{3,2,1,0:T(8,128)(2,1)} %get-tuple-element.12.other_hbm), custom_call_target="tpu_custom_call" | custom-call | tf_op jit(solution)/shard_map/apply/pallas_call | solution.py:513

commit v5 on v4

--- a/solution.py
+++ b/solution.py
@@ -435,7 +435,7 @@
     )(counts, volume, other, matrix, values, errors, cells)
 
 
-def apply_kernel(points_ref, tent_x_ref, tent_y_ref, state_hbm, other_hbm, out_ref, states, fine, flat, result, sems):
+def apply_kernel(points_ref, tent_x_ref, tent_y_ref, state_hbm, other_hbm, out_hbm, states, out_ref, fine, flat, result, sems, out_sems):
     levels, width_x, width_y = state_hbm.shape[1:]
     own = out_ref.shape[0]
     members = 2 * own
@@ -504,7 +504,16 @@
         )
         return carry
 
-    lax.fori_loop(0, own, narrow, 0)
+    parts = out_sems.shape[0]
+    share = own // parts
+    leaving = []
+    for index in range(parts):
+        lax.fori_loop(index * share, (index + 1) * share, narrow, 0)
+        part = pl.ds(index * share, share)
+        leaving.append(pltpu.make_async_copy(out_ref.at[part], out_hbm.at[part], out_sems.at[index]))
+        leaving[index].start()
+    for copy in leaving:
+        copy.wait()
 
 
 def apply(points, tent_x, tent_y, state, other):
@@ -514,13 +523,15 @@
         apply_kernel,
         out_shape=jax.ShapeDtypeStruct((own, levels, width_x, width_y), jnp.bfloat16),
         in_specs=[pl.BlockSpec(memory_space=pltpu.VMEM)] * 3 + [pl.BlockSpec(memory_space=pl.ANY)] * 2,
-        out_specs=pl.BlockSpec(memory_space=pltpu.VMEM),
+        out_specs=pl.BlockSpec(memory_space=pl.ANY),
         scratch_shapes=[
             pltpu.VMEM((2,) + state.shape, state.dtype),
+            pltpu.VMEM(state.shape, state.dtype),
             pltpu.VMEM((width_x, points.shape[1], width_y), jnp.float32),
             pltpu.VMEM((members * levels * width_x, width_y), jnp.float32),
             pltpu.VMEM((own * levels * width_x, width_y), jnp.float32),
             pltpu.SemaphoreType.DMA((2,)),
+            pltpu.SemaphoreType.DMA((4,)),
         ],
         compiler_params=pltpu.CompilerParams(vmem_limit_bytes=60 * 1024 * 1024),
         name="apply",
@@ -528,26 +539,15 @@
 
 
 def swap_kernel(volume_ref, other_ref, send, recv):
-    mem = lax.axis_index("mem")
-    mate = (lax.axis_index("tx"), lax.axis_index("ty"), 1 - mem)
+    mate = (lax.axis_index("tx"), lax.axis_index("ty"), 1 - lax.axis_index("mem"))
     barrier = pltpu.get_barrier_semaphore()
     pl.semaphore_signal(barrier, inc=1, device_id=mate, device_id_type=MESH)
     pl.semaphore_wait(barrier, 1)
-    count = send.shape[0]
-    share = volume_ref.shape[0] // count
-    copies = []
-    for index in range(count):
-        part = pl.ds(index * share, share)
-        copies.append(
-            pltpu.make_async_remote_copy(
-                src_ref=volume_ref.at[part], dst_ref=other_ref.at[part], send_sem=send.at[index],
-                recv_sem=recv.at[index], device_id=mate, device_id_type=MESH,
-            )
-        )
-    for copy in copies:
-        copy.start()
-    for copy in copies:
-        copy.wait()
+    copy = pltpu.make_async_remote_copy(
+        src_ref=volume_ref, dst_ref=other_ref, send_sem=send, recv_sem=recv, device_id=mate, device_id_type=MESH
+    )
+    copy.start()
+    copy.wait()
 
 
 def swap(volume):
@@ -556,7 +556,7 @@
         out_shape=jax.ShapeDtypeStruct(volume.shape, volume.dtype),
         in_specs=[pl.BlockSpec(memory_space=pl.ANY)],
         out_specs=pl.BlockSpec(memory_space=pl.ANY),
-        scratch_shapes=[pltpu.SemaphoreType.DMA((4,)), pltpu.SemaphoreType.DMA((4,))],
+        scratch_shapes=[pltpu.SemaphoreType.DMA, pltpu.SemaphoreType.DMA],
         compiler_params=pltpu.CompilerParams(
             collective_id=0, has_side_effects=True, vmem_limit_bytes=60 * 1024 * 1024
         ),
@@ -565,10 +565,10 @@
 
 
 def coarse_kernel(
-    ab_ref, c_ref, pick_ref, eighth_ref, lane_ref, state_ref, points_ref, other_ref,
+    ab_ref, c_ref, pick_ref, eighth_ref, lane_hbm, state_ref, points_ref, other_ref,
     whole_ab, whole_c, pass_a, pass_b, pass_c, via_a, via_b, via_c, got_a, got_b, got_c,
     next_a, next_b, next_c, got_a2, got_b2, got_c2, last_a, last_b, last_c, got_a3, got_b3, got_c3,
-    folded, summed, pick, eighth, picked, spread_rows, rows, edges, columns, halo, corners,
+    folded, summed, pick, eighth, lane_ref, picked, spread_rows, rows, edges, columns, halo, corners,
     send, recv, local,
 ):
     x, ty, mem = lax.axis_index("tx"), lax.axis_index("ty"), lax.axis_index("mem")
@@ -611,6 +611,7 @@
     tables = [
         pltpu.make_async_copy(pick_ref, pick, local.at[2]),
         pltpu.make_async_copy(eighth_ref, eighth, local.at[3]),
+        pltpu.make_async_copy(lane_hbm, lane_ref, local.at[4]),
     ]
     for copy in tables:
         copy.start()
@@ -623,63 +624,57 @@
         copy.wait()
     pl.semaphore_wait(barrier, len(peers))
 
-    started = []
-
-    def link(source, target, index, device, landing=None):
-        copy = pltpu.make_async_remote_copy(
-            src_ref=source, dst_ref=target, send_sem=send.at[index],
-            recv_sem=recv.at[index if landing is None else landing], device_id=device, device_id_type=MESH,
+    def link(source, target, sent, landed, device):
+        pltpu.make_async_remote_copy(
+            src_ref=source, dst_ref=target, send_sem=send.at[sent], recv_sem=recv.at[landed],
+            device_id=device, device_id_type=MESH,
+        ).start()
+
+    def whole(ref, sent, landed):
+        return pltpu.make_async_remote_copy(
+            src_ref=ref, dst_ref=ref, send_sem=send.at[sent], recv_sem=recv.at[landed],
+            device_id=mate, device_id_type=MESH,
         )
-        copy.start()
-        started.append(copy)
-        return copy
-
-    relays, plains, finals = [[], [], []], [], [[], [], []]
+
+    def wait_landed(ref, landed):
+        whole(ref, 0, landed).wait_recv()
+
+    def wait_sent(ref, sent):
+        whole(ref, sent, 0).wait_send()
+
     every, halves = pl.ds(0, 4), (pl.ds(0, 2), pl.ds(2, 2))
     for turn, blocks in enumerate(halves):
         for index, (axis, piece, size) in enumerate(parts):
             half = size // 2
             opposite = (spot[axis] + 2) % 4
-            relays[index].append(
-                [
-                    link(
-                        piece(opposite, blocks, way * half, half), vias[index].at[way, blocks],
-                        68 + 4 * index + 2 * turn + way, along(axis, 1 + 2 * way),
-                    )
-                    for way in range(2)
-                ]
-            )
+            for way in range(2):
+                link(
+                    piece(opposite, blocks, way * half, half), vias[index].at[way, blocks],
+                    index, 2 * index + turn, along(axis, 1 + 2 * way),
+                )
     for index, (axis, piece, size) in enumerate(parts):
         half = size // 2
         up, down = (spot[axis] + 1) % 4, (spot[axis] + 3) % 4
-        plains.append(
-            [
-                link(piece(up, every, half, half), gots[index].at[0, :, pl.ds(half, half)], 2 * index, along(axis, 1)),
-                link(piece(down, every, 0, half), gots[index].at[1, :, pl.ds(0, half)], 2 * index + 1, along(axis, 3)),
-            ]
-        )
-    state_copy = link(state_ref, other_ref, 18, mate)
+        link(piece(up, every, half, half), gots[index].at[0, :, pl.ds(half, half)], index, 6 + index, along(axis, 1))
+        link(piece(down, every, 0, half), gots[index].at[1, :, pl.ds(0, half)], index, 6 + index, along(axis, 3))
+    link(state_ref, other_ref, 14, 17, mate)
     for turn, blocks in enumerate(halves):
         for index, (axis, piece, size) in enumerate(parts):
             half = size // 2
+            wait_landed(vias[index].at[:, blocks], 2 * index + turn)
             for way in range(2):
-                relays[index][turn][way].wait_recv()
                 own = piece((spot[axis] + 1 + 2 * way) % 4, every, way * half, half)
                 for block in (2 * turn, 2 * turn + 1):
                     passes[index][way, block] = (
                         own[block].astype(jnp.float32) + vias[index][way, block].astype(jnp.float32)
                     ).astype(jnp.bfloat16)
-                target = gots[index].at[way, blocks, pl.ds(way * half, half)]
-                finals[index].append(
-                    link(
-                        passes[index].at[way, blocks], target, 6 + 4 * index + 2 * turn + way,
-                        along(axis, 1 + 2 * way),
-                    )
+                link(
+                    passes[index].at[way, blocks], gots[index].at[way, blocks, pl.ds(way * half, half)],
+                    3 + index, 6 + index, along(axis, 1 + 2 * way),
                 )
 
     def arrive(index):
-        for copy in plains[index] + finals[index]:
-            copy.wait_recv()
+        wait_landed(gots[index], 6 + index)
 
     def add_up(index, block):
         axis, piece, size = parts[index]
@@ -688,16 +683,10 @@
             value = value + gots[index][way, block].astype(jnp.float32)
         return value
 
-    def stage(first, axis, source, target):
-        copies = []
+    def stage(index, axis, source, target):
         for turn in (2, 1, 3):
             place = (spot[axis] + turn) % 4
-            copies.append(link(source.at[place], target.at[turn - 1], first + turn - 1, along(axis, turn)))
-        return copies
-
-    def wait_all(copies):
-        for copy in copies:
-            copy.wait_recv()
+            link(source.at[place], target.at[turn - 1], 6 + index, 9 + index, along(axis, turn))
 
     def add_last(own, got):
         value = own.astype(jnp.float32)
@@ -708,15 +697,15 @@
     arrive(0)
     for block in range(4):
         next_a[block] = add_up(0, block).astype(jnp.bfloat16)
-    second_a = stage(19, 1, next_a, got_a2)
+    stage(0, 1, next_a, got_a2)
     arrive(1)
     for block, value in enumerate(block_swap([add_up(1, block) for block in range(4)])):
         next_b[block] = value.astype(jnp.bfloat16)
-    second_b = stage(22, 2, next_b, got_b2)
+    stage(1, 2, next_b, got_b2)
     arrive(2)
     for block in range(4):
         next_c[block] = add_up(2, block).astype(jnp.bfloat16)
-    second_c = stage(25, 0, next_c, got_c2)
+    stage(2, 0, next_c, got_c2)
 
     def fold(value, target):
         size = value.shape[0] // 8
@@ -725,33 +714,18 @@
         for index, part in enumerate(block_swap(pieces)):
             target[index] = part
 
-    def third(number, axis, source, target):
-        first = 28 + 8 * number
+    def third(index, axis, source, target):
         for turn in (2, 1, 3, 0):
             place = (spot[axis] + turn) % 4
-            for other in range(2):
-                if turn == 0 and other == 0:
-                    continue
-                core = 1 - mem if other else mem
+            for core in (1 - mem,) if turn == 0 else (mem, 1 - mem):
                 link(
-                    source.at[place * 2 + core], target.at[mem * 4 + turn], first + 2 * turn + other,
-                    along(axis, turn, core), first + 2 * turn + mem,
+                    source.at[place * 2 + core], target.at[mem * 4 + turn], 9 + index, 12 + index,
+                    along(axis, turn, core),
                 )
         target[mem * 4] = source[spot[axis] * 2 + mem]
 
-    def sum_third(number, source, target, row):
-        first = 28 + 8 * number
-
-        def landed(core, turn):
-            pltpu.make_async_remote_copy(
-                src_ref=source.at[0], dst_ref=target.at[core * 4 + turn], send_sem=send.at[first],
-                recv_sem=recv.at[first + 2 * turn + core], device_id=mate, device_id_type=MESH,
-            ).wait_recv()
-
-        landed(1 - mem, 0)
-        for turn in range(1, 4):
-            for core in range(2):
-                landed(core, turn)
+    def sum_third(index, source, target, row):
+        wait_landed(target.at[pl.ds(0, 7)], 12 + index)
         size = source.shape[1]
         for core in range(2):
             value = target[core * 4]
@@ -759,13 +733,13 @@
                 value = value + target[core * 4 + turn]
             summed[core * 56 + row:core * 56 + row + size, :] = value
 
-    wait_all(second_a)
+    wait_landed(got_a2, 9)
     fold(add_last(next_a[y], got_a2), last_a)
     third(0, 2, last_a, got_a3)
-    wait_all(second_b)
+    wait_landed(got_b2, 10)
     fold(add_last(next_b[z], got_b2), last_b)
     third(1, 0, last_b, got_b3)
-    wait_all(second_c)
+    wait_landed(got_c2, 11)
     fold(add_last(next_c[x], got_c2), last_c)
     third(2, 1, last_c, got_c3)
     sum_third(0, last_a, got_a3, 0)
@@ -789,36 +763,30 @@
         side, core = index // 2, index % 2
         for device, turn in ((straight, 1), (slanted, outer)):
             slot = (side * 3 + turn) * 2 + mem
-            link(
-                columns.at[core, side], corners.at[pl.ds(slot * 16, 16)],
-                52 + 2 * index + (1 if device is slanted else 0), device, 52 + slot,
-            )
+            link(columns.at[core, side], corners.at[pl.ds(slot * 16, 16)], 12, 15, device)
     for core in range(2):
         edges[core] = gather_members(rows.at[core]).astype(jnp.bfloat16)
-    link(edges.at[1 - mem], halo.at[mem], 60, mate, 64 + mem)
+    link(edges.at[1 - mem], halo.at[mem], 13, 16, mate)
     for other in range(2):
         core = 1 - mem if other else mem
-        link(edges.at[core], halo.at[3 - mem], 61 + other, ((x + ahead + 4) % 4, ty, core), 64 + 3 - mem)
+        link(edges.at[core], halo.at[3 - mem], 13, 16, ((x + ahead + 4) % 4, ty, core))
     points_ref[pl.ds(pl.multiple_of(mem * 16, 16), 16), :] = edges[mem]
 
-    def landed(source, target, index):
-        pltpu.make_async_remote_copy(
-            src_ref=source, dst_ref=target, send_sem=send.at[0], recv_sem=recv.at[index],
-            device_id=mate, device_id_type=MESH,
-        ).wait_recv()
-
-    for slot in (1, 2, 3, 4, 7, 8, 9, 10):
-        landed(columns.at[0, 0], corners.at[pl.ds(slot * 16, 16)], 52 + slot)
+    wait_landed(corners.at[pl.ds(0, 128)], 15)
     for q in range(7):
         points_ref[64:80, q * 128:q * 128 + 128] = corners[pl.ds(q, 16, stride=16), :].astype(jnp.bfloat16)
-    landed(edges.at[0], halo.at[1 - mem], 64 + 1 - mem)
+    wait_landed(halo.at[pl.ds(0, 3)], 16)
     points_ref[pl.ds(pl.multiple_of((1 - mem) * 16, 16), 16), :] = halo[1 - mem]
     for slot in (2, 3):
-        landed(edges.at[0], halo.at[slot], 64 + slot)
         points_ref[slot * 16:slot * 16 + 16, :] = halo[slot]
-    state_copy.wait_recv()
-    for copy in started:
-        copy.wait_send()
+    for index in range(3):
+        wait_sent(gots[index], index)
+        wait_sent(passes[index], 3 + index)
+        wait_sent((got_a2, got_b2, got_c2)[index], 6 + index)
+        wait_sent((got_a3, got_b3, got_c3)[index].at[pl.ds(0, 7)], 9 + index)
+    wait_sent(corners.at[pl.ds(0, 128)], 12)
+    wait_sent(halo.at[pl.ds(0, 3)], 13)
+    whole(other_ref, 14, 17).wait()
 
 
 def coarse(partial_ab, partial_c, state):
@@ -832,7 +800,7 @@
             jax.ShapeDtypeStruct((80, LINK_LANES), bf16),
             jax.ShapeDtypeStruct(state.shape, state.dtype),
         ),
-        in_specs=[hbm, hbm, hbm, hbm, vmem, hbm],
+        in_specs=[hbm] * 6,
         out_specs=(vmem, hbm),
         scratch_shapes=[pltpu.VMEM((4, 4, PART_A + PART_B, 128), bf16), pltpu.VMEM((4, 4, PART_C, 128), bf16)]
         + [pltpu.VMEM((2, 4, size // 2, 128), bf16) for size in sizes]
@@ -847,6 +815,7 @@
             pltpu.VMEM((112, 128), f32),
             pltpu.VMEM((1648, 128), bf16),
             pltpu.VMEM((1648, 128), bf16),
+            pltpu.VMEM((8, WIDE), jnp.int32),
             pltpu.VMEM((1648, WIDE), bf16),
             pltpu.VMEM((1648, WIDE), f32),
             pltpu.VMEM((2, 704, 128), f32),
@@ -854,9 +823,9 @@
             pltpu.VMEM((2, 2, 16, 128), f32),
             pltpu.VMEM((4, 16, LINK_LANES), bf16),
             pltpu.VMEM((256, 128), f32),
-            pltpu.SemaphoreType.DMA((80,)),
-            pltpu.SemaphoreType.DMA((80,)),
-            pltpu.SemaphoreType.DMA((4,)),
+            pltpu.SemaphoreType.DMA((15,)),
+            pltpu.SemaphoreType.DMA((18,)),
+            pltpu.SemaphoreType.DMA((5,)),
         ],
         compiler_params=pltpu.CompilerParams(
             collective_id=1, has_side_effects=True, vmem_limit_bytes=60 * 1024 * 1024

time: 67.3 us -> 65.8 us (0.978)
  Pallas kernels: 67 us -> 65.6 us
    pallas_call x1, Pallas kernels: 37.1 us -> 35.1 us  [coarse(): pl.pallas_call(coarse_kernel, out_shape=(jax.ShapeDtypeStruct((80, LINK_L...]
where the time goes in v5:
time: 65.8 us; the launch traced here: 65.6 us
  Pallas kernels  65.6 us (100%)
    pallas_call x1, Pallas kernels, coarse(): pl.pallas_call(coarse_kernel, out_shape=(jax.ShapeDtypeStruct((80, LINK_L...  35.1 us
    pallas_call x1, Pallas kernels, gram(): pl.pallas_call(gram_kernel, out_shape=(jax.ShapeDtypeStruct((4, 4, PART_A...  18.3 us
    pallas_call x1, Pallas kernels, apply(): pl.pallas_call(apply_kernel, out_shape=jax.ShapeDtypeStruct((own, levels,...  8.13 us
    pallas_call x1, Pallas kernels, swap(): pl.pallas_call(swap_kernel, out_shape=jax.ShapeDtypeStruct(volume.shape,...  3.98 us

profile of v5, /device:TPU:1, one launch (start us, length us, event | category | flops | bytes accessed | tf_op | source)
XLA Modules:
  0.0 65.6 jit_solution(8080351303096786735)
XLA Ops:
  0.0 4.0 %swap.1.other_hbm = bf16[20,192,128]{2,1,0:T(8,128)(2,1)} custom-call(bf16[20,192,128]{2,1,0:T(8,128)(2,1)} %bitcast.3), custom_call_target="tpu_custom_call" | custom-call | tf_op jit(solution)/shard_map/swap/pallas_call | solution.py:554
  4.0 18.3 %gram.1 = (bf16[4,4,320,128]{3,2,1,0:T(8,128)(2,1)}, bf16[4,4,128,128]{3,2,1,0:T(8,128)(2,1)}) custom-call(s32[1,64]{1,0:T(1,128)} %count_ref.1, bf16[20,192,128]{2,1,0:T(8,128)(2,1)} %bitcast.4, bf16[20,192,128]{2,1,0:T(8,128)(2,1)} %swap.1.other_hbm, bf16[192,128,128]{2,1,0:T(8,128)(2,1)} %bitcast.2, bf16[1,24576]{1,0:T(2,128)(2,1)} %value_ref.1, ...), custom_call_target="tpu_custom_call" | custom-call | tf_op jit(solution)/shard_map/gram/pallas_call | solution.py:407
  22.3 35.1 %coarse.1 = (bf16[80,896]{1,0:T(8,128)(2,1)}, bf16[20,8,16,128]{3,2,1,0:T(8,128)(2,1)}) custom-call(bf16[4,4,320,128]{3,2,1,0:T(8,128)(2,1)} %get-tuple-element.9.ab_ref, bf16[4,4,128,128]{3,2,1,0:T(8,128)(2,1)} %get-tuple-element.10.c_ref, bf16[1648,128]{1,0:T(8,128)(2,1)} %constant.10.clone.pick_ref, bf16[1648,128]{1,0:T(8,128)(2,1)} %constant.11.clone.eighth_ref, ...), custom_call_target="tpu_custom_call" | custom-call | tf_op jit(solution)/shard_map/coarse/pallas_call | solution.py:797
  57.4 8.1 %apply.1 = bf16[20,8,16,128]{3,2,1,0:T(8,128)(2,1)} custom-call(bf16[80,896]{1,0:T(8,128)(2,1)} %get-tuple-element.11.points_ref, f32[3,80,16]{2,1,0:T(8,128)} %constant.13.clone.tent_x_ref, f32[3,80,128]{2,1,0:T(8,128)} %constant.14.clone.tent_y_ref, bf16[20,8,16,128]{3,2,1,0:T(8,128)(2,1)} %state_hbm.1, bf16[20,8,16,128]{3,2,1,0:T(8,128)(2,1)} %get-tuple-element.12.other_hbm), custom_call_target="tpu_custom_call" | custom-call | tf_op jit(solution)/shard_map/apply/pallas_call | solution.py:522

commit v6 on v5

--- a/solution.py
+++ b/solution.py
@@ -1,3 +1,5 @@
+import functools
+
 import numpy as np
 import jax
 import jax.numpy as jnp
@@ -210,7 +212,7 @@
     return jnp.concatenate(pieces, axis=1)
 
 
-UNROLL = 2
+UNROLL = 16
 
 
 def core_products():
@@ -370,8 +372,8 @@
             start = (jnp.int32(0), jnp.int32(0))
             build(start, lhs0, rhs0, products)
 
-            def body(item):
-                for turn in range(UNROLL):
+            def body(turns, item):
+                for turn in range(turns):
                     lhs, rhs = (lhs0, rhs0) if turn % 2 == 0 else (lhs1, rhs1)
                     other_lhs, other_rhs = (lhs1, rhs1) if turn % 2 == 0 else (lhs0, rhs0)
                     following = follow(item)
@@ -380,7 +382,10 @@
                     item = following
                 return item
 
-            lax.while_loop(lambda item: item[0] < steps, body, start)
+            item = lax.while_loop(
+                lambda item: item[0] <= steps - UNROLL, functools.partial(body, UNROLL), start
+            )
+            lax.while_loop(lambda item: item[0] < steps, functools.partial(body, 2), item)
 
     results = []
     for x in range(4):
@@ -417,7 +422,7 @@
             pltpu.VMEM((4, 4, PART_C, 128), jnp.bfloat16),
             pltpu.VMEM((members, blocks, 128), jnp.bfloat16),
             pltpu.VMEM((blocks, 128, 128), jnp.bfloat16),
-            pltpu.VMEM((members * (blocks // CHUNKS), 128), jnp.float32),
+            pltpu.VMEM((members * (blocks // CHUNKS) + 512, 128), jnp.float32),
             pltpu.VMEM((blocks, members, 128), jnp.float32),
             pltpu.VMEM((blocks, 8, 128), jnp.float32),
             pltpu.VMEM((steps, 32, STEP), jnp.bfloat16),
@@ -456,8 +461,8 @@
             [tent_x[:, x + i:x + i + 1] * tent_y for i in range(2)], axis=1
         ).astype(jnp.bfloat16)
         made = jnp.dot(points, tent, preferred_element_type=jnp.float32)
-        fine[x] = made[:, :128]
-        fine[x + 1] = made[:, 128:]
+        fine[x, :made.shape[0], :] = made[:, :128]
+        fine[x + 1, :made.shape[0], :] = made[:, 128:]
 
     for copy in copies:
         copy.wait()
@@ -527,9 +532,9 @@
         scratch_shapes=[
             pltpu.VMEM((2,) + state.shape, state.dtype),
             pltpu.VMEM(state.shape, state.dtype),
-            pltpu.VMEM((width_x, points.shape[1], width_y), jnp.float32),
-            pltpu.VMEM((members * levels * width_x, width_y), jnp.float32),
-            pltpu.VMEM((own * levels * width_x, width_y), jnp.float32),
+            pltpu.VMEM((width_x, points.shape[1] + 16, width_y), jnp.float32),
+            pltpu.VMEM((members * levels * width_x + 256, width_y), jnp.float32),
+            pltpu.VMEM((own * levels * width_x + 256, width_y), jnp.float32),
             pltpu.SemaphoreType.DMA((2,)),
             pltpu.SemaphoreType.DMA((4,)),
         ],
@@ -818,11 +823,11 @@
             pltpu.VMEM((8, WIDE), jnp.int32),
             pltpu.VMEM((1648, WIDE), bf16),
             pltpu.VMEM((1648, WIDE), f32),
-            pltpu.VMEM((2, 704, 128), f32),
+            pltpu.VMEM((2, 1024, 128), f32),
             pltpu.VMEM((2, 16, LINK_LANES), bf16),
             pltpu.VMEM((2, 2, 16, 128), f32),
             pltpu.VMEM((4, 16, LINK_LANES), bf16),
-            pltpu.VMEM((256, 128), f32),
+            pltpu.VMEM((512, 128), f32),
             pltpu.SemaphoreType.DMA((15,)),
             pltpu.SemaphoreType.DMA((18,)),
             pltpu.SemaphoreType.DMA((5,)),

time: 65.8 us -> 64.2 us (0.976)
  Pallas kernels: 65.6 us -> 64.2 us
    pallas_call x1, Pallas kernels: 18.3 us -> 16.2 us  [gram(): pl.pallas_call(gram_kernel, out_shape=(jax.ShapeDtypeStruct((4, 4, PART_A...]
    pallas_call x1, Pallas kernels: 35.1 us -> 35.9 us  [coarse(): pl.pallas_call(coarse_kernel, out_shape=(jax.ShapeDtypeStruct((80, LINK_L...]
where the time goes in v6:
time: 64.2 us; the launch traced here: 64.4 us
  Pallas kernels  64.2 us (100%)
    pallas_call x1, Pallas kernels, coarse(): pl.pallas_call(coarse_kernel, out_shape=(jax.ShapeDtypeStruct((80, LINK_L...  35.9 us
    pallas_call x1, Pallas kernels, gram(): pl.pallas_call(gram_kernel, out_shape=(jax.ShapeDtypeStruct((4, 4, PART_A...  16.2 us
    pallas_call x1, Pallas kernels, apply(): pl.pallas_call(apply_kernel, out_shape=jax.ShapeDtypeStruct((own, levels,...  8.13 us
    pallas_call x1, Pallas kernels, swap(): pl.pallas_call(swap_kernel, out_shape=jax.ShapeDtypeStruct(volume.shape,...  3.98 us

profile of v6, /device:TPU:1, one launch (start us, length us, event | category | flops | bytes accessed | tf_op | source)
XLA Modules:
  0.0 64.4 jit_solution(4336076603805396848)
XLA Ops:
  0.0 4.0 %swap.1.other_hbm = bf16[20,192,128]{2,1,0:T(8,128)(2,1)} custom-call(bf16[20,192,128]{2,1,0:T(8,128)(2,1)} %bitcast.3), custom_call_target="tpu_custom_call" | custom-call | tf_op jit(solution)/shard_map/swap/pallas_call | solution.py:559
  4.0 16.2 %gram.1 = (bf16[4,4,320,128]{3,2,1,0:T(8,128)(2,1)}, bf16[4,4,128,128]{3,2,1,0:T(8,128)(2,1)}) custom-call(s32[1,64]{1,0:T(1,128)} %count_ref.1, bf16[20,192,128]{2,1,0:T(8,128)(2,1)} %bitcast.4, bf16[20,192,128]{2,1,0:T(8,128)(2,1)} %swap.1.other_hbm, bf16[192,128,128]{2,1,0:T(8,128)(2,1)} %bitcast.2, bf16[1,24576]{1,0:T(2,128)(2,1)} %value_ref.1, ...), custom_call_target="tpu_custom_call" | custom-call | tf_op jit(solution)/shard_map/gram/pallas_call | solution.py:412
  20.2 35.9 %coarse.1 = (bf16[80,896]{1,0:T(8,128)(2,1)}, bf16[20,8,16,128]{3,2,1,0:T(8,128)(2,1)}) custom-call(bf16[4,4,320,128]{3,2,1,0:T(8,128)(2,1)} %get-tuple-element.9.ab_ref, bf16[4,4,128,128]{3,2,1,0:T(8,128)(2,1)} %get-tuple-element.10.c_ref, bf16[1648,128]{1,0:T(8,128)(2,1)} %constant.10.clone.pick_ref, bf16[1648,128]{1,0:T(8,128)(2,1)} %constant.11.clone.eighth_ref, ...), custom_call_target="tpu_custom_call" | custom-call | tf_op jit(solution)/shard_map/coarse/pallas_call | solution.py:802
  56.1 8.1 %apply.1 = bf16[20,8,16,128]{3,2,1,0:T(8,128)(2,1)} custom-call(bf16[80,896]{1,0:T(8,128)(2,1)} %get-tuple-element.11.points_ref, f32[3,80,16]{2,1,0:T(8,128)} %constant.13.clone.tent_x_ref, f32[3,80,128]{2,1,0:T(8,128)} %constant.14.clone.tent_y_ref, bf16[20,8,16,128]{3,2,1,0:T(8,128)(2,1)} %state_hbm.1, bf16[20,8,16,128]{3,2,1,0:T(8,128)(2,1)} %get-tuple-element.12.other_hbm), custom_call_target="tpu_custom_call" | custom-call | tf_op jit(solution)/shard_map/apply/pallas_call | solution.py:527
